TPU v7x, 32 devices: a whole 2x2x4 slice. The times are simulated.
32 devices in a mesh: seq: 2 (over y), expert: 16 (over z, x, core).
Axes of the slice: x: 2, y: 2, z: 4, core: 2. Of those that a mesh axis runs over, the one named last changes fastest.
Arguments:
- tokens: bfloat16 [4096, 2048], P(('seq', 'expert')), may hold values from -4 to 4
- routes: int32 [4096, 8], P(('seq', 'expert')), may hold values from 0 to 31, all different within a row; in each aligned block of 128 rows (0 to 127, 128 to 255, ...) at most 64 rows name the same one
- gate_shares: int32 [4096, 8], P(('seq', 'expert')), may hold values from 1 to 65536
- gate_up: bfloat16 [32, 2048, 768], P('expert', 'seq'), may hold values from -0.125 to 0.125
Outputs:
- gram: float32 [32, 384, 384], P('expert', 'seq')
- maxima: float32 [32, 2048], P('expert', 'seq')
Inputs may be any that keep to these rules, and one draw needn't show every extreme that they name: `routes`: among the 128 rows of one device no expert is named more than 64 times.
All inputs are finite; a program needn't handle non-finite values.
Results may differ from a plain program's by a relative error of at most 0.0049.
Values may be sent and summed in bfloat16 or wider, within the bound.
No kernel may reach another device: no remote copies, remote signals or barrier semaphores. Data moves between devices by JAX's collectives and lax.ppermute only.
A program may use at most 64 MiB of HBM per device.

v0:
```python
import jax
import jax.numpy as jnp
from jax import lax
from jax.sharding import PartitionSpec as P

D = 2048
FWIN = 384


def hidden_of(projected):
    return (jax.nn.silu(projected[..., :FWIN]) * projected[..., FWIN:]).astype(jnp.bfloat16)


def split_weighted(hidden, row_shares):
    weighted = hidden.astype(jnp.float32) * row_shares[..., None]
    weighted_high = weighted.astype(jnp.bfloat16)
    weighted_low = (weighted - weighted_high.astype(jnp.float32)).astype(jnp.bfloat16)
    return (weighted_high, weighted_low)


def body(tokens, routes, gate_shares, gate_up):
    tok_rows = tokens.shape[0]
    top_count = routes.shape[1]
    expert_count = lax.axis_size("expert")
    seq_count = lax.axis_size("seq")
    local_count = gate_up.shape[0]
    all_experts = local_count * expert_count
    capacity = 2 * tok_rows * top_count // all_experts
    norm_factor = all_experts / (tok_rows * seq_count * expert_count * top_count)
    chosen = routes.reshape(-1)
    shares = gate_shares.reshape(-1).astype(jnp.float32) / 65536.0
    one_hot = (chosen[:, None] == jnp.arange(all_experts, dtype=jnp.int32)[None, :]).astype(
        jnp.int32
    )
    ranked = jnp.sum((jnp.cumsum(one_hot, axis=0) - one_hot) * one_hot, axis=1)
    slot_index = chosen * capacity + ranked
    token_index = jnp.arange(tok_rows * top_count, dtype=jnp.int32) // top_count
    outgoing_rows = (
        jnp.zeros((all_experts * capacity, D), jnp.bfloat16).at[slot_index].set(tokens[token_index])
    )
    out_shares = jnp.zeros((all_experts * capacity,), jnp.float32).at[slot_index].set(shares)
    outgoing_rows = outgoing_rows.reshape(expert_count, local_count, capacity, D)
    out_shares = out_shares.reshape(expert_count, local_count, capacity)
    arrived, arrived_shares = (
        lax.all_to_all(outgoing_rows, "expert", split_axis=0, concat_axis=0, tiled=True),
        lax.all_to_all(
            out_shares.astype(jnp.bfloat16), "expert", split_axis=0, concat_axis=0, tiled=True
        ).astype(out_shares.dtype),
    )
    is_live = arrived_shares > 0.0
    channel_max = jnp.max(jnp.where(is_live[..., None], jnp.abs(arrived), 0), axis=(0, 2)).astype(
        jnp.float32
    )
    projected = jnp.einsum(
        "slcd,ldf->lscf",
        arrived,
        lax.all_gather(gate_up, "seq", axis=1, tiled=True),
        preferred_element_type=jnp.float32,
    )
    hidden = hidden_of(projected).reshape(local_count, expert_count * capacity, FWIN)
    row_shares = jnp.transpose(arrived_shares, (1, 0, 2)).reshape(
        local_count, expert_count * capacity
    )
    weighted_high, weighted_low = split_weighted(hidden, row_shares)
    gram_part = jnp.einsum(
        "lrf,lrg->lfg", hidden, weighted_high, preferred_element_type=jnp.float32
    )
    gram_part = gram_part + jnp.einsum(
        "lrf,lrg->lfg", hidden, weighted_low, preferred_element_type=jnp.float32
    )
    gram_part = gram_part * norm_factor
    gram = lax.psum_scatter(gram_part, "seq", scatter_dimension=1, tiled=True)
    full_max = lax.pmax(channel_max, "seq")
    slice_width = D // seq_count
    maxima = lax.dynamic_slice_in_dim(full_max, lax.axis_index("seq") * slice_width, slice_width, 1)
    return (gram, maxima)


def solution(mesh):
    return jax.shard_map(
        body,
        mesh=mesh,
        in_specs=(
            P(("seq", "expert"), None),
            P(("seq", "expert"), None),
            P(("seq", "expert"), None),
            P("expert", "seq", None),
        ),
        out_specs=(P("expert", "seq", None), P("expert", "seq")),
        check_vma=False,
    )
```

profile of v0, /device:TPU:0, one launch (start us, length us, event | category | flops | bytes accessed | tf_op | source)
XLA Modules:
  0.0 288.8 jit_solution(7268599794049211713)
XLA Ops:
  7.2 0.0 copy-start
  7.2 0.8 copy.30
  8.0 0.1 eq.29
  8.1 0.1 eq.25
  8.2 0.7 broadcast_multiply_fusion
  8.9 9.0 %reduce-window.6 = s32[32,8,128]{2,1,0:T(8,128)S(1)} reduce-window(s32[32,8,128]{2,1,0:T(8,128)S(1)} %fusion.22, s32[]{:T(128)} %constant.40.clone.1), window={size=1x1x128 pad=0_0x0_0x127_0}, to_apply=%region_0.0 | reduce-window | flops 4161536 | bytes 262148 | tf_op jit(solution)/shard_map/reduce-window
  17.9 0.1 slice.18
  18.0 0.1 copy.32
  18.2 0.1 copy.33
  18.3 0.1 broadcast_add_fusion
  18.4 0.1 copy.29
  18.5 0.1 mul.47
  18.6 0.7 convert_multiply_fusion.1
  19.3 0.1 copy.35
  19.4 0.1 reshape.130
  19.5 4.3 %scatter_custom_fusion.1 = f32[2048]{0:T(1024)S(1)} fusion(s32[1024]{0:T(1024)S(1)} %bitcast.39, f32[1024]{0:T(1024)S(1)} %reshape.130, f32[]{:T(128)} %constant.48.clone.1), kind=kCustom, calls=%fused_computation.38 | custom fusion | bytes 8196 | tf_op jit(solution)/shard_map/scatter | solution.py:41
  23.9 0.7 convert_element_type.46
  24.6 7.4 %all-to-all-start.1 = ((bf16[16,2,64]{2,1,0:T(2,128)(2,1)}), bf16[16,2,64]{2,1,0:T(2,128)(2,1)S(1)}, u32[]{:S(2)}, u32[]{:S(2)}) async-start(bf16[16,2,64]{2,1,0:T(2,128)(2,1)} %convert_element_type.46), calls=%async_computation.1 | async-start | bytes 16384 | tf_op jit(solution)/shard_map/all_to_all | solution.py:46
  31.9 0.0 copy-done
  32.0 24.9 %scatter_custom_fusion = bf16[2048,2048]{1,0:T(8,128)(2,1)} fusion(s32[1024]{0:T(1024)S(1)} %bitcast.40, bf16[128,2048]{1,0:T(8,128)(2,1)S(1)} %copy-done, s32[1024]{0:T(1024)S(1)} %broadcast_clamp_fusion, bf16[]{:T(256)} %constant.19.clone.1), kind=kCustom, calls=%fused_computation.7 | custom fusion | bytes 8388610 | tf_op jit(solution)/shard_map/scatter | solution.py:39
  56.9 0.0 all-to-all-done.1
  56.9 6.1 %all-to-all-start = ((bf16[16,2,64,2048]{3,2,1,0:T(8,128)(2,1)}), bf16[16,2,64,2048]{3,2,1,0:T(8,128)(2,1)}, u32[]{:S(2)}, u32[]{:S(2)}) async-start(bf16[16,2,64,2048]{3,2,1,0:T(8,128)(2,1)} %bitcast.32), calls=%async_computation | async-start | bytes 16777216 | tf_op jit(solution)/shard_map/all_to_all | solution.py:45
  62.9 0.0 all-gather.2.cloned.1.call-start
  63.0 0.7 all-gather.2.cloned.1.call-update
  63.7 0.0 reduce-scatter.2.cloned.1.call-start
  63.7 0.1 mul.51
  63.8 83.2 %all-gather.2.cloned.1.call-done = bf16[2,2048,768]{2,1,0:T(8,128)(2,1)} async-done(((bf16[2,1024,768]{2,1,0:T(8,128)(2,1)}), bf16[2,2048,768]{2,1,0:T(8,128)(2,1)}) %all-gather.2.cloned.1.call-update) | async-done | bytes 6291472 | tf_op jit(solution)/shard_map/all_gather | solution.py:57
  147.0 66.6 %all-to-all-done = bf16[16,2,64,2048]{3,2,1,0:T(8,128)(2,1)} async-done(((bf16[16,2,64,2048]{3,2,1,0:T(8,128)(2,1)}), bf16[16,2,64,2048]{3,2,1,0:T(8,128)(2,1)}, u32[]{:S(2)}, u32[]{:S(2)}) %all-to-all-start) | async-done | bytes 8388640 | tf_op jit(solution)/shard_map/all_to_all | solution.py:45
  213.6 10.0 %fusion = f32[2,16,64,768]{3,2,1,0:T(8,128)S(1)} fusion(bf16[16,2,64,2048]{3,2,1,0:T(8,128)(2,1)} %all-to-all-done, bf16[2,2048,768]{2,1,0:T(8,128)(2,1)} %all-gather.2.cloned.1.call-done), kind=kOutput, calls=%fused_computation.3 | convolution fusion | flops 6442450944 | bytes 20971520 | tf_op jit(solution)/shard_map/slcd,ldf->lscf/dot_general | solution.py:54
  223.7 0.9 fusion.6
  224.6 1.2 fusion.10
  225.8 2.4 fusion.16
  228.2 0.0 reduce-scatter.2.cloned.1.call-update
  228.3 5.2 %select_reduce_fusion = bf16[2,2048]{1,0:T(2,128)(2,1)S(1)} fusion(bf16[16,2,64,2048]{3,2,1,0:T(8,128)(2,1)} %all-to-all-done, pred[16,2,64]{2,1,0:T(4,128)(4,1)S(1)} %convert_compare_fusion), kind=kLoop, calls=%fused_computation.5 | loop fusion | flops 12578816 | bytes 8398848 | tf_op jit(solution)/shard_map/reduce_max | solution.py:51
  233.4 8.1 %pmax.7 = f32[2,2048]{1,0:T(2,128)S(1)} all-reduce(bf16[2,2048]{1,0:T(2,128)(2,1)S(1)} %select_reduce_fusion), channel_id=1, replica_groups=mesh['seq'=2,'expert'=16] {'seq'}, use_global_device_ids=true, to_apply=%region_7.8 | all-reduce | flops 4096 | bytes 24576 | tf_op jit(solution)/shard_map/pmax | solution.py:73
  241.5 0.6 constant_dynamic-slice_fusion
  242.1 39.8 %reduce-scatter.2.cloned.1.call-done = f32[2,192,384]{2,1,0:T(8,128)} async-done(((f32[2,384,384]{2,1,0:T(8,128)}), f32[2,192,384]{2,1,0:T(8,128)}) %reduce-scatter.2.cloned.1.call-update) | async-done | bytes 589840 | tf_op jit(solution)/shard_map/reduce_scatter | solution.py:72
  (11 shorter events, 0.1 us)
Async XLA Ops:
  7.2 24.8 %copy-start = (bf16[128,2048]{1,0:T(8,128)(2,1)S(1)}, bf16[128,2048]{1,0:T(8,128)(2,1)}, u32[]{:S(2)}) copy-start(bf16[128,2048]{1,0:T(8,128)(2,1)} %param.4) | copy-start | bytes 1572868
  24.6 32.3 %all-to-all-start.1 = ((bf16[16,2,64]{2,1,0:T(2,128)(2,1)}), bf16[16,2,64]{2,1,0:T(2,128)(2,1)S(1)}, u32[]{:S(2)}, u32[]{:S(2)}) async-start(bf16[16,2,64]{2,1,0:T(2,128)(2,1)} %convert_element_type.46), calls=%async_computation.1 | async-start | bytes 16384 | tf_op jit(solution)/shard_map/all_to_all | solution.py:46
  56.9 156.8 %all-to-all-start = ((bf16[16,2,64,2048]{3,2,1,0:T(8,128)(2,1)}), bf16[16,2,64,2048]{3,2,1,0:T(8,128)(2,1)}, u32[]{:S(2)}, u32[]{:S(2)}) async-start(bf16[16,2,64,2048]{3,2,1,0:T(8,128)(2,1)} %bitcast.32), calls=%async_computation | async-start | bytes 16777216 | tf_op jit(solution)/shard_map/all_to_all | solution.py:45
  62.9 84.1 %all-gather.2.cloned.1.call-start = ((), (), s32[]{:S(2)}) async-start(), calls=%async_computation.3 | async-start | bytes 9437184 | tf_op jit(solution)/shard_map/all_gather | solution.py:57
  63.7 218.3 %reduce-scatter.2.cloned.1.call-start = ((), (), s32[]{:S(2)}) async-start(), calls=%async_computation.4 | async-start | bytes 1769472 | tf_op jit(solution)/shard_map/reduce_scatter | solution.py:72
Sparse Core Ops, SparseCore 0:
  65.3 81.6 all-gather.1
  228.3 53.5 reduce-scatter.1
where the time goes:
time: 289 us
  waiting for transfers between devices  190 us (66%)
  local copies, waits for them, and re-layouts  32.3 us (11%)
  other arithmetic  16.7 us (6%)
  between operations  14.2 us (5%)
  matrix products  13.6 us (5%)
  starting transfers between devices  13.5 us (5%)
  blocking collectives  8.13 us (3%)
    all_gather x1, waiting for transfers between devices, body(): lax.all_gather(gate_up, 'seq', axis=1, tiled=True)  83.2 us
    all_to_all x1, waiting for transfers between devices, body(): lax.all_to_all(outgoing_rows, 'expert', split_axis=0, concat_axis=0, tile...  66.6 us
    reduce_scatter x1, waiting for transfers between devices, body(): gram = lax.psum_scatter(gram_part, 'seq', scatter_dimension=1, tiled=True)  39.8 us
    scatter x1, local copies, waits for them, and re-layouts, body(): jnp.zeros((all_experts * capacity, D), jnp.bfloat16).at[slot_index]  24.9 us
    dot_general x1, matrix products, body(): jnp.einsum('slcd,ldf->lscf', arrived, lax.all_gather(gate_up, 'seq', axis...  10 us
    another operation x3, other arithmetic  9.15 us
    pmax x1, blocking collectives, body(): full_max = lax.pmax(channel_max, 'seq')  8.13 us
    all_to_all x1, starting transfers between devices, body(): lax.all_to_all(out_shares.astype(jnp.bfloat16), 'expert', split_axis=0, c...  7.36 us
  transfers between devices with their start and end apart: 4, of which 3 were waited for; matrix products, arithmetic and copies ran while one was open for 11% of the time, Pallas kernels for 0%

commit v1 on v0

v1 whole, which is shorter than its diff:
```python
import functools

import jax
import jax.numpy as jnp
from jax import lax
from jax.experimental import pallas as pl
from jax.experimental.pallas import tpu as pltpu
from jax.sharding import PartitionSpec as P

VMEM_LIMIT = 48 * 1024 * 1024
VM = pl.BlockSpec(memory_space=pltpu.VMEM)
SM = pl.BlockSpec(memory_space=pltpu.SMEM)


def params():
    return pltpu.CompilerParams(vmem_limit_bytes=VMEM_LIMIT)


def cost(flops, moved):
    return pl.CostEstimate(flops=int(flops), bytes_accessed=int(moved), transcendentals=0)


def pack_kernel(experts, tok_ref, routes_ref, shares_ref, out_ref):
    rows, width = tok_ref.shape
    extra = out_ref.shape[1] - width
    out_ref[:, :width] = tok_ref[...]
    lane = lax.broadcasted_iota(jnp.int32, (rows, extra), 1)
    expert = jnp.where(lane < experts, lane, lane - experts)
    value = jnp.zeros((rows, extra), jnp.int32)
    for k in range(routes_ref.shape[1]):
        value = value + jnp.where(routes_ref[:, k : k + 1] == expert, shares_ref[:, k : k + 1], 0)
    share = value.astype(jnp.float32) / 65536.0
    high = share.astype(jnp.bfloat16).astype(jnp.float32)
    low = share - high
    out_ref[:, width:] = jnp.where(lane < experts, high, low).astype(jnp.bfloat16)


def rows_kernel(experts, cap, count, *refs):
    where_ref, w_ref = refs[0], refs[1]
    blocks = refs[2 : 2 + count]
    x_ref, share_ref, p_ref, max_ref = refs[2 + count :]
    local, depth, _ = w_ref.shape
    width = x_ref.shape[2]
    rows = blocks[0].shape[0]
    extra = blocks[0].shape[1] - width
    first = where_ref[0] * local
    lane = lax.broadcasted_iota(jnp.int32, (1, extra), 1)
    slot = lax.broadcasted_iota(jnp.int32, (1, cap), 1).astype(jnp.float32)
    below = (
        lax.broadcasted_iota(jnp.int32, (rows, rows), 0)
        > lax.broadcasted_iota(jnp.int32, (rows, rows), 1)
    ).astype(jnp.bfloat16)
    largest = [jnp.zeros((1, width), jnp.float32) for _ in range(local)]
    for b, block in enumerate(blocks):
        side = block[:, width:].astype(jnp.float32)
        live = jnp.where((side > 0.0) & (lane < experts), 1.0, 0.0)
        rank = jnp.dot(below, live.astype(jnp.bfloat16), preferred_element_type=jnp.float32)
        place = jnp.where(live > 0.0, rank, -1.0)
        picks = []
        for i in range(local):
            mine = jnp.sum(jnp.where(lane == first + i, place, 0.0), axis=1, keepdims=True)
            picks.append(jnp.where(mine == slot, 1.0, 0.0))
        pick = jnp.concatenate(picks, axis=1).astype(jnp.bfloat16)
        taken = lax.dot_general(
            pick, block[...], (((0,), (0,)), ((), ())), preferred_element_type=jnp.float32
        )
        for i in range(local):
            part = taken[i * cap : (i + 1) * cap]
            x_ref[i, b * cap : (b + 1) * cap, :] = part[:, :width].astype(jnp.bfloat16)
            both = (lane == first + i) | (lane == experts + first + i)
            share = jnp.sum(jnp.where(both, part[:, width:], 0.0), axis=1, keepdims=True)
            share_ref[i, b * cap : (b + 1) * cap, :] = jnp.broadcast_to(share, (cap, 128))
            largest[i] = jnp.maximum(
                largest[i], jnp.max(jnp.abs(part[:, :width]), axis=0, keepdims=True)
            )
    for i in range(local):
        max_ref[i : i + 1, :] = largest[i]
    start = pl.multiple_of(where_ref[1] * depth, 128)
    for i in range(local):
        p_ref[i] = jnp.dot(
            x_ref[i, :, pl.ds(start, depth)], w_ref[i], preferred_element_type=jnp.float32
        )


def rows_of(experts, cap, where, weights, blocks):
    count, local, depth, fan = len(blocks), *weights.shape
    rows, full = blocks[0].shape
    width = 2 * depth
    total = count * cap
    return pl.pallas_call(
        functools.partial(rows_kernel, experts, cap, count),
        out_shape=(
            jax.ShapeDtypeStruct((local, total, width), jnp.bfloat16),
            jax.ShapeDtypeStruct((local, total, 128), jnp.float32),
            jax.ShapeDtypeStruct((local, total, fan), jnp.float32),
            jax.ShapeDtypeStruct((local, width), jnp.float32),
        ),
        in_specs=[SM] + [VM] * (1 + count),
        out_specs=(VM,) * 4,
        compiler_params=params(),
        cost_estimate=cost(
            2 * local * total * depth * fan + 2 * count * rows * local * cap * full,
            2 * count * rows * full + 2 * local * depth * fan + local * total * (2 * width + 4 * fan),
        ),
        name="expert_rows",
    )(where, weights, *blocks)


def more_kernel(offset, where_ref, w_ref, x_ref, p_ref, out_ref):
    depth = w_ref.shape[0]
    half = x_ref.shape[2] // 2
    start = pl.multiple_of((1 - where_ref[1]) * half + offset, 128)
    out_ref[0] = p_ref[0] + jnp.dot(
        x_ref[0, :, pl.ds(start, depth)], w_ref[...], preferred_element_type=jnp.float32
    )


def expert_spec(array, expert):
    return pl.BlockSpec((1,) + array.shape[1:], lambda g, e=expert: (e, 0, 0))


def more_of(where, weights, x, p, expert, offset):
    rows, fan = p.shape[1:]
    depth = weights.shape[0]
    return pl.pallas_call(
        functools.partial(more_kernel, offset),
        grid=(1,),
        out_shape=jax.ShapeDtypeStruct((1, rows, fan), jnp.float32),
        in_specs=[
            SM,
            pl.BlockSpec(weights.shape, lambda g: (0, 0)),
            expert_spec(x, expert),
            expert_spec(p, expert),
        ],
        out_specs=pl.BlockSpec((1, rows, fan), lambda g: (0, 0, 0)),
        compiler_params=params(),
        cost_estimate=cost(2 * rows * depth * fan, 8 * rows * fan + 2 * rows * x.shape[2]),
        name="more_terms",
    )(where, weights, x, p)


def gram_kernel(offsets, groups, carried, last, factor, *refs):
    where_ref = refs[0]
    w_refs = refs[1 : 1 + len(offsets)]
    ins = refs[1 + len(offsets) :]
    fan = w_refs[0].shape[1]
    wide = fan // 2
    total = None
    for g in range(groups):
        x_ref, share_ref, p_ref = ins[3 * g : 3 * g + 3]
        half = x_ref.shape[2] // 2
        value = p_ref[0]
        for offset, w_ref in zip(offsets, w_refs):
            start = pl.multiple_of((1 - where_ref[1]) * half + offset, 128)
            value = value + jnp.dot(
                x_ref[0, :, pl.ds(start, w_ref.shape[0])],
                w_ref[...],
                preferred_element_type=jnp.float32,
            )
        gate = value[:, :wide]
        hidden = (gate / (1.0 + jnp.exp(-gate)) * value[:, wide:]).astype(jnp.bfloat16)
        weighted = hidden.astype(jnp.float32) * share_ref[0, :, 0:1]
        high = weighted.astype(jnp.bfloat16)
        low = (weighted - high.astype(jnp.float32)).astype(jnp.bfloat16)
        dims = (((0,), (0,)), ((), ()))
        term = lax.dot_general(hidden, high, dims, preferred_element_type=jnp.float32)
        term = term + lax.dot_general(hidden, low, dims, preferred_element_type=jnp.float32)
        total = term if total is None else total + term
    rest = ins[3 * groups :]
    if carried:
        total = total + rest[0][...]
        rest = rest[1:]
    if not last:
        rest[0][...] = total
        return
    own_ref, send_ref, hold_ref = rest
    hold_ref[...] = total * factor
    part = own_ref.shape[0]
    own_ref[...] = hold_ref[pl.ds(pl.multiple_of(where_ref[1] * part, 16), part), :]
    send_ref[...] = hold_ref[pl.ds(pl.multiple_of((1 - where_ref[1]) * part, 16), part), :].astype(
        jnp.bfloat16
    )


def gram_of(where, weights, offsets, groups, expert, carried, last, factor):
    fan = weights[0].shape[1]
    wide = fan // 2
    ins, specs, rows = [], [], 0
    for x, share, p, place in groups:
        ins += [x, share, p]
        specs += [expert_spec(x, expert), expert_spec(share, expert), expert_spec(p, place)]
        rows += x.shape[1]
    whole = pl.BlockSpec((wide, wide), lambda g: (0, 0))
    if carried is not None:
        ins.append(carried)
        specs.append(whole)
    if last:
        piece = pl.BlockSpec((wide // 2, wide), lambda g: (0, 0))
        out_shape = (
            jax.ShapeDtypeStruct((wide // 2, wide), jnp.float32),
            jax.ShapeDtypeStruct((wide // 2, wide), jnp.bfloat16),
        )
        out_specs = (piece, piece)
        scratch = [pltpu.VMEM((wide, wide), jnp.float32)]
    else:
        out_shape = jax.ShapeDtypeStruct((wide, wide), jnp.float32)
        out_specs = whole
        scratch = []
    depth = sum(w.shape[0] for w in weights)
    return pl.pallas_call(
        functools.partial(
            gram_kernel, offsets, len(groups), carried is not None, last, factor
        ),
        grid=(1,),
        out_shape=out_shape,
        in_specs=[SM] + [pl.BlockSpec(w.shape, lambda g: (0, 0)) for w in weights] + specs,
        out_specs=out_specs,
        scratch_shapes=scratch,
        compiler_params=params(),
        cost_estimate=cost(
            2 * rows * (depth * fan + 2 * wide * wide), rows * (4 * fan + 4 * depth) + 2 * depth * fan
        ),
        name="expert_gram",
    )(where, *weights, *ins)


def tie(*arrays):
    return lax.optimization_barrier(arrays)


def gather_body(capacity, tokens, routes, gate_shares, gate_up):
    tok_rows, width = tokens.shape
    top_count = routes.shape[1]
    expert_count = lax.axis_size("expert")
    seq_count = lax.axis_size("seq")
    local_count, depth, _ = gate_up.shape
    all_experts = local_count * expert_count
    factor = all_experts / (tok_rows * seq_count * expert_count * top_count)
    columns = expert_count // 4

    def moved(array, target):
        places = [(z, x, c) for z in range(columns) for x in range(2) for c in range(2)]
        number = {place: n for n, place in enumerate(places)}
        return lax.ppermute(array, "expert", [(number[p], number[target(*p)]) for p in places])

    def along_z(array, k):
        return moved(array, lambda z, x, c: ((z + k) % columns, x, c))

    def along_x(array):
        return moved(array, lambda z, x, c: (z, 1 - x, c))

    def along_core(array):
        return moved(array, lambda z, x, c: (z, x, 1 - c))

    def swapped(array):
        return lax.ppermute(array, "seq", [(0, 1), (1, 0)])

    where = jnp.stack([lax.axis_index("expert"), lax.axis_index("seq")]).astype(jnp.int32)
    extra = -(-2 * all_experts // 128) * 128
    own = pl.pallas_call(
        functools.partial(pack_kernel, all_experts),
        out_shape=jax.ShapeDtypeStruct((tok_rows, width + extra), jnp.bfloat16),
        in_specs=[VM] * 3,
        out_specs=VM,
        compiler_params=params(),
        cost_estimate=cost(0, 4 * tok_rows * width),
        name="packed_tokens",
    )(tokens, routes, gate_shares)
    rows_from = functools.partial(rows_of, all_experts, capacity, where, gate_up)

    cut = depth // 2
    w00 = swapped(gate_up[0, :cut])
    w01 = swapped(gate_up[0, cut:])
    z1 = along_z(own, 1)
    x0 = along_x(own)
    z3 = along_z(own, columns - 1)
    c0 = along_core(own)
    x0, c0 = tie(x0, c0)
    cx0 = along_core(x0)
    own2, z1, z3, cx0, x0, c0, w00, w1a, w1b = tie(
        own, z1, z3, cx0, x0, c0, w00, gate_up[1, :cut], gate_up[1, cut:]
    )
    w10 = swapped(w1a)
    z2 = along_z(own2, 2)
    x1, x3, c1, c3 = along_x(z1), along_x(z3), along_core(z1), along_core(z3)
    g0 = rows_from((own2, c0, x0, cx0))
    z2, x1, x3, c1, c3, w01, w1b, *g0 = tie(z2, x1, x3, c1, c3, w01, w1b, *g0)
    w11 = swapped(w1b)
    x2, c2, cx1, cx3 = along_x(z2), along_core(z2), along_core(x1), along_core(x3)
    g1 = rows_from((z1, c1, x1, cx1, z3, c3, x3, cx3))
    e0 = gram_of(
        where, (w00, w01), (0, cut), [(g[0], g[1], g[2], 0) for g in (g0, g1)], 0, None, False, factor
    )
    x2, e0, *g1 = tie(x2, e0, *g1)
    cx2 = along_core(x2)
    p1 = [more_of(where, w10, g[0], g[2], 1, 0) for g in (g0, g1)]
    cx2, *p1 = tie(cx2, *p1)
    g2 = rows_from((z2, c2, x2, cx2))
    own0, send0 = gram_of(
        where, (w00, w01), (0, cut), [(g2[0], g2[1], g2[2], 0)], 0, e0, True, factor
    )
    p1.append(more_of(where, w10, g2[0], g2[2], 1, 0))
    got0 = swapped(send0)
    largest = functools.reduce(jnp.maximum, [g[3] for g in (g0, g1, g2)])
    mine = lax.axis_index("seq")
    keep = lax.dynamic_slice_in_dim(largest, mine * depth, depth, 1)
    give = lax.dynamic_slice_in_dim(largest, (1 - mine) * depth, depth, 1)
    maxima = jnp.maximum(keep, swapped(give))
    own1, send1 = gram_of(
        where,
        (w11,),
        (cut,),
        [(g[0], g[1], p, 0) for g, p in zip((g0, g1, g2), p1)],
        1,
        None,
        True,
        factor,
    )
    got1 = swapped(send1)
    gram = jnp.stack([own0 + got0.astype(jnp.float32), own1 + got1.astype(jnp.float32)])
    return (gram, maxima)


def routed_body(capacity, tokens, routes, gate_shares, gate_up):
    tok_rows, width = tokens.shape
    top_count = routes.shape[1]
    expert_count = lax.axis_size("expert")
    seq_count = lax.axis_size("seq")
    local_count, _, fan = gate_up.shape
    wide = fan // 2
    all_experts = local_count * expert_count
    norm_factor = all_experts / (tok_rows * seq_count * expert_count * top_count)
    chosen = routes.reshape(-1)
    shares = gate_shares.reshape(-1).astype(jnp.float32) / 65536.0
    one_hot = (chosen[:, None] == jnp.arange(all_experts, dtype=jnp.int32)[None, :]).astype(jnp.int32)
    ranked = jnp.sum((jnp.cumsum(one_hot, axis=0) - one_hot) * one_hot, axis=1)
    slot_index = chosen * capacity + ranked
    token_index = jnp.arange(tok_rows * top_count, dtype=jnp.int32) // top_count
    outgoing = (
        jnp.zeros((all_experts * capacity, width), jnp.bfloat16)
        .at[slot_index]
        .set(tokens[token_index])
        .reshape(expert_count, local_count, capacity, width)
    )
    out_shares = (
        jnp.zeros((all_experts * capacity,), jnp.float32)
        .at[slot_index]
        .set(shares)
        .reshape(expert_count, local_count, capacity)
    )
    arrived = lax.all_to_all(outgoing, "expert", split_axis=0, concat_axis=0, tiled=True)
    arrived_shares = lax.all_to_all(out_shares, "expert", split_axis=0, concat_axis=0, tiled=True)
    channel_max = jnp.max(
        jnp.where(arrived_shares[..., None] > 0.0, jnp.abs(arrived), 0), axis=(0, 2)
    ).astype(jnp.float32)
    projected = jnp.einsum(
        "slcd,ldf->lscf",
        arrived,
        lax.all_gather(gate_up, "seq", axis=1, tiled=True),
        preferred_element_type=jnp.float32,
    )
    hidden = (jax.nn.silu(projected[..., :wide]) * projected[..., wide:]).astype(jnp.bfloat16)
    hidden = hidden.reshape(local_count, expert_count * capacity, wide)
    row_shares = jnp.transpose(arrived_shares, (1, 0, 2)).reshape(local_count, -1)
    weighted = hidden.astype(jnp.float32) * row_shares[..., None]
    high = weighted.astype(jnp.bfloat16)
    low = (weighted - high.astype(jnp.float32)).astype(jnp.bfloat16)
    gram = jnp.einsum("lrf,lrg->lfg", hidden, high, preferred_element_type=jnp.float32)
    gram = gram + jnp.einsum("lrf,lrg->lfg", hidden, low, preferred_element_type=jnp.float32)
    gram = lax.psum_scatter(gram * norm_factor, "seq", scatter_dimension=1, tiled=True)
    full_max = lax.pmax(channel_max, "seq")
    part = width // seq_count
    maxima = lax.dynamic_slice_in_dim(full_max, lax.axis_index("seq") * part, part, 1)
    return (gram, maxima)


def body(tokens, routes, gate_shares, gate_up):
    expert_count = lax.axis_size("expert")
    local_count = gate_up.shape[0]
    rows = tokens.shape[0]
    capacity = 2 * rows * routes.shape[1] // (local_count * expert_count)
    whole_rows = rows <= local_count * capacity
    shaped = lax.axis_size("seq") == 2 and expert_count == 16 and local_count == 2
    plan = gather_body if whole_rows and shaped else routed_body
    return plan(capacity, tokens, routes, gate_shares, gate_up)


def solution(mesh):
    return jax.shard_map(
        body,
        mesh=mesh,
        in_specs=(
            P(("seq", "expert"), None),
            P(("seq", "expert"), None),
            P(("seq", "expert"), None),
            P("expert", "seq", None),
        ),
        out_specs=(P("expert", "seq", None), P("expert", "seq")),
        check_vma=False,
    )
```

time: 289 us -> 127 us (0.44)
  waiting for transfers between devices: 190 us -> 49 us
  Pallas kernels: 0 us -> 39.2 us
  local copies, waits for them, and re-layouts: 32.3 us -> 12.7 us
  other arithmetic: 16.7 us -> 1.6 us
  matrix products: 13.6 us -> 0 us
  between operations: 14.2 us -> 0.88 us
  starting transfers between devices: 13.5 us -> 23.5 us
  blocking collectives: 8.13 us -> 0 us
    all_gather x1 -> x0, waiting for transfers between devices: 83.2 us -> none  [body(): lax.all_gather(gate_up, 'seq', axis=1, tiled=True)]
    all_to_all x2 -> x0, waiting for transfers between devices: 66.6 us -> none  [the longest x1 66.6 us: body(): lax.all_to_all(outgoing_rows, 'expert', split_axis=0, concat_axis=0, tile...]
    ppermute x0 -> x22, waiting for transfers between devices: none -> 49 us  [the longest x15 41.5 us: moved(): lax.ppermute(array, 'expert', [(number[p], number[target(*p)]) for p in p...]
    reduce_scatter x1 -> x0, waiting for transfers between devices: 39.8 us -> none  [body(): gram = lax.psum_scatter(gram_part, 'seq', scatter_dimension=1, tiled=True)]
    pallas_call x0 -> x10, Pallas kernels: none -> 39.2 us  [the longest x3 21.4 us: rows_of(): pl.pallas_call(functools.partial(rows_kernel, experts, cap, count), out_s...]
    scatter x2 -> x0, local copies, waits for them, and re-layouts: 29.2 us -> none  [the longest x1 24.9 us: body(): jnp.zeros((all_experts * capacity, D), jnp.bfloat16).at[slot_index]]
    ppermute x0 -> x22, starting transfers between devices: none -> 23.5 us  [the longest x15 14.6 us: moved(): lax.ppermute(array, 'expert', [(number[p], number[target(*p)]) for p in p...]
    dot_general x3 -> x0, matrix products: 13.6 us -> none  [the longest x1 10 us: body(): jnp.einsum('slcd,ldf->lscf', arrived, lax.all_gather(gate_up, 'seq', axis...]
  transfers between devices with their start and end apart: 4 -> 22, of which waited for: 3 -> 9; matrix products, arithmetic and copies ran while one was open for 11% -> 3% of each run, Pallas kernels for 0% -> 31%
where the time goes in v1:
time: 127 us
  waiting for transfers between devices  49 us (39%)
  Pallas kernels  39.2 us (31%)
  starting transfers between devices  23.5 us (19%)
  local copies, waits for them, and re-layouts  12.7 us (10%)
  other arithmetic  1.6 us (1%)
    ppermute x15, waiting for transfers between devices, moved(): lax.ppermute(array, 'expert', [(number[p], number[target(*p)]) for p in p...  41.5 us
    pallas_call x3, Pallas kernels, rows_of(): pl.pallas_call(functools.partial(rows_kernel, experts, cap, count), out_s...  21.4 us
    ppermute x15, starting transfers between devices, moved(): lax.ppermute(array, 'expert', [(number[p], number[target(*p)]) for p in p...  14.6 us
    pallas_call x3, Pallas kernels, gram_of(): pl.pallas_call(functools.partial(gram_kernel, offsets, len(groups), carri...  13.4 us
    unnamed x42, local copies, waits for them, and re-layouts  9.46 us
    ppermute x7, starting transfers between devices, swapped(): return lax.ppermute(array, 'seq', [(0, 1), (1, 0)])  8.84 us
    ppermute x7, waiting for transfers between devices, swapped(): return lax.ppermute(array, 'seq', [(0, 1), (1, 0)])  7.53 us
    pallas_call x3, Pallas kernels, more_of(): pl.pallas_call(functools.partial(more_kernel, offset), grid=(1,), out_sha...  4 us
  transfers between devices with their start and end apart: 22, of which 9 were waited for; matrix products, arithmetic and copies ran while one was open for 3% of the time, Pallas kernels for 31%

profile of v1, /device:TPU:0, one launch (start us, length us, event | category | flops | bytes accessed | tf_op | source)
XLA Modules:
  0.0 126.8 jit_solution(2614704150543007557)
XLA Ops:
  0.6 0.8 copy.6.routes_ref
  1.4 0.8 copy.7.shares_ref
  2.2 1.0 copy-done.17
  3.2 0.4 packed_tokens.1.refs_2_
  3.6 3.0 %collective-permute-start.2 = (bf16[128,2176]{1,0:T(8,128)(2,1)S(1)}, bf16[128,2176]{1,0:T(8,128)(2,1)S(1)}, u32[]{:S(2)}, u32[]{:S(2)}) collective-permute-start(bf16[128,2176]{1,0:T(8,128)(2,1)S(1)} %packed_tokens.1.refs_2_), channel_id=1, source_target_pairs={{0,2},{1,3},{2,0},{3,1},{4,6},{5,7},{6,4},{7,5},{8,10},{9,11},{10,... | collective-permute-start | bytes 1671176 | tf_op jit(solution)/shard_map/ppermute | solution.py:244
  6.6 3.2 %slice_bitcast_fusion = (bf16[512,768]{1,0:T(8,128)(2,1)S(1)}, bf16[512,768]{1,0:T(8,128)(2,1)}, bf16[512,768]{1,0:T(8,128)(2,1)}, bf16[512,768]{1,0:T(8,128)(2,1)S(1)}) fusion(bf16[2,1024,768]{2,1,0:T(8,128)(2,1)} %refs_1_.5), kind=kLoop, calls=%fused_computation | loop fusion | bytes 6291456 | tf_op jit(solution)/shard_map/squeeze | solution.py:273
  9.8 1.5 %collective-permute-start.5 = (bf16[512,768]{1,0:T(8,128)(2,1)S(1)}, bf16[512,768]{1,0:T(8,128)(2,1)S(1)}, u32[]{:S(2)}, u32[]{:S(2)}) collective-permute-start(bf16[512,768]{1,0:T(8,128)(2,1)S(1)} %get-tuple-element.99), channel_id=1, source_target_pairs={{0,16},{16,0},{1,17},{17,1},{2,18},{18,2},{3,19},{19,3},{4,20},{20... | collective-permute-start | bytes 2359304 | tf_op jit(solution)/shard_map/ppermute | solution.py:256
  11.3 0.5 collective-permute-start.11
  11.8 1.6 %collective-permute-start = (bf16[128,2176]{1,0:T(8,128)(2,1)S(1)}, bf16[128,2176]{1,0:T(8,128)(2,1)S(1)}, u32[]{:S(2)}, u32[]{:S(2)}) collective-permute-start(bf16[128,2176]{1,0:T(8,128)(2,1)S(1)} %packed_tokens.1.refs_2_), channel_id=1, source_target_pairs={{0,4},{1,5},{2,6},{3,7},{4,8},{5,9},{6,10},{7,11},{8,12},{9,13},{1... | collective-permute-start | bytes 1671176 | tf_op jit(solution)/shard_map/ppermute | solution.py:244
  13.4 5.8 %collective-permute-done.2.refs_4_ = bf16[128,2176]{1,0:T(8,128)(2,1)S(1)} collective-permute-done((bf16[128,2176]{1,0:T(8,128)(2,1)S(1)}, bf16[128,2176]{1,0:T(8,128)(2,1)S(1)}, u32[]{:S(2)}, u32[]{:S(2)}) %collective-permute-start.2) | collective-permute-done | bytes 557088 | tf_op jit(solution)/shard_map/ppermute | solution.py:244
  19.2 3.9 %collective-permute-start.1 = (bf16[128,2176]{1,0:T(8,128)(2,1)S(1)}, bf16[128,2176]{1,0:T(8,128)(2,1)S(1)}, u32[]{:S(2)}, u32[]{:S(2)}) collective-permute-start(bf16[128,2176]{1,0:T(8,128)(2,1)S(1)} %packed_tokens.1.refs_2_), channel_id=1, source_target_pairs={{0,12},{1,13},{2,14},{3,15},{4,0},{5,1},{6,2},{7,3},{8,4},{9,5},{1... | collective-permute-start | bytes 1671176 | tf_op jit(solution)/shard_map/ppermute | solution.py:244
  23.1 6.1 %collective-permute-done.refs_2_ = bf16[128,2176]{1,0:T(8,128)(2,1)S(1)} collective-permute-done((bf16[128,2176]{1,0:T(8,128)(2,1)S(1)}, bf16[128,2176]{1,0:T(8,128)(2,1)S(1)}, u32[]{:S(2)}, u32[]{:S(2)}) %collective-permute-start) | collective-permute-done | bytes 557088 | tf_op jit(solution)/shard_map/ppermute | solution.py:244
  29.2 10.9 %collective-permute-done.1.refs_6_ = bf16[128,2176]{1,0:T(8,128)(2,1)S(1)} collective-permute-done((bf16[128,2176]{1,0:T(8,128)(2,1)S(1)}, bf16[128,2176]{1,0:T(8,128)(2,1)S(1)}, u32[]{:S(2)}, u32[]{:S(2)}) %collective-permute-start.1) | collective-permute-done | bytes 557088 | tf_op jit(solution)/shard_map/ppermute | solution.py:244
  40.1 0.9 copy-done.7
  41.0 0.5 collective-permute-start.8
  41.5 0.8 copy-done.18
  42.3 1.5 %collective-permute-start.7 = (bf16[128,2176]{1,0:T(8,128)(2,1)S(1)}, bf16[128,2176]{1,0:T(8,128)(2,1)}, u32[]{:S(2)}, u32[]{:S(2)}) collective-permute-start(bf16[128,2176]{1,0:T(8,128)(2,1)S(1)} %collective-permute-done.refs_2_), channel_id=1, source_target_pairs={{0,2},{1,3},{2,0},{3,1},{4,6},{5,7},{6,4},{7,5},{8,10},{9,11},{10,... | collective-permute-start | bytes 1671176 | tf_op jit(solution)/shard_map/ppermute | solution.py:244
  43.8 2.8 %collective-permute-done.11.refs_2_ = bf16[512,768]{1,0:T(8,128)(2,1)S(1)} collective-permute-done((bf16[512,768]{1,0:T(8,128)(2,1)S(1)}, bf16[512,768]{1,0:T(8,128)(2,1)S(1)}, u32[]{:S(2)}, u32[]{:S(2)}) %collective-permute-start.11) | collective-permute-done | bytes 786464 | tf_op jit(solution)/shard_map/ppermute | solution.py:256
  46.6 0.9 copy-done.10
  47.5 2.6 %collective-permute-start.6 = (bf16[128,2176]{1,0:T(8,128)(2,1)S(1)}, bf16[128,2176]{1,0:T(8,128)(2,1)}, u32[]{:S(2)}, u32[]{:S(2)}) collective-permute-start(bf16[128,2176]{1,0:T(8,128)(2,1)S(1)} %packed_tokens.1.refs_2_), channel_id=1, source_target_pairs={{0,8},{1,9},{2,10},{3,11},{4,12},{5,13},{6,14},{7,15},{8,0},{9,1},... | collective-permute-start | bytes 1671176 | tf_op jit(solution)/shard_map/ppermute | solution.py:244
  50.2 5.0 %expert_rows.3 = (bf16[2,256,2048]{2,1,0:T(8,128)(2,1)S(1)}, f32[2,256,128]{2,1,0:T(8,128)S(1)}, f32[2,256,768]{2,1,0:T(8,128)S(1)}, f32[2,2048]{1,0:T(2,128)S(1)}) custom-call(s32[2]{0:T(128)S(1)} %pad_add_fusion.refs_0_.where_ref, bf16[2,1024,768]{2,1,0:T(8,128)(2,1)} %refs_1_.5, bf16[128,2176]{1,0:T(8,128)(2,1)S(1)} %packed_tokens.1.refs_2_, ...), custom_call_target="tpu_custom_call" | custom-call | flops 1090519040 | bytes 9043968 | tf_op jit(solution)/shard_map/expert_rows/pallas_call | solution.py:90
  55.2 1.4 %copy-done.2 = bf16[2,256,2048]{2,1,0:T(8,128)(2,1)} copy-done((bf16[2,256,2048]{2,1,0:T(8,128)(2,1)}, bf16[2,256,2048]{2,1,0:T(8,128)(2,1)S(1)}, u32[]{:S(2)}) %copy-start.2) | copy-done | bytes 2097176
  56.6 11.5 %collective-permute-done.7.refs_4_ = bf16[128,2176]{1,0:T(8,128)(2,1)} collective-permute-done((bf16[128,2176]{1,0:T(8,128)(2,1)S(1)}, bf16[128,2176]{1,0:T(8,128)(2,1)}, u32[]{:S(2)}, u32[]{:S(2)}) %collective-permute-start.7) | collective-permute-done | bytes 557088 | tf_op jit(solution)/shard_map/ppermute | solution.py:244
  68.1 6.7 %collective-permute-done.6.refs_2_ = bf16[128,2176]{1,0:T(8,128)(2,1)} collective-permute-done((bf16[128,2176]{1,0:T(8,128)(2,1)S(1)}, bf16[128,2176]{1,0:T(8,128)(2,1)}, u32[]{:S(2)}, u32[]{:S(2)}) %collective-permute-start.6) | collective-permute-done | bytes 557088 | tf_op jit(solution)/shard_map/ppermute | solution.py:244
  74.8 0.5 collective-permute-start.15
  75.3 0.5 collective-permute-start.13
  75.8 1.6 %collective-permute-start.17 = (bf16[512,768]{1,0:T(8,128)(2,1)}, bf16[512,768]{1,0:T(8,128)(2,1)S(1)}, u32[]{:S(2)}, u32[]{:S(2)}) collective-permute-start(bf16[512,768]{1,0:T(8,128)(2,1)} %get-tuple-element.77), channel_id=1, source_target_pairs={{0,16},{16,0},{1,17},{17,1},{2,18},{18,2},{3,19},{19,3},{4,20},{20... | collective-permute-start | bytes 2359304 | tf_op jit(solution)/shard_map/ppermute | solution.py:256
  77.4 0.4 collective-permute-done.15.refs_9_
  77.8 10.7 %expert_rows.4 = (bf16[2,512,2048]{2,1,0:T(8,128)(2,1)}, f32[2,512,128]{2,1,0:T(8,128)S(1)}, f32[2,512,768]{2,1,0:T(8,128)}, f32[2,2048]{1,0:T(2,128)S(1)}) custom-call(s32[2]{0:T(128)S(1)} %pad_add_fusion.refs_0_.where_ref, bf16[2,1024,768]{2,1,0:T(8,128)(2,1)} %refs_1_.5, bf16[128,2176]{1,0:T(8,128)(2,1)S(1)} %collective-permute-done.refs_2_, ...), custom_call_target="tpu_custom_call" | custom-call | flops 2181038080 | bytes 14942208 | tf_op jit(solution)/shard_map/expert_rows/pallas_call | solution.py:90
  88.5 5.5 %expert_gram.3.refs_6_ = f32[384,384]{1,0:T(8,128)S(1)} custom-call(s32[2]{0:T(128)S(1)} %pad_add_fusion.refs_0_.where_ref, bf16[512,768]{1,0:T(8,128)(2,1)S(1)} %copy-done.8, bf16[512,768]{1,0:T(8,128)(2,1)S(1)} %copy-done.11, bf16[2,256,2048]{2,1,0:T(8,128)(2,1)} %copy-done.2, f32[2,256,128]{2,1,0:T(8,128)S(1)} %get-tuple-element.66.refs_4_.refs_3_, ...), custom_call_target="tpu_custom_call" | custom-call | flops 1660944384 | bytes 7077888 | tf_op jit(solution)/shard_map/expert_gram/pallas_call | solution.py:210
  94.0 0.2 collective-permute-start.16
  94.2 0.4 collective-permute-start.12
  94.6 1.5 %collective-permute-start.19 = (bf16[512,768]{1,0:T(8,128)(2,1)}, bf16[512,768]{1,0:T(8,128)(2,1)}, u32[]{:S(2)}, u32[]{:S(2)}) collective-permute-start(bf16[512,768]{1,0:T(8,128)(2,1)} %get-tuple-element.87), channel_id=1, source_target_pairs={{0,16},{16,0},{1,17},{17,1},{2,18},{18,2},{3,19},{19,3},{4,20},{20... | collective-permute-start | bytes 2359304 | tf_op jit(solution)/shard_map/ppermute | solution.py:256
  96.1 1.4 %copy-done.6 = f32[2,256,768]{2,1,0:T(8,128)S(1)} copy-done((f32[2,256,768]{2,1,0:T(8,128)S(1)}, f32[2,256,768]{2,1,0:T(8,128)}, u32[]{:S(2)}) %copy-start.6) | copy-done | bytes 1572888
  97.5 0.9 more_terms.3.refs_4_
  98.4 2.2 %more_terms.4.refs_7_ = f32[1,512,768]{2,1,0:T(8,128)S(1)} custom-call(s32[2]{0:T(128)S(1)} %pad_add_fusion.refs_0_.where_ref, bf16[512,768]{1,0:T(8,128)(2,1)S(1)} %collective-permute-done.17.w_ref, bf16[2,512,2048]{2,1,0:T(8,128)(2,1)} %get-tuple-element.78.refs_6_.x_ref.refs_5_, f32[2,512,768]{2,1,0:T(8,128)S(1)} %copy-done.4), custom_call_target="tpu_custom_call" | custom-call | flops 402653184 | bytes 5242880 | tf_op jit(solution)/shard_map/more_terms/pallas_call | solution.py:125
  100.7 5.7 %expert_rows.5 = (bf16[2,256,2048]{2,1,0:T(8,128)(2,1)S(1)}, f32[2,256,128]{2,1,0:T(8,128)S(1)}, f32[2,256,768]{2,1,0:T(8,128)S(1)}, f32[2,2048]{1,0:T(2,128)S(1)}) custom-call(s32[2]{0:T(128)S(1)} %pad_add_fusion.refs_0_.where_ref, bf16[2,1024,768]{2,1,0:T(8,128)(2,1)} %refs_1_.5, bf16[128,2176]{1,0:T(8,128)(2,1)} %collective-permute-done.6.refs_2_, ...), custom_call_target="tpu_custom_call" | custom-call | flops 1090519040 | bytes 9043968 | tf_op jit(solution)/shard_map/expert_rows/pallas_call | solution.py:90
  106.4 1.4 %copy-done = bf16[2,256,2048]{2,1,0:T(8,128)(2,1)} copy-done((bf16[2,256,2048]{2,1,0:T(8,128)(2,1)}, bf16[2,256,2048]{2,1,0:T(8,128)(2,1)S(1)}, u32[]{:S(2)}) %copy-start) | copy-done | bytes 2097176
  107.8 1.0 collective-permute-start.21
  108.9 2.6 %expert_gram.4 = (f32[192,384]{1,0:T(8,128)S(1)}, bf16[192,384]{1,0:T(8,128)(2,1)S(1)}) custom-call(s32[2]{0:T(128)S(1)} %pad_add_fusion.refs_0_.where_ref, bf16[512,768]{1,0:T(8,128)(2,1)S(1)} %copy-done.9, bf16[512,768]{1,0:T(8,128)(2,1)S(1)} %copy-done.12, bf16[2,256,2048]{2,1,0:T(8,128)(2,1)} %copy-done, ...), custom_call_target="tpu_custom_call" | custom-call | flops 553648128 | bytes 3407872 | tf_op jit(solution)/shard_map/expert_gram/pallas_call | solution.py:210
  111.4 1.2 collective-permute-start.18
  112.6 0.9 more_terms.5.refs_10_
  113.5 1.8 %collective-permute-done.19.refs_1_ = bf16[512,768]{1,0:T(8,128)(2,1)} collective-permute-done((bf16[512,768]{1,0:T(8,128)(2,1)}, bf16[512,768]{1,0:T(8,128)(2,1)}, u32[]{:S(2)}, u32[]{:S(2)}) %collective-permute-start.19) | collective-permute-done | bytes 786464 | tf_op jit(solution)/shard_map/ppermute | solution.py:256
  115.3 5.4 %expert_gram.5 = (f32[192,384]{1,0:T(8,128)S(1)}, bf16[192,384]{1,0:T(8,128)(2,1)S(1)}) custom-call(s32[2]{0:T(128)S(1)} %pad_add_fusion.refs_0_.where_ref, bf16[512,768]{1,0:T(8,128)(2,1)} %collective-permute-done.19.refs_1_, bf16[2,256,2048]{2,1,0:T(8,128)(2,1)} %copy-done.2, f32[2,256,128]{2,1,0:T(8,128)S(1)} %copy-done.16, ...), custom_call_target="tpu_custom_call" | custom-call | flops 1409286144 | bytes 6029312 | tf_op jit(solution)/shard_map/expert_gram/pallas_call | solution.py:210
  120.7 1.6 %collective-permute-start.20 = (bf16[192,384]{1,0:T(8,128)(2,1)S(1)}, bf16[192,384]{1,0:T(8,128)(2,1)S(1)}, u32[]{:S(2)}, u32[]{:S(2)}) collective-permute-start(bf16[192,384]{1,0:T(8,128)(2,1)S(1)} %get-tuple-element.92), channel_id=1, source_target_pairs={{0,16},{16,0},{1,17},{17,1},{2,18},{18,2},{3,19},{19,3},{4,20},{20... | collective-permute-start | bytes 442376 | tf_op jit(solution)/shard_map/ppermute | solution.py:256
  122.2 0.6 dynamic-slice_maximum_fusion
  122.9 3.0 %collective-permute-done.20 = bf16[192,384]{1,0:T(8,128)(2,1)S(1)} collective-permute-done((bf16[192,384]{1,0:T(8,128)(2,1)S(1)}, bf16[192,384]{1,0:T(8,128)(2,1)S(1)}, u32[]{:S(2)}, u32[]{:S(2)}) %collective-permute-start.20) | collective-permute-done | bytes 147488 | tf_op jit(solution)/shard_map/ppermute | solution.py:256
  125.9 0.9 pad_maximum_fusion
  (56 shorter events, 0.3 us)
Async XLA Ops:
  2.2 1.0 copy-start.17
  3.6 15.6 %collective-permute-start.2 = (bf16[128,2176]{1,0:T(8,128)(2,1)S(1)}, bf16[128,2176]{1,0:T(8,128)(2,1)S(1)}, u32[]{:S(2)}, u32[]{:S(2)}) collective-permute-start(bf16[128,2176]{1,0:T(8,128)(2,1)S(1)} %packed_tokens.1.refs_2_), channel_id=1, source_target_pairs={{0,2},{1,3},{2,0},{3,1},{4,6},{5,7},{6,4},{7,5},{8,10},{9,11},{10,... | collective-permute-start | bytes 1671176 | tf_op jit(solution)/shard_map/ppermute | solution.py:244
  6.6 16.5 %collective-permute-start.3 = (bf16[128,2176]{1,0:T(8,128)(2,1)S(1)}, bf16[128,2176]{1,0:T(8,128)(2,1)S(1)}, u32[]{:S(2)}, u32[]{:S(2)}) collective-permute-start(bf16[128,2176]{1,0:T(8,128)(2,1)S(1)} %packed_tokens.1.refs_2_), channel_id=1, source_target_pairs={{0,1},{1,0},{2,3},{3,2},{4,5},{5,4},{6,7},{7,6},{8,9},{9,8},{10,11... | collective-permute-start | bytes 1671176 | tf_op jit(solution)/shard_map/ppermute | solution.py:244
  9.8 30.3 %collective-permute-start.5 = (bf16[512,768]{1,0:T(8,128)(2,1)S(1)}, bf16[512,768]{1,0:T(8,128)(2,1)S(1)}, u32[]{:S(2)}, u32[]{:S(2)}) collective-permute-start(bf16[512,768]{1,0:T(8,128)(2,1)S(1)} %get-tuple-element.99), channel_id=1, source_target_pairs={{0,16},{16,0},{1,17},{17,1},{2,18},{18,2},{3,19},{19,3},{4,20},{20... | collective-permute-start | bytes 2359304 | tf_op jit(solution)/shard_map/ppermute | solution.py:256
  11.3 35.3 %collective-permute-start.11 = (bf16[512,768]{1,0:T(8,128)(2,1)S(1)}, bf16[512,768]{1,0:T(8,128)(2,1)S(1)}, u32[]{:S(2)}, u32[]{:S(2)}) collective-permute-start(bf16[512,768]{1,0:T(8,128)(2,1)S(1)} %get-tuple-element.96), channel_id=1, source_target_pairs={{0,16},{16,0},{1,17},{17,1},{2,18},{18,2},{3,19},{19,3},{4,20},{20... | collective-permute-start | bytes 2359304 | tf_op jit(solution)/shard_map/ppermute | solution.py:256
  11.8 17.3 %collective-permute-start = (bf16[128,2176]{1,0:T(8,128)(2,1)S(1)}, bf16[128,2176]{1,0:T(8,128)(2,1)S(1)}, u32[]{:S(2)}, u32[]{:S(2)}) collective-permute-start(bf16[128,2176]{1,0:T(8,128)(2,1)S(1)} %packed_tokens.1.refs_2_), channel_id=1, source_target_pairs={{0,4},{1,5},{2,6},{3,7},{4,8},{5,9},{6,10},{7,11},{8,12},{9,13},{1... | collective-permute-start | bytes 1671176 | tf_op jit(solution)/shard_map/ppermute | solution.py:244
  19.2 20.9 %collective-permute-start.1 = (bf16[128,2176]{1,0:T(8,128)(2,1)S(1)}, bf16[128,2176]{1,0:T(8,128)(2,1)S(1)}, u32[]{:S(2)}, u32[]{:S(2)}) collective-permute-start(bf16[128,2176]{1,0:T(8,128)(2,1)S(1)} %packed_tokens.1.refs_2_), channel_id=1, source_target_pairs={{0,12},{1,13},{2,14},{3,15},{4,0},{5,1},{6,2},{7,3},{8,4},{9,5},{1... | collective-permute-start | bytes 1671176 | tf_op jit(solution)/shard_map/ppermute | solution.py:244
  23.1 17.9 %collective-permute-start.4 = (bf16[128,2176]{1,0:T(8,128)(2,1)S(1)}, bf16[128,2176]{1,0:T(8,128)(2,1)S(1)}, u32[]{:S(2)}, u32[]{:S(2)}) collective-permute-start(bf16[128,2176]{1,0:T(8,128)(2,1)S(1)} %collective-permute-done.2.refs_4_), channel_id=1, source_target_pairs={{0,1},{1,0},{2,3},{3,2},{4,5},{5,4},{6,7},{7,6},{8,9},{9,8},{10,11... | collective-permute-start | bytes 1671176 | tf_op jit(solution)/shard_map/ppermute | solution.py:244
  40.1 0.9 copy-start.7
  41.0 15.6 %collective-permute-start.10 = (bf16[128,2176]{1,0:T(8,128)(2,1)S(1)}, bf16[128,2176]{1,0:T(8,128)(2,1)}, u32[]{:S(2)}, u32[]{:S(2)}) collective-permute-start(bf16[128,2176]{1,0:T(8,128)(2,1)S(1)} %collective-permute-done.1.refs_6_), channel_id=1, source_target_pairs={{0,1},{1,0},{2,3},{3,2},{4,5},{5,4},{6,7},{7,6},{8,9},{9,8},{10,11... | collective-permute-start | bytes 1671176 | tf_op jit(solution)/shard_map/ppermute | solution.py:244
  41.0 27.1 %collective-permute-start.8 = (bf16[128,2176]{1,0:T(8,128)(2,1)S(1)}, bf16[128,2176]{1,0:T(8,128)(2,1)}, u32[]{:S(2)}, u32[]{:S(2)}) collective-permute-start(bf16[128,2176]{1,0:T(8,128)(2,1)S(1)} %collective-permute-done.1.refs_6_), channel_id=1, source_target_pairs={{0,2},{1,3},{2,0},{3,1},{4,6},{5,7},{6,4},{7,5},{8,10},{9,11},{10,... | collective-permute-start | bytes 1671176 | tf_op jit(solution)/shard_map/ppermute | solution.py:244
  41.5 0.8 copy-start.18
  42.3 25.7 %collective-permute-start.7 = (bf16[128,2176]{1,0:T(8,128)(2,1)S(1)}, bf16[128,2176]{1,0:T(8,128)(2,1)}, u32[]{:S(2)}, u32[]{:S(2)}) collective-permute-start(bf16[128,2176]{1,0:T(8,128)(2,1)S(1)} %collective-permute-done.refs_2_), channel_id=1, source_target_pairs={{0,2},{1,3},{2,0},{3,1},{4,6},{5,7},{6,4},{7,5},{8,10},{9,11},{10,... | collective-permute-start | bytes 1671176 | tf_op jit(solution)/shard_map/ppermute | solution.py:244
  43.8 24.3 %collective-permute-start.9 = (bf16[128,2176]{1,0:T(8,128)(2,1)S(1)}, bf16[128,2176]{1,0:T(8,128)(2,1)}, u32[]{:S(2)}, u32[]{:S(2)}) collective-permute-start(bf16[128,2176]{1,0:T(8,128)(2,1)S(1)} %collective-permute-done.refs_2_), channel_id=1, source_target_pairs={{0,1},{1,0},{2,3},{3,2},{4,5},{5,4},{6,7},{7,6},{8,9},{9,8},{10,11... | collective-permute-start | bytes 1671176 | tf_op jit(solution)/shard_map/ppermute | solution.py:244
  46.6 0.9 copy-start.10
  47.5 27.3 %collective-permute-start.6 = (bf16[128,2176]{1,0:T(8,128)(2,1)S(1)}, bf16[128,2176]{1,0:T(8,128)(2,1)}, u32[]{:S(2)}, u32[]{:S(2)}) collective-permute-start(bf16[128,2176]{1,0:T(8,128)(2,1)S(1)} %packed_tokens.1.refs_2_), channel_id=1, source_target_pairs={{0,8},{1,9},{2,10},{3,11},{4,12},{5,13},{6,14},{7,15},{8,0},{9,1},... | collective-permute-start | bytes 1671176 | tf_op jit(solution)/shard_map/ppermute | solution.py:244
  50.2 27.6 %copy-start.19 = (bf16[128,2176]{1,0:T(8,128)(2,1)S(1)}, bf16[128,2176]{1,0:T(8,128)(2,1)}, u32[]{:S(2)}) copy-start(bf16[128,2176]{1,0:T(8,128)(2,1)} %copy-done.18) | copy-start | bytes 1671172
  55.2 1.4 %copy-start.2 = (bf16[2,256,2048]{2,1,0:T(8,128)(2,1)}, bf16[2,256,2048]{2,1,0:T(8,128)(2,1)S(1)}, u32[]{:S(2)}) copy-start(bf16[2,256,2048]{2,1,0:T(8,128)(2,1)S(1)} %get-tuple-element.65.refs_3_.x_ref.refs_2_) | copy-start | bytes 6291460
  56.6 31.9 %copy-start.5 = (f32[2,256,768]{2,1,0:T(8,128)}, f32[2,256,768]{2,1,0:T(8,128)S(1)}, u32[]{:S(2)}) copy-start(f32[2,256,768]{2,1,0:T(8,128)S(1)} %get-tuple-element.67.refs_5_.p_ref) | copy-start | bytes 4718596
  56.6 31.9 %copy-start.15 = (f32[2,256,128]{2,1,0:T(8,128)}, f32[2,256,128]{2,1,0:T(8,128)S(1)}, u32[]{:S(2)}) copy-start(f32[2,256,128]{2,1,0:T(8,128)S(1)} %get-tuple-element.66.refs_4_.refs_3_) | copy-start | bytes 786436
  74.8 13.6 %copy-start.8 = (bf16[512,768]{1,0:T(8,128)(2,1)S(1)}, bf16[512,768]{1,0:T(8,128)(2,1)}, u32[]{:S(2)}) copy-start(bf16[512,768]{1,0:T(8,128)(2,1)} %copy-done.7) | copy-start | bytes 2359300
  74.8 13.6 %copy-start.11 = (bf16[512,768]{1,0:T(8,128)(2,1)S(1)}, bf16[512,768]{1,0:T(8,128)(2,1)}, u32[]{:S(2)}) copy-start(bf16[512,768]{1,0:T(8,128)(2,1)} %copy-done.10) | copy-start | bytes 2359300
  74.8 2.6 %collective-permute-start.14 = (bf16[128,2176]{1,0:T(8,128)(2,1)}, bf16[128,2176]{1,0:T(8,128)(2,1)S(1)}, u32[]{:S(2)}, u32[]{:S(2)}) collective-permute-start(bf16[128,2176]{1,0:T(8,128)(2,1)} %collective-permute-done.7.refs_4_), channel_id=1, source_target_pairs={{0,1},{1,0},{2,3},{3,2},{4,5},{5,4},{6,7},{7,6},{8,9},{9,8},{10,11... | collective-permute-start | bytes 1671176 | tf_op jit(solution)/shard_map/ppermute | solution.py:244
  74.8 3.0 %collective-permute-start.15 = (bf16[128,2176]{1,0:T(8,128)(2,1)}, bf16[128,2176]{1,0:T(8,128)(2,1)S(1)}, u32[]{:S(2)}, u32[]{:S(2)}) collective-permute-start(bf16[128,2176]{1,0:T(8,128)(2,1)} %collective-permute-done.8.refs_8_), channel_id=1, source_target_pairs={{0,1},{1,0},{2,3},{3,2},{4,5},{5,4},{6,7},{7,6},{8,9},{9,8},{10,11... | collective-permute-start | bytes 1671176 | tf_op jit(solution)/shard_map/ppermute | solution.py:244
  75.3 18.7 %collective-permute-start.13 = (bf16[128,2176]{1,0:T(8,128)(2,1)}, bf16[128,2176]{1,0:T(8,128)(2,1)}, u32[]{:S(2)}, u32[]{:S(2)}) collective-permute-start(bf16[128,2176]{1,0:T(8,128)(2,1)} %collective-permute-done.6.refs_2_), channel_id=1, source_target_pairs={{0,2},{1,3},{2,0},{3,1},{4,6},{5,7},{6,4},{7,5},{8,10},{9,11},{10,... | collective-permute-start | bytes 1671176 | tf_op jit(solution)/shard_map/ppermute | solution.py:244
  75.8 20.3 %collective-permute-start.17 = (bf16[512,768]{1,0:T(8,128)(2,1)}, bf16[512,768]{1,0:T(8,128)(2,1)S(1)}, u32[]{:S(2)}, u32[]{:S(2)}) collective-permute-start(bf16[512,768]{1,0:T(8,128)(2,1)} %get-tuple-element.77), channel_id=1, source_target_pairs={{0,16},{16,0},{1,17},{17,1},{2,18},{18,2},{3,19},{19,3},{4,20},{20... | collective-permute-start | bytes 2359304 | tf_op jit(solution)/shard_map/ppermute | solution.py:256
  88.4 5.5 %copy-start.13 = (f32[2,512,128]{2,1,0:T(8,128)}, f32[2,512,128]{2,1,0:T(8,128)S(1)}, u32[]{:S(2)}) copy-start(f32[2,512,128]{2,1,0:T(8,128)S(1)} %get-tuple-element.89.refs_7_.refs_6_) | copy-start | bytes 1572868
  88.5 7.6 %copy-start.3 = (bf16[2,256,2048]{2,1,0:T(8,128)(2,1)S(1)}, bf16[2,256,2048]{2,1,0:T(8,128)(2,1)}, u32[]{:S(2)}) copy-start(bf16[2,256,2048]{2,1,0:T(8,128)(2,1)} %copy-done.2) | copy-start | bytes 6291460
  94.0 6.6 %collective-permute-start.16 = (bf16[128,2176]{1,0:T(8,128)(2,1)}, bf16[128,2176]{1,0:T(8,128)(2,1)}, u32[]{:S(2)}, u32[]{:S(2)}) collective-permute-start(bf16[128,2176]{1,0:T(8,128)(2,1)} %collective-permute-done.13.refs_4_), channel_id=1, source_target_pairs={{0,1},{1,0},{2,3},{3,2},{4,5},{5,4},{6,7},{7,6},{8,9},{9,8},{10,11... | collective-permute-start | bytes 1671176 | tf_op jit(solution)/shard_map/ppermute | solution.py:244
  94.2 6.4 %collective-permute-start.12 = (bf16[128,2176]{1,0:T(8,128)(2,1)}, bf16[128,2176]{1,0:T(8,128)(2,1)}, u32[]{:S(2)}, u32[]{:S(2)}) collective-permute-start(bf16[128,2176]{1,0:T(8,128)(2,1)} %collective-permute-done.6.refs_2_), channel_id=1, source_target_pairs={{0,1},{1,0},{2,3},{3,2},{4,5},{5,4},{6,7},{7,6},{8,9},{9,8},{10,11... | collective-permute-start | bytes 1671176 | tf_op jit(solution)/shard_map/ppermute | solution.py:244
  94.6 3.8 %copy-start.4 = (f32[2,512,768]{2,1,0:T(8,128)S(1)}, f32[2,512,768]{2,1,0:T(8,128)}, u32[]{:S(2)}) copy-start(f32[2,512,768]{2,1,0:T(8,128)} %get-tuple-element.79.refs_8_.p_ref) | copy-start | bytes 9437188
  94.6 20.7 %collective-permute-start.19 = (bf16[512,768]{1,0:T(8,128)(2,1)}, bf16[512,768]{1,0:T(8,128)(2,1)}, u32[]{:S(2)}, u32[]{:S(2)}) collective-permute-start(bf16[512,768]{1,0:T(8,128)(2,1)} %get-tuple-element.87), channel_id=1, source_target_pairs={{0,16},{16,0},{1,17},{17,1},{2,18},{18,2},{3,19},{19,3},{4,20},{20... | collective-permute-start | bytes 2359304 | tf_op jit(solution)/shard_map/ppermute | solution.py:256
  96.1 1.4 %copy-start.6 = (f32[2,256,768]{2,1,0:T(8,128)S(1)}, f32[2,256,768]{2,1,0:T(8,128)}, u32[]{:S(2)}) copy-start(f32[2,256,768]{2,1,0:T(8,128)} %copy-done.5) | copy-start | bytes 4718596
  100.6 8.2 %copy-start.9 = (bf16[512,768]{1,0:T(8,128)(2,1)S(1)}, bf16[512,768]{1,0:T(8,128)(2,1)}, u32[]{:S(2)}) copy-start(bf16[512,768]{1,0:T(8,128)(2,1)} %copy-done.7) | copy-start | bytes 2359300
  100.6 8.2 %copy-start.12 = (bf16[512,768]{1,0:T(8,128)(2,1)S(1)}, bf16[512,768]{1,0:T(8,128)(2,1)}, u32[]{:S(2)}) copy-start(bf16[512,768]{1,0:T(8,128)(2,1)} %copy-done.10) | copy-start | bytes 2359300
  106.4 1.4 %copy-start = (bf16[2,256,2048]{2,1,0:T(8,128)(2,1)}, bf16[2,256,2048]{2,1,0:T(8,128)(2,1)S(1)}, u32[]{:S(2)}) copy-start(bf16[2,256,2048]{2,1,0:T(8,128)(2,1)S(1)} %get-tuple-element.81.refs_3_.x_ref.refs_8_) | copy-start | bytes 6291460
  107.8 14.4 %collective-permute-start.21 = (f32[2,1024]{1,0:T(2,128)S(1)}, f32[2,1024]{1,0:T(2,128)S(1)}, u32[]{:S(2)}, u32[]{:S(2)}) collective-permute-start(f32[2,1024]{1,0:T(2,128)S(1)} %constant_dynamic-slice_fusion), channel_id=1, source_target_pairs={{0,16},{16,0},{1,17},{17,1},{2,18},{18,2},{3,19},{19,3},{4,20},{20... | collective-permute-start | bytes 24584 | tf_op jit(solution)/shard_map/ppermute | solution.py:256
  108.9 3.7 %copy-start.1 = (bf16[2,256,2048]{2,1,0:T(8,128)(2,1)S(1)}, bf16[2,256,2048]{2,1,0:T(8,128)(2,1)}, u32[]{:S(2)}) copy-start(bf16[2,256,2048]{2,1,0:T(8,128)(2,1)} %copy-done) | copy-start | bytes 6291460
  111.4 3.9 %copy-start.14 = (f32[2,512,128]{2,1,0:T(8,128)S(1)}, f32[2,512,128]{2,1,0:T(8,128)}, u32[]{:S(2)}) copy-start(f32[2,512,128]{2,1,0:T(8,128)} %copy-done.13) | copy-start | bytes 1572868
  111.4 3.8 %copy-start.16 = (f32[2,256,128]{2,1,0:T(8,128)S(1)}, f32[2,256,128]{2,1,0:T(8,128)}, u32[]{:S(2)}) copy-start(f32[2,256,128]{2,1,0:T(8,128)} %copy-done.15) | copy-start | bytes 786436
  111.4 11.4 %collective-permute-start.18 = (bf16[192,384]{1,0:T(8,128)(2,1)S(1)}, bf16[192,384]{1,0:T(8,128)(2,1)S(1)}, u32[]{:S(2)}, u32[]{:S(2)}) collective-permute-start(bf16[192,384]{1,0:T(8,128)(2,1)S(1)} %get-tuple-element.86), channel_id=1, source_target_pairs={{0,16},{16,0},{1,17},{17,1},{2,18},{18,2},{3,19},{19,3},{4,20},{20... | collective-permute-start | bytes 442376 | tf_op jit(solution)/shard_map/ppermute | solution.py:256
  120.7 5.2 %collective-permute-start.20 = (bf16[192,384]{1,0:T(8,128)(2,1)S(1)}, bf16[192,384]{1,0:T(8,128)(2,1)S(1)}, u32[]{:S(2)}, u32[]{:S(2)}) collective-permute-start(bf16[192,384]{1,0:T(8,128)(2,1)S(1)} %get-tuple-element.92), channel_id=1, source_target_pairs={{0,16},{16,0},{1,17},{17,1},{2,18},{18,2},{3,19},{19,3},{4,20},{20... | collective-permute-start | bytes 442376 | tf_op jit(solution)/shard_map/ppermute | solution.py:256

commit v2 on v0

v2 whole, which is shorter than its diff:
```python
import functools
import math

import jax
import jax.numpy as jnp
from jax import lax
from jax.experimental import pallas as pl
from jax.experimental.pallas import tpu as pltpu
from jax.sharding import PartitionSpec as P

VMEM_LIMIT = 18 * 1024 * 1024
FIRST_LIMIT = 60 * 1024 * 1024
VM = pl.BlockSpec(memory_space=pltpu.VMEM)
SM = pl.BlockSpec(memory_space=pltpu.SMEM)


def params(limit=VMEM_LIMIT):
    return pltpu.CompilerParams(vmem_limit_bytes=limit)


def cost(flops, moved):
    return pl.CostEstimate(flops=16 * int(flops), bytes_accessed=16 * int(moved), transcendentals=0)


def pack_kernel(experts, tok_ref, routes_ref, shares_ref, w_ref, out_ref, piece_ref, small_ref, sems):
    rows, width = tok_ref.shape
    top = routes_ref.shape[0]
    extra = out_ref.shape[1] - width
    copies = [
        pltpu.make_async_copy(source, target, sems.at[k])
        for k, (source, target) in enumerate(
            (
                (routes_ref, small_ref.at[0]),
                (shares_ref, small_ref.at[1]),
                (tok_ref, out_ref.at[:, pl.ds(0, width)]),
                (w_ref.at[pl.ds(0, piece_ref.shape[0]), :], piece_ref),
            )
        )
    ]
    for copy in copies:
        copy.start()
    copies[0].wait()
    copies[1].wait()
    routes, shares = small_ref[0].T, small_ref[1].T
    lane = lax.broadcasted_iota(jnp.int32, (rows, extra), 1)
    expert = jnp.where(lane < experts, lane, lane - experts)
    value = jnp.zeros((rows, extra), jnp.int32)
    for k in range(top):
        value = value + jnp.where(routes[:, k : k + 1] == expert, shares[:, k : k + 1], 0)
    share = value.astype(jnp.float32) / 65536.0
    high = share.astype(jnp.bfloat16).astype(jnp.float32)
    low = share - high
    out_ref[:, width:] = jnp.where(lane < experts, high, low).astype(jnp.bfloat16)
    copies[2].wait()
    copies[3].wait()


def pick_kernel(experts, cap, count, *refs):
    where_ref = refs[0]
    blocks = refs[1 : 1 + count]
    own_ref, other_ref = refs[1 + count :]
    rows, full = blocks[0].shape
    local = own_ref.shape[0] // (count * cap)
    extra = -(-2 * experts // 128) * 128
    width = full - extra
    lane = lax.broadcasted_iota(jnp.int32, (1, extra), 1)
    slot = lax.broadcasted_iota(jnp.int32, (1, cap), 1).astype(jnp.float32)
    below = (
        lax.broadcasted_iota(jnp.int32, (rows, rows), 0)
        > lax.broadcasted_iota(jnp.int32, (rows, rows), 1)
    ).astype(jnp.bfloat16)
    firsts = (where_ref[0] * local, where_ref[1] * local)
    lives = []
    for block in blocks:
        side = block[:, width:].astype(jnp.float32)
        lives.append(jnp.where((side > 0.0) & (lane < experts), 1.0, 0.0))
    live = jnp.concatenate(lives, axis=1)
    rank = jnp.dot(below, live.astype(jnp.bfloat16), preferred_element_type=jnp.float32)
    place = jnp.where(live > 0.0, rank, -1.0)
    picks = []
    for b in range(count):
        at = place[:, b * extra : (b + 1) * extra]
        mine = [
            jnp.sum(jnp.where(lane == first + i, at, 0.0), axis=1, keepdims=True)
            for first in firsts
            for i in range(local)
        ]
        pick = jnp.concatenate([jnp.where(m == slot, 1.0, 0.0) for m in mine], axis=1)
        picks.append(pick.astype(jnp.bfloat16))
    for b, block in enumerate(blocks):
        taken = lax.dot_general(
            picks[b], block[...], (((0,), (0,)), ((), ())), preferred_element_type=jnp.float32
        ).astype(jnp.bfloat16)
        for k, ref in enumerate((own_ref, other_ref)):
            for i in range(local):
                at = (i * count + b) * cap
                got = (k * local + i) * cap
                ref[at : at + cap, :] = taken[got : got + cap]


def picked(experts, cap, local, where, blocks):
    count = len(blocks)
    rows, full = blocks[0].shape
    out = jax.ShapeDtypeStruct((local * count * cap, full), jnp.bfloat16)
    return pl.pallas_call(
        functools.partial(pick_kernel, experts, cap, count),
        out_shape=(out, out),
        in_specs=[SM] + [VM] * count,
        out_specs=(VM, VM),
        compiler_params=params(),
        cost_estimate=cost(
            4 * count * rows * local * cap * full, 2 * count * full * (rows + 2 * local * cap)
        ),
        name="picked_rows",
    )(where, *blocks)


def hidden_terms(value, share):
    wide = value.shape[1] // 2
    gate = value[:, :wide]
    hidden = (gate / (1.0 + jnp.exp(-gate)) * value[:, wide:]).astype(jnp.bfloat16)
    weighted = hidden.astype(jnp.float32) * share
    high = weighted.astype(jnp.bfloat16)
    low = (weighted - high.astype(jnp.float32)).astype(jnp.bfloat16)
    return hidden, high, low


def gram_terms(hidden_ref, weighted_ref):
    wide = hidden_ref.shape[1]
    both = lax.dot_general(
        hidden_ref[...],
        weighted_ref[...],
        (((0,), (0,)), ((), ())),
        preferred_element_type=jnp.float32,
    )
    return both[:, :wide] + both[:, wide:]


def hidden_and_gram(value, share, hidden_ref, weighted_ref):
    wide = hidden_ref.shape[1]
    hidden_ref[...], weighted_ref[:, :wide], weighted_ref[:, wide:] = hidden_terms(value, share)
    return gram_terms(hidden_ref, weighted_ref)


def give_out(total, seq, own_ref, send_ref, hold_ref):
    hold_ref[...] = total
    part = own_ref.shape[0]
    own_ref[...] = hold_ref[pl.ds(pl.multiple_of(seq * part, 16), part), :]
    send_ref[...] = hold_ref[pl.ds(pl.multiple_of((1 - seq) * part, 16), part), :].astype(
        jnp.bfloat16
    )


def experts_kernel(experts, pieces, count, carried, final, factor, *refs):
    where_ref, w_ref = refs[:2]
    far_refs = refs[2 : 2 + pieces]
    groups = refs[2 + pieces : 2 + pieces + count]
    rest = refs[2 + pieces + count :]
    if carried:
        gram_in_ref, max_in_ref = rest[:2]
        rest = rest[2:]
    max_ref, p_ref, late_ref = rest[:3]
    hidden_ref, weighted_ref = rest[-2:]
    rest = rest[3:-2]
    local, depth, fan = w_ref.shape
    extra = -(-2 * experts // 128) * 128
    width = groups[0].shape[1] - extra
    lane = lax.broadcasted_iota(jnp.int32, (1, extra), 1)
    first, seq = where_ref[0] * local, where_ref[2]
    near, far = pl.multiple_of(seq * depth, 128), pl.multiple_of((1 - seq) * depth, 128)

    def part(i, columns):
        each = [g.shape[0] // local for g in groups]
        return jnp.concatenate(
            [g[i * n : (i + 1) * n, columns] for g, n in zip(groups, each)], axis=0
        )

    def share_of(i):
        both = (lane == first + i) | (lane == experts + first + i)
        side = part(i, slice(width, width + extra)).astype(jnp.float32)
        return jnp.sum(jnp.where(both, side, 0.0), axis=1, keepdims=True)

    def product(a, w):
        return jnp.dot(a, w, preferred_element_type=jnp.float32)

    values = [product(part(i, pl.ds(near, depth)), w_ref[i]) for i in range(local)]
    at = 0
    for far_ref in far_refs:
        end = at + far_ref.shape[0]
        for i in range(local):
            low, high = max(at, i * depth), min(end, (i + 1) * depth)
            if low < high:
                columns = pl.ds(pl.multiple_of(far + low - i * depth, 128), high - low)
                values[i] = values[i] + product(part(i, columns), far_ref[low - at : high - at, :])
        at = end
    known = at - depth
    total = hidden_and_gram(values[0], share_of(0), hidden_ref, weighted_ref)
    p_ref[:, :fan] = values[1]
    p_ref[:, fan:] = jnp.broadcast_to(share_of(1), (p_ref.shape[0], 128))
    late_ref[...] = part(1, pl.ds(pl.multiple_of(far + known, 128), depth - known))
    for i in range(local):
        size = jnp.abs(part(i, slice(0, width)))
        largest = max_in_ref[i * 16 : (i + 1) * 16, :] if carried else size[:16]
        for r in range(0 if carried else 16, size.shape[0], 16):
            largest = jnp.maximum(largest, size[r : r + 16])
        max_ref[i * 16 : (i + 1) * 16, :] = largest
    if carried:
        total = total + gram_in_ref[...]
    if final:
        give_out(total * factor, seq, *rest)
    else:
        rest[0][...] = total


def experts_of(experts, where, weights, far, groups, carried, final, factor):
    local, depth, fan = weights.shape
    wide = fan // 2
    rows = sum(g.shape[0] for g in groups) // local
    width = 2 * depth
    out = [
        jax.ShapeDtypeStruct((local * 16, width), jnp.bfloat16),
        jax.ShapeDtypeStruct((rows, fan + 128), jnp.float32),
        jax.ShapeDtypeStruct((rows, 2 * depth - depth_of(far)), jnp.bfloat16),
    ]
    scratch = [pltpu.VMEM((rows, wide), jnp.bfloat16), pltpu.VMEM((rows, fan), jnp.bfloat16)]
    if final:
        out += [
            jax.ShapeDtypeStruct((wide // 2, wide), jnp.float32),
            jax.ShapeDtypeStruct((wide // 2, wide), jnp.bfloat16),
        ]
        scratch = [pltpu.VMEM((wide, wide), jnp.float32)] + scratch
    else:
        out.append(jax.ShapeDtypeStruct((wide, wide), jnp.float32))
    ins = [weights, *far, *groups, *(carried or ())]
    return pl.pallas_call(
        functools.partial(experts_kernel, experts, len(far), len(groups), bool(carried), final, factor),
        out_shape=tuple(out),
        in_specs=[SM] + [VM] * len(ins),
        out_specs=(VM,) * len(out),
        scratch_shapes=scratch,
        compiler_params=params(),
        cost_estimate=cost(2 * rows * (depth + depth_of(far)) * fan, 0),
        name="expert_terms",
    )(where, *ins)


def more_kernel(pieces, count, *refs):
    w_refs = refs[:pieces]
    outs = refs[pieces + 2 * count :]
    fan = w_refs[0].shape[1]
    for g in range(count):
        x_ref, p_ref = refs[pieces + 2 * g : pieces + 2 * g + 2]
        value, at = p_ref[:, :fan], 0
        for w_ref in w_refs:
            depth = w_ref.shape[0]
            value = value + jnp.dot(
                x_ref[:, at : at + depth], w_ref[...], preferred_element_type=jnp.float32
            )
            at += depth
        outs[g][:, :fan] = value


def more_of(weights, parts):
    ins = [array for part in parts for array in part]
    return pl.pallas_call(
        functools.partial(more_kernel, len(weights), len(parts)),
        out_shape=tuple(jax.ShapeDtypeStruct(p.shape, p.dtype) for _, p in parts),
        in_specs=[VM] * (len(weights) + len(ins)),
        out_specs=(VM,) * len(parts),
        input_output_aliases={len(weights) + 2 * g + 1: g for g in range(len(parts))},
        compiler_params=params(),
        cost_estimate=cost(
            2 * sum(p.shape[0] for _, p in parts) * depth_of(weights) * weights[0].shape[1], 0
        ),
        name="more_terms",
    )(*weights, *ins)


def last_kernel(step, firsts, factor, *refs):
    where_ref, w_ref = refs[:2]
    count = len(firsts) - 1
    groups = refs[2 : 2 + 2 * count]
    own_ref, send_ref, hold_ref, hidden_ref, weighted_ref = refs[2 + 2 * count :]
    fan = w_ref.shape[1]
    wide = fan // 2
    now = pl.program_id(0)
    for g in range(count):

        @pl.when((now >= firsts[g]) & (now < firsts[g + 1]))
        def _(g=g):
            x_ref, p_ref = groups[2 * g : 2 * g + 2]
            value = p_ref[:, :fan] + jnp.dot(
                x_ref[...], w_ref[...], preferred_element_type=jnp.float32
            )
            hidden, high, low = hidden_terms(value, p_ref[:, fan : fan + 1])
            rows = pl.ds(pl.multiple_of(now * step, step), step)
            hidden_ref[rows, :] = hidden
            weighted_ref[rows, :wide] = high
            weighted_ref[rows, wide:] = low

    @pl.when(now == firsts[-1] - 1)
    def _():
        total = gram_terms(hidden_ref, weighted_ref)
        give_out(total * factor, where_ref[2], own_ref, send_ref, hold_ref)


def last_of(where, weights, parts, factor):
    depth, fan = weights.shape
    wide = fan // 2
    rows = [p.shape[0] for _, p in parts]
    step = functools.reduce(math.gcd, rows, 256)
    firsts = [0]
    ins, specs = [], []
    for x, p in parts:
        first, number = firsts[-1], p.shape[0] // step
        firsts.append(first + number)
        for array, columns in ((x, depth), (p, p.shape[1])):
            ins.append(array)
            specs.append(
                pl.BlockSpec(
                    (step, columns),
                    lambda g, first=first, number=number, at=array.shape[1] // columns - 1: (
                        jnp.clip(g - first, 0, number - 1),
                        at,
                    ),
                )
            )
    return pl.pallas_call(
        functools.partial(last_kernel, step, tuple(firsts), factor),
        grid=(firsts[-1],),
        out_shape=(
            jax.ShapeDtypeStruct((wide // 2, wide), jnp.float32),
            jax.ShapeDtypeStruct((wide // 2, wide), jnp.bfloat16),
        ),
        in_specs=[SM, pl.BlockSpec(weights.shape, lambda g: (0, 0))] + specs,
        out_specs=(pl.BlockSpec((wide // 2, wide), lambda g: (0, 0)),) * 2,
        scratch_shapes=[
            pltpu.VMEM((wide, wide), jnp.float32),
            pltpu.VMEM((sum(rows), wide), jnp.bfloat16),
            pltpu.VMEM((sum(rows), fan), jnp.bfloat16),
        ],
        compiler_params=params(),
        cost_estimate=cost(2 * sum(rows) * depth * fan, 0),
        name="last_terms",
    )(where, weights, *ins)


def depth_of(weights):
    return sum(w.shape[0] for w in weights)


def split_kernel(pieces, w_ref, after_ref, *refs):
    outs, sems = refs[: len(pieces)], refs[len(pieces)]
    copies = [
        pltpu.make_async_copy(w_ref.at[pl.ds(r, n), :], out, sems.at[k])
        for k, ((r, n), out) in enumerate(zip(pieces, outs))
    ]
    for copy in copies:
        copy.start()
    for copy in copies:
        copy.wait()


def split_of(flat, after, pieces):
    anywhere = pl.BlockSpec(memory_space=pl.ANY)
    return pl.pallas_call(
        functools.partial(split_kernel, pieces),
        out_shape=tuple(jax.ShapeDtypeStruct((n, flat.shape[1]), flat.dtype) for _, n in pieces),
        in_specs=[anywhere, anywhere],
        out_specs=(anywhere,) * len(pieces),
        scratch_shapes=[pltpu.SemaphoreType.DMA((len(pieces),))],
        compiler_params=params(),
        cost_estimate=cost(0, 0),
        name="weight_pieces",
    )(flat, after)


def tie(*arrays):
    return lax.optimization_barrier(arrays)


def gather_body(capacity, tokens, routes, gate_shares, gate_up):
    tok_rows, width = tokens.shape
    top_count = routes.shape[1]
    expert_count = lax.axis_size("expert")
    seq_count = lax.axis_size("seq")
    local_count, depth, fan = gate_up.shape
    all_experts = local_count * expert_count
    factor = all_experts / (tok_rows * seq_count * expert_count * top_count)
    columns = expert_count // 4

    def moved(array, target):
        places = [(z, x, c) for z in range(columns) for x in range(2) for c in range(2)]
        number = {place: n for n, place in enumerate(places)}
        return lax.ppermute(array, "expert", [(number[p], number[target(*p)]) for p in places])

    def hop(array, pairs):
        return lax.ppermute(
            array, "expert", [(4 * a + n, 4 * b + n) for a, b in pairs for n in range(4)]
        )

    def along_x(array):
        return moved(array, lambda z, x, c: (z, 1 - x, c))

    def along_core(array):
        return moved(array, lambda z, x, c: (z, x, 1 - c))

    def swapped(array):
        return lax.ppermute(array, "seq", [(0, 1), (1, 0)])

    index, seq = lax.axis_index("expert"), lax.axis_index("seq")
    where = jnp.stack([index, index + 1 - 2 * (index % 2), seq]).astype(jnp.int32)
    extra = -(-2 * all_experts // 128) * 128
    flat = gate_up.reshape(local_count * depth, fan)
    cuts = [depth // 8 * n for n in (0, 8, 11, 14, 16)]
    spans = [(low, high - low) for low, high in zip(cuts, cuts[1:])]
    anywhere = pl.BlockSpec(memory_space=pl.ANY)
    own, piece = pl.pallas_call(
        functools.partial(pack_kernel, all_experts),
        out_shape=(
            jax.ShapeDtypeStruct((tok_rows, width + extra), jnp.bfloat16),
            jax.ShapeDtypeStruct((spans[0][1], fan), jnp.bfloat16),
        ),
        in_specs=[anywhere] * 4,
        out_specs=(VM, VM),
        scratch_shapes=[
            pltpu.VMEM((2, top_count, tok_rows), jnp.int32),
            pltpu.SemaphoreType.DMA((4,)),
        ],
        compiler_params=params(FIRST_LIMIT),
        cost_estimate=cost(0, 4 * tok_rows * width),
        name="packed_tokens",
    )(tokens, routes.T, gate_shares.T, flat)
    far1 = swapped(piece)
    pick = functools.partial(picked, all_experts, capacity, local_count, where)
    terms = functools.partial(experts_of, all_experts, where, gate_up)

    outer = (index // 4 == 0) | (index // 4 == columns - 1)
    za, zm, x0 = hop(own, ((0, 1), (1, 0), (2, 3), (3, 2))), hop(own, ((1, 2), (2, 1))), along_x(own)
    pieces = split_of(flat, own, tuple(spans[1:]))
    own, za, zm, x0, *pieces = tie(own, za, zm, x0, *pieces)
    zo, zi, xa = hop(zm, ((1, 0), (2, 3))), hop(za, ((1, 2), (2, 1))), along_x(za)
    m0, o0 = pick((own, x0))
    zc = jnp.where(outer, zo, zi)
    zc, xa, o0, far1, zm, za, *pieces = tie(zc, xa, o0, far1, zm, za, *pieces)
    zr, xc = hop(zc, ((1, 0), (2, 3))), along_x(zc)
    far2 = swapped(pieces[0])
    r0 = along_core(o0)
    m1, o1 = pick((za, xa))
    zb = jnp.where(outer, zr, zm)
    zb, xc, r0, o1, zc, far2, *pieces = tie(zb, xc, r0, o1, zc, far2, *pieces)
    xb = along_x(zb)
    r1 = along_core(o1)
    far3 = swapped(pieces[1])
    m2, o2 = pick((zc, xc))
    max0, p0, late0, gram0 = terms((far1,), (m0, r0, m1, r1), None, False, factor)
    xb, o2, gram0, max0, far3, zb, *pieces = tie(xb, o2, gram0, max0, far3, zb, *pieces)
    far4 = swapped(pieces[2])
    r2 = along_core(o2)
    m3, o3 = pick((zb, xb))
    r3 = along_core(o3)
    max0, p1, late1, gram0 = terms((far1,), (m2, r2), (gram0, max0), False, factor)
    p0, p1 = more_of((far2, far3), ((late0, p0), (late1, p1)))
    largest, p2, late2, own0, send0 = terms(
        (far1, far2, far3), (m3, r3), (gram0, max0), True, factor
    )
    got0 = swapped(send0)
    largest = jnp.max(largest.reshape(local_count, -1, width), axis=1).astype(jnp.float32)
    keep = lax.dynamic_slice_in_dim(largest, seq * depth, depth, 1)
    give = lax.dynamic_slice_in_dim(largest, (1 - seq) * depth, depth, 1)
    maxima = jnp.maximum(keep, swapped(give))
    own1, send1 = last_of(where, far4, ((late0, p0), (late1, p1), (late2, p2)), factor)
    got1 = swapped(send1)
    gram = jnp.stack([own0 + got0.astype(jnp.float32), own1 + got1.astype(jnp.float32)])
    return (gram, maxima)


def routed_body(capacity, tokens, routes, gate_shares, gate_up):
    tok_rows, width = tokens.shape
    top_count = routes.shape[1]
    expert_count = lax.axis_size("expert")
    seq_count = lax.axis_size("seq")
    local_count, _, fan = gate_up.shape
    wide = fan // 2
    all_experts = local_count * expert_count
    norm_factor = all_experts / (tok_rows * seq_count * expert_count * top_count)
    chosen = routes.reshape(-1)
    shares = gate_shares.reshape(-1).astype(jnp.float32) / 65536.0
    one_hot = (chosen[:, None] == jnp.arange(all_experts, dtype=jnp.int32)[None, :]).astype(jnp.int32)
    ranked = jnp.sum((jnp.cumsum(one_hot, axis=0) - one_hot) * one_hot, axis=1)
    slot_index = chosen * capacity + ranked
    token_index = jnp.arange(tok_rows * top_count, dtype=jnp.int32) // top_count
    outgoing = (
        jnp.zeros((all_experts * capacity, width), jnp.bfloat16)
        .at[slot_index]
        .set(tokens[token_index])
        .reshape(expert_count, local_count, capacity, width)
    )
    out_shares = (
        jnp.zeros((all_experts * capacity,), jnp.float32)
        .at[slot_index]
        .set(shares)
        .reshape(expert_count, local_count, capacity)
    )
    arrived = lax.all_to_all(outgoing, "expert", split_axis=0, concat_axis=0, tiled=True)
    arrived_shares = lax.all_to_all(out_shares, "expert", split_axis=0, concat_axis=0, tiled=True)
    channel_max = jnp.max(
        jnp.where(arrived_shares[..., None] > 0.0, jnp.abs(arrived), 0), axis=(0, 2)
    ).astype(jnp.float32)
    projected = jnp.einsum(
        "slcd,ldf->lscf",
        arrived,
        lax.all_gather(gate_up, "seq", axis=1, tiled=True),
        preferred_element_type=jnp.float32,
    )
    hidden = (jax.nn.silu(projected[..., :wide]) * projected[..., wide:]).astype(jnp.bfloat16)
    hidden = hidden.reshape(local_count, expert_count * capacity, wide)
    row_shares = jnp.transpose(arrived_shares, (1, 0, 2)).reshape(local_count, -1)
    weighted = hidden.astype(jnp.float32) * row_shares[..., None]
    high = weighted.astype(jnp.bfloat16)
    low = (weighted - high.astype(jnp.float32)).astype(jnp.bfloat16)
    gram = jnp.einsum("lrf,lrg->lfg", hidden, high, preferred_element_type=jnp.float32)
    gram = gram + jnp.einsum("lrf,lrg->lfg", hidden, low, preferred_element_type=jnp.float32)
    gram = lax.psum_scatter(gram * norm_factor, "seq", scatter_dimension=1, tiled=True)
    full_max = lax.pmax(channel_max, "seq")
    part = width // seq_count
    maxima = lax.dynamic_slice_in_dim(full_max, lax.axis_index("seq") * part, part, 1)
    return (gram, maxima)


def body(tokens, routes, gate_shares, gate_up):
    expert_count = lax.axis_size("expert")
    local_count = gate_up.shape[0]
    rows = tokens.shape[0]
    capacity = 2 * rows * routes.shape[1] // (local_count * expert_count)
    whole_rows = rows <= local_count * capacity
    shaped = lax.axis_size("seq") == 2 and expert_count == 16 and local_count == 2
    plan = gather_body if whole_rows and shaped else routed_body
    return plan(capacity, tokens, routes, gate_shares, gate_up)


def solution(mesh):
    return jax.shard_map(
        body,
        mesh=mesh,
        in_specs=(
            P(("seq", "expert"), None),
            P(("seq", "expert"), None),
            P(("seq", "expert"), None),
            P("expert", "seq", None),
        ),
        out_specs=(P("expert", "seq", None), P("expert", "seq")),
        check_vma=False,
    )
```

time: 289 us -> 109 us (0.38)
  waiting for transfers between devices: 190 us -> 36.3 us
  Pallas kernels: 0 us -> 30.3 us
  local copies, waits for them, and re-layouts: 32.3 us -> 14.3 us
  other arithmetic: 16.7 us -> 2.84 us
  matrix products: 13.6 us -> 0 us
  between operations: 14.2 us -> 0.99 us
  starting transfers between devices: 13.5 us -> 23.3 us
  blocking collectives: 8.13 us -> 0 us
    all_gather x1 -> x0, waiting for transfers between devices: 83.2 us -> none  [body(): lax.all_gather(gate_up, 'seq', axis=1, tiled=True)]
    all_to_all x2 -> x0, waiting for transfers between devices: 66.6 us -> none  [the longest x1 66.6 us: body(): lax.all_to_all(outgoing_rows, 'expert', split_axis=0, concat_axis=0, tile...]
    reduce_scatter x1 -> x0, waiting for transfers between devices: 39.8 us -> none  [body(): gram = lax.psum_scatter(gram_part, 'seq', scatter_dimension=1, tiled=True)]
    ppermute x0 -> x20, waiting for transfers between devices: none -> 36.3 us  [the longest x5 25.2 us: hop(): lax.ppermute(array, 'expert', [(4 * a + n, 4 * b + n) for a, b in pairs f...]
    pallas_call x0 -> x11, Pallas kernels: none -> 30.3 us  [the longest x3 13.7 us: experts_of(): pl.pallas_call(functools.partial(experts_kernel, experts, len(far), len(g...]
    scatter x2 -> x0, local copies, waits for them, and re-layouts: 29.2 us -> none  [the longest x1 24.9 us: body(): jnp.zeros((all_experts * capacity, D), jnp.bfloat16).at[slot_index]]
    ppermute x0 -> x20, starting transfers between devices: none -> 23.3 us  [the longest x7 8.81 us: swapped(): return lax.ppermute(array, 'seq', [(0, 1), (1, 0)])]
    dot_general x3 -> x0, matrix products: 13.6 us -> none  [the longest x1 10 us: body(): jnp.einsum('slcd,ldf->lscf', arrived, lax.all_gather(gate_up, 'seq', axis...]
  transfers between devices with their start and end apart: 4 -> 20, of which waited for: 3 -> 8; matrix products, arithmetic and copies ran while one was open for 11% -> 2% of each run, Pallas kernels for 0% -> 25%
where the time goes in v2:
time: 109 us; the launch traced here: 108 us
  waiting for transfers between devices  36.3 us (33%)
  Pallas kernels  30.3 us (28%)
  starting transfers between devices  23.3 us (21%)
  local copies, waits for them, and re-layouts  14.3 us (13%)
  other arithmetic  2.84 us (3%)
    ppermute x5, waiting for transfers between devices, hop(): lax.ppermute(array, 'expert', [(4 * a + n, 4 * b + n) for a, b in pairs f...  25.2 us
    unnamed x54, local copies, waits for them, and re-layouts  14.3 us
    pallas_call x3, Pallas kernels, experts_of(): pl.pallas_call(functools.partial(experts_kernel, experts, len(far), len(g...  13.7 us
    ppermute x7, starting transfers between devices, swapped(): return lax.ppermute(array, 'seq', [(0, 1), (1, 0)])  8.81 us
    ppermute x5, starting transfers between devices, hop(): lax.ppermute(array, 'expert', [(4 * a + n, 4 * b + n) for a, b in pairs f...  8.79 us
    pallas_call x4, Pallas kernels, picked(): pl.pallas_call(functools.partial(pick_kernel, experts, cap, count), out_s...  8.25 us
    ppermute x7, waiting for transfers between devices, swapped(): return lax.ppermute(array, 'seq', [(0, 1), (1, 0)])  8 us
    ppermute x8, starting transfers between devices, moved(): lax.ppermute(array, 'expert', [(number[p], number[target(*p)]) for p in p...  5.66 us
  transfers between devices with their start and end apart: 20, of which 8 were waited for; matrix products, arithmetic and copies ran while one was open for 2% of the time, Pallas kernels for 25%

profile of v2, /device:TPU:0, one launch (start us, length us, event | category | flops | bytes accessed | tf_op | source)
XLA Modules:
  0.0 108.0 jit_solution(10010979562301388160)
XLA Ops:
  0.6 3.1 %packed_tokens.1 = (bf16[128,2176]{1,0:T(8,128)(2,1)}, bf16[1024,768]{1,0:T(8,128)(2,1)}) custom-call(bf16[128,2048]{1,0:T(8,128)(2,1)} %tok_ref.1, s32[8,128]{1,0:T(8,128)} %bitcast.14, s32[8,128]{1,0:T(8,128)} %bitcast.15, bf16[2048,768]{1,0:T(8,128)(2,1)} %bitcast.12), custom_call_target="tpu_custom_call" | custom-call | bytes 16777216 | tf_op jit(solution)/shard_map/packed_tokens/pallas_call | solution.py:418
  3.8 3.1 %collective-permute-start = (bf16[128,2176]{1,0:T(8,128)(2,1)}, bf16[128,2176]{1,0:T(8,128)(2,1)}, u32[]{:S(2)}, u32[]{:S(2)}) collective-permute-start(bf16[128,2176]{1,0:T(8,128)(2,1)} %get-tuple-element.69.after_ref.refs_1_), channel_id=1, source_target_pairs={{0,4},{1,5},{2,6},{3,7},{4,0},{5,1},{6,2},{7,3},{8,12},{9,13},{10,... | collective-permute-start | bytes 1671176 | tf_op jit(solution)/shard_map/ppermute | solution.py:398
  6.9 1.5 %collective-permute-start.1 = (bf16[128,2176]{1,0:T(8,128)(2,1)}, bf16[128,2176]{1,0:T(8,128)(2,1)}, u32[]{:S(2)}, u32[]{:S(2)}) collective-permute-start(bf16[128,2176]{1,0:T(8,128)(2,1)} %get-tuple-element.69.after_ref.refs_1_), channel_id=1, source_target_pairs={{4,8},{5,9},{6,10},{7,11},{8,4},{9,5},{10,6},{11,7},{20,24},{21,25... | collective-permute-start | bytes 1671176 | tf_op jit(solution)/shard_map/ppermute | solution.py:398
  8.4 1.5 %collective-permute-start.2 = (bf16[128,2176]{1,0:T(8,128)(2,1)}, bf16[128,2176]{1,0:T(8,128)(2,1)S(1)}, u32[]{:S(2)}, u32[]{:S(2)}) collective-permute-start(bf16[128,2176]{1,0:T(8,128)(2,1)} %get-tuple-element.69.after_ref.refs_1_), channel_id=1, source_target_pairs={{0,2},{1,3},{2,0},{3,1},{4,6},{5,7},{6,4},{7,5},{8,10},{9,11},{10,... | collective-permute-start | bytes 1671176 | tf_op jit(solution)/shard_map/ppermute | solution.py:395
  9.8 1.5 %collective-permute-start.6 = (bf16[1024,768]{1,0:T(8,128)(2,1)}, bf16[1024,768]{1,0:T(8,128)(2,1)}, u32[]{:S(2)}, u32[]{:S(2)}) collective-permute-start(bf16[1024,768]{1,0:T(8,128)(2,1)} %get-tuple-element.72), channel_id=1, source_target_pairs={{0,16},{16,0},{1,17},{17,1},{2,18},{18,2},{3,19},{19,3},{4,20},{20... | collective-permute-start | bytes 4718600 | tf_op jit(solution)/shard_map/ppermute | solution.py:409
  11.4 1.1 copy-done.1
  12.9 0.8 copy-done.5
  13.7 0.8 copy-done.7
  14.5 5.3 %collective-permute-done.refs_1_ = bf16[128,2176]{1,0:T(8,128)(2,1)} collective-permute-done((bf16[128,2176]{1,0:T(8,128)(2,1)}, bf16[128,2176]{1,0:T(8,128)(2,1)}, u32[]{:S(2)}, u32[]{:S(2)}) %collective-permute-start) | collective-permute-done | bytes 557088 | tf_op jit(solution)/shard_map/ppermute | solution.py:398
  19.8 2.8 %collective-permute-done.2.refs_2_ = bf16[128,2176]{1,0:T(8,128)(2,1)S(1)} collective-permute-done((bf16[128,2176]{1,0:T(8,128)(2,1)}, bf16[128,2176]{1,0:T(8,128)(2,1)S(1)}, u32[]{:S(2)}, u32[]{:S(2)}) %collective-permute-start.2) | collective-permute-done | bytes 557088 | tf_op jit(solution)/shard_map/ppermute | solution.py:395
  22.7 0.8 copy-done.13
  23.5 1.5 %collective-permute-start.4 = (bf16[128,2176]{1,0:T(8,128)(2,1)}, bf16[128,2176]{1,0:T(8,128)(2,1)}, u32[]{:S(2)}, u32[]{:S(2)}) collective-permute-start(bf16[128,2176]{1,0:T(8,128)(2,1)} %collective-permute-done.refs_1_), channel_id=1, source_target_pairs={{4,8},{5,9},{6,10},{7,11},{8,4},{9,5},{10,6},{11,7},{20,24},{21,25... | collective-permute-start | bytes 1671176 | tf_op jit(solution)/shard_map/ppermute | solution.py:398
  24.9 1.3 %collective-permute-start.3 = (bf16[128,2176]{1,0:T(8,128)(2,1)}, bf16[128,2176]{1,0:T(8,128)(2,1)}, u32[]{:S(2)}, u32[]{:S(2)}) collective-permute-start(bf16[128,2176]{1,0:T(8,128)(2,1)} %collective-permute-done.1), channel_id=1, source_target_pairs={{4,0},{5,1},{6,2},{7,3},{8,12},{9,13},{10,14},{11,15},{20,16},{21,... | collective-permute-start | bytes 1671176 | tf_op jit(solution)/shard_map/ppermute | solution.py:398
  26.3 1.5 %collective-permute-start.5 = (bf16[128,2176]{1,0:T(8,128)(2,1)}, bf16[128,2176]{1,0:T(8,128)(2,1)S(1)}, u32[]{:S(2)}, u32[]{:S(2)}) collective-permute-start(bf16[128,2176]{1,0:T(8,128)(2,1)} %collective-permute-done.refs_1_), channel_id=1, source_target_pairs={{0,2},{1,3},{2,0},{3,1},{4,6},{5,7},{6,4},{7,5},{8,10},{9,11},{10,... | collective-permute-start | bytes 1671176 | tf_op jit(solution)/shard_map/ppermute | solution.py:395
  27.8 1.1 copy-done.2
  28.9 1.1 copy-done.14
  29.9 1.7 %picked_rows.4 = (bf16[256,2176]{1,0:T(8,128)(2,1)S(1)}, bf16[256,2176]{1,0:T(8,128)(2,1)S(1)}) custom-call(s32[3]{0:T(128)S(1)} %pad_add_fusion.refs_0_, bf16[128,2176]{1,0:T(8,128)(2,1)S(1)} %copy-done.2, bf16[128,2176]{1,0:T(8,128)(2,1)S(1)} %copy-done.14), custom_call_target="tpu_custom_call" | custom-call | flops 4563402752 | bytes 53477376 | tf_op jit(solution)/shard_map/picked_rows/pallas_call | solution.py:105
  31.6 10.2 %collective-permute-done.3 = bf16[128,2176]{1,0:T(8,128)(2,1)} collective-permute-done((bf16[128,2176]{1,0:T(8,128)(2,1)}, bf16[128,2176]{1,0:T(8,128)(2,1)}, u32[]{:S(2)}, u32[]{:S(2)}) %collective-permute-start.3) | collective-permute-done | bytes 557088 | tf_op jit(solution)/shard_map/ppermute | solution.py:398
  41.9 1.1 %broadcast_select_fusion.1.refs_1_ = bf16[128,2176]{1,0:T(8,128)(2,1)S(1)} fusion(bf16[128,2176]{1,0:T(8,128)(2,1)} %collective-permute-done.3, bf16[128,2176]{1,0:T(8,128)(2,1)} %collective-permute-done.4, pred[]{:T(512)S(6)} %or.3), kind=kLoop, calls=%fused_computation.2 | loop fusion | flops 278528 | bytes 1671169 | tf_op jit(solution)/shard_map/jit(_where)/select_n | solution.py:444
  43.0 2.8 %collective-permute-done.6.refs_2_ = bf16[1024,768]{1,0:T(8,128)(2,1)} collective-permute-done((bf16[1024,768]{1,0:T(8,128)(2,1)}, bf16[1024,768]{1,0:T(8,128)(2,1)}, u32[]{:S(2)}, u32[]{:S(2)}) %collective-permute-start.6) | collective-permute-done | bytes 1572896 | tf_op jit(solution)/shard_map/ppermute | solution.py:409
  45.7 1.5 %collective-permute-start.7 = (bf16[128,2176]{1,0:T(8,128)(2,1)S(1)}, bf16[128,2176]{1,0:T(8,128)(2,1)S(1)}, u32[]{:S(2)}, u32[]{:S(2)}) collective-permute-start(bf16[128,2176]{1,0:T(8,128)(2,1)S(1)} %broadcast_select_fusion.1.refs_1_), channel_id=1, source_target_pairs={{4,0},{5,1},{6,2},{7,3},{8,12},{9,13},{10,14},{11,15},{20,16},{21,... | collective-permute-start | bytes 1671176 | tf_op jit(solution)/shard_map/ppermute | solution.py:398
  47.8 1.5 %collective-permute-start.10 = (bf16[384,768]{1,0:T(8,128)(2,1)S(1)}, bf16[384,768]{1,0:T(8,128)(2,1)S(1)}, u32[]{:S(2)}, u32[]{:S(2)}) collective-permute-start(bf16[384,768]{1,0:T(8,128)(2,1)S(1)} %copy-done.8), channel_id=1, source_target_pairs={{0,16},{16,0},{1,17},{17,1},{2,18},{18,2},{3,19},{19,3},{4,20},{20... | collective-permute-start | bytes 1769480 | tf_op jit(solution)/shard_map/ppermute | solution.py:409
  49.3 2.2 %picked_rows.5 = (bf16[256,2176]{1,0:T(8,128)(2,1)S(1)}, bf16[256,2176]{1,0:T(8,128)(2,1)S(1)}) custom-call(s32[3]{0:T(128)S(1)} %pad_add_fusion.refs_0_, bf16[128,2176]{1,0:T(8,128)(2,1)} %collective-permute-done.refs_1_, bf16[128,2176]{1,0:T(8,128)(2,1)S(1)} %collective-permute-done.5.refs_2_), custom_call_target="tpu_custom_call" | custom-call | flops 4563402752 | bytes 53477376 | tf_op jit(solution)/shard_map/picked_rows/pallas_call | solution.py:105
  51.6 9.6 %collective-permute-done.7 = bf16[128,2176]{1,0:T(8,128)(2,1)S(1)} collective-permute-done((bf16[128,2176]{1,0:T(8,128)(2,1)S(1)}, bf16[128,2176]{1,0:T(8,128)(2,1)S(1)}, u32[]{:S(2)}, u32[]{:S(2)}) %collective-permute-start.7) | collective-permute-done | bytes 557088 | tf_op jit(solution)/shard_map/ppermute | solution.py:398
  61.3 2.3 %collective-permute-done.10.refs_3_.refs_0_ = bf16[384,768]{1,0:T(8,128)(2,1)S(1)} collective-permute-done((bf16[384,768]{1,0:T(8,128)(2,1)S(1)}, bf16[384,768]{1,0:T(8,128)(2,1)S(1)}, u32[]{:S(2)}, u32[]{:S(2)}) %collective-permute-start.10) | collective-permute-done | bytes 589856 | tf_op jit(solution)/shard_map/ppermute | solution.py:409
  63.6 1.6 %collective-permute-start.13 = (bf16[384,768]{1,0:T(8,128)(2,1)S(1)}, bf16[384,768]{1,0:T(8,128)(2,1)S(1)}, u32[]{:S(2)}, u32[]{:S(2)}) collective-permute-start(bf16[384,768]{1,0:T(8,128)(2,1)S(1)} %copy-done.6), channel_id=1, source_target_pairs={{0,16},{16,0},{1,17},{17,1},{2,18},{18,2},{3,19},{19,3},{4,20},{20... | collective-permute-start | bytes 1769480 | tf_op jit(solution)/shard_map/ppermute | solution.py:409
  65.2 1.5 %collective-permute-start.11 = (bf16[128,2176]{1,0:T(8,128)(2,1)S(1)}, bf16[128,2176]{1,0:T(8,128)(2,1)S(1)}, u32[]{:S(2)}, u32[]{:S(2)}) collective-permute-start(bf16[128,2176]{1,0:T(8,128)(2,1)S(1)} %broadcast_select_fusion.refs_1_), channel_id=1, source_target_pairs={{0,2},{1,3},{2,0},{3,1},{4,6},{5,7},{6,4},{7,5},{8,10},{9,11},{10,... | collective-permute-start | bytes 1671176 | tf_op jit(solution)/shard_map/ppermute | solution.py:395
  66.7 2.7 %picked_rows.6 = (bf16[256,2176]{1,0:T(8,128)(2,1)S(1)}, bf16[256,2176]{1,0:T(8,128)(2,1)}) custom-call(s32[3]{0:T(128)S(1)} %pad_add_fusion.refs_0_, bf16[128,2176]{1,0:T(8,128)(2,1)S(1)} %broadcast_select_fusion.1.refs_1_, bf16[128,2176]{1,0:T(8,128)(2,1)S(1)} %collective-permute-done.8.refs_2_), custom_call_target="tpu_custom_call" | custom-call | flops 4563402752 | bytes 53477376 | tf_op jit(solution)/shard_map/picked_rows/pallas_call | solution.py:105
  69.3 1.0 copy-done.19
  70.4 5.4 %expert_terms.3 = (bf16[32,2048]{1,0:T(8,128)(2,1)S(1)}, f32[512,896]{1,0:T(8,128)S(1)}, bf16[512,1024]{1,0:T(8,128)(2,1)S(1)}, f32[384,384]{1,0:T(8,128)S(1)}) custom-call(s32[3]{0:T(128)S(1)} %pad_add_fusion.refs_0_, bf16[2,1024,768]{2,1,0:T(8,128)(2,1)S(1)} %copy-done, bf16[1024,768]{1,0:T(8,128)(2,1)} %collective-permute-done.6.refs_2_, ...), custom_call_target="tpu_custom_call" | custom-call | flops 25769803776 | tf_op jit(solution)/shard_map/expert_terms/pallas_call | solution.py:235
  75.8 1.3 %copy-done.17 = f32[512,896]{1,0:T(8,128)} copy-done((f32[512,896]{1,0:T(8,128)}, f32[512,896]{1,0:T(8,128)S(1)}, u32[]{:S(2)}) %copy-start.17) | copy-done | bytes 1835032
  77.0 1.0 copy-done.21
  78.1 0.8 copy-done.23
  78.9 0.7 copy-done.25
  79.9 0.8 copy-done.15
  80.7 0.9 copy-done.11
  81.6 1.1 copy-done.4
  82.6 1.1 copy-done.16
  83.7 1.7 %picked_rows.7 = (bf16[256,2176]{1,0:T(8,128)(2,1)S(1)}, bf16[256,2176]{1,0:T(8,128)(2,1)S(1)}) custom-call(s32[3]{0:T(128)S(1)} %pad_add_fusion.refs_0_, bf16[128,2176]{1,0:T(8,128)(2,1)S(1)} %copy-done.4, bf16[128,2176]{1,0:T(8,128)(2,1)S(1)} %copy-done.16), custom_call_target="tpu_custom_call" | custom-call | flops 4563402752 | bytes 53477376 | tf_op jit(solution)/shard_map/picked_rows/pallas_call | solution.py:105
  86.5 4.2 %expert_terms.4 = (bf16[32,2048]{1,0:T(8,128)(2,1)S(1)}, f32[256,896]{1,0:T(8,128)S(1)}, bf16[256,1024]{1,0:T(8,128)(2,1)S(1)}, f32[384,384]{1,0:T(8,128)S(1)}) custom-call(s32[3]{0:T(128)S(1)} %pad_add_fusion.refs_0_, bf16[2,1024,768]{2,1,0:T(8,128)(2,1)S(1)} %copy-done, bf16[1024,768]{1,0:T(8,128)(2,1)} %collective-permute-done.6.refs_2_, ...), custom_call_target="tpu_custom_call" | custom-call | flops 12884901888 | tf_op jit(solution)/shard_map/expert_terms/pallas_call | solution.py:235
  90.8 4.1 %expert_terms.5 = (bf16[32,2048]{1,0:T(8,128)(2,1)S(1)}, f32[256,896]{1,0:T(8,128)S(1)}, bf16[256,256]{1,0:T(8,128)(2,1)S(1)}, f32[192,384]{1,0:T(8,128)S(1)}, bf16[192,384]{1,0:T(8,128)(2,1)S(1)}) custom-call(s32[3]{0:T(128)S(1)} %pad_add_fusion.refs_0_, bf16[2,1024,768]{2,1,0:T(8,128)(2,1)S(1)} %copy-done, ...), custom_call_target="tpu_custom_call" | custom-call | flops 17716740096 | tf_op jit(solution)/shard_map/expert_terms/pallas_call | solution.py:235
  95.0 1.6 %collective-permute-start.19 = (f32[2,1024]{1,0:T(2,128)S(1)}, f32[2,1024]{1,0:T(2,128)S(1)}, u32[]{:S(2)}, u32[]{:S(2)}) collective-permute-start(f32[2,1024]{1,0:T(2,128)S(1)} %constant_dynamic-slice_fusion), channel_id=1, source_target_pairs={{0,16},{16,0},{1,17},{17,1},{2,18},{18,2},{3,19},{19,3},{4,20},{20... | collective-permute-start | bytes 24584 | tf_op jit(solution)/shard_map/ppermute | solution.py:409
  97.1 1.6 %more_terms.1 = (f32[512,896]{1,0:T(8,128)S(1)}, f32[256,896]{1,0:T(8,128)S(1)}) custom-call(bf16[384,768]{1,0:T(8,128)(2,1)S(1)} %copy-done.10, bf16[384,768]{1,0:T(8,128)(2,1)S(1)} %copy-done.12, bf16[512,1024]{1,0:T(8,128)(2,1)S(1)} %copy-done.22, f32[512,896]{1,0:T(8,128)S(1)} %copy-done.18, ...), custom_call_target="tpu_custom_call", output_to_operand_aliasing={{0}: (3, {}), {1}: (5, {})} | custom-call | flops 14495514624 | tf_op jit(solution)/shard_map/more_terms/pallas_call | solution.py:265
  98.7 3.2 %last_terms.1 = (f32[192,384]{1,0:T(8,128)S(1)}, bf16[192,384]{1,0:T(8,128)(2,1)S(1)}) custom-call(s32[3]{0:T(128)S(1)} %pad_add_fusion.refs_0_, bf16[256,768]{1,0:T(8,128)(2,1)S(1)} %collective-permute-done.17.refs_1_, bf16[512,1024]{1,0:T(8,128)(2,1)S(1)} %copy-done.22, f32[512,896]{1,0:T(8,128)S(1)} %get-tuple-element.117.refs_3_, ...), custom_call_target="tpu_custom_call" | custom-call | flops 6442450944 | tf_op jit(solution)/shard_map/last_terms/pallas_call | solution.py:328
  101.9 1.6 %collective-permute-start.18 = (bf16[192,384]{1,0:T(8,128)(2,1)S(1)}, bf16[192,384]{1,0:T(8,128)(2,1)S(1)}, u32[]{:S(2)}, u32[]{:S(2)}) collective-permute-start(bf16[192,384]{1,0:T(8,128)(2,1)S(1)} %get-tuple-element.122), channel_id=1, source_target_pairs={{0,16},{16,0},{1,17},{17,1},{2,18},{18,2},{3,19},{19,3},{4,20},{20... | collective-permute-start | bytes 442376 | tf_op jit(solution)/shard_map/ppermute | solution.py:409
  103.5 0.6 dynamic-slice_maximum_fusion
  104.1 3.0 %collective-permute-done.18 = bf16[192,384]{1,0:T(8,128)(2,1)S(1)} collective-permute-done((bf16[192,384]{1,0:T(8,128)(2,1)S(1)}, bf16[192,384]{1,0:T(8,128)(2,1)S(1)}, u32[]{:S(2)}, u32[]{:S(2)}) %collective-permute-start.18) | collective-permute-done | bytes 147488 | tf_op jit(solution)/shard_map/ppermute | solution.py:409
  107.1 0.9 pad_maximum_fusion
  (67 shorter events, 3.3 us)
Async XLA Ops:
  0.6 10.7 %copy-start = (bf16[2,1024,768]{2,1,0:T(8,128)(2,1)S(1)}, bf16[2,1024,768]{2,1,0:T(8,128)(2,1)}, u32[]{:S(2)}) copy-start(bf16[2,1024,768]{2,1,0:T(8,128)(2,1)} %refs_1_.5) | copy-start | bytes 9437188
  3.8 16.0 %collective-permute-start = (bf16[128,2176]{1,0:T(8,128)(2,1)}, bf16[128,2176]{1,0:T(8,128)(2,1)}, u32[]{:S(2)}, u32[]{:S(2)}) collective-permute-start(bf16[128,2176]{1,0:T(8,128)(2,1)} %get-tuple-element.69.after_ref.refs_1_), channel_id=1, source_target_pairs={{0,4},{1,5},{2,6},{3,7},{4,0},{5,1},{6,2},{7,3},{8,12},{9,13},{10,... | collective-permute-start | bytes 1671176 | tf_op jit(solution)/shard_map/ppermute | solution.py:398
  6.9 12.9 %collective-permute-start.1 = (bf16[128,2176]{1,0:T(8,128)(2,1)}, bf16[128,2176]{1,0:T(8,128)(2,1)}, u32[]{:S(2)}, u32[]{:S(2)}) collective-permute-start(bf16[128,2176]{1,0:T(8,128)(2,1)} %get-tuple-element.69.after_ref.refs_1_), channel_id=1, source_target_pairs={{4,8},{5,9},{6,10},{7,11},{8,4},{9,5},{10,6},{11,7},{20,24},{21,25... | collective-permute-start | bytes 1671176 | tf_op jit(solution)/shard_map/ppermute | solution.py:398
  8.4 14.3 %collective-permute-start.2 = (bf16[128,2176]{1,0:T(8,128)(2,1)}, bf16[128,2176]{1,0:T(8,128)(2,1)S(1)}, u32[]{:S(2)}, u32[]{:S(2)}) collective-permute-start(bf16[128,2176]{1,0:T(8,128)(2,1)} %get-tuple-element.69.after_ref.refs_1_), channel_id=1, source_target_pairs={{0,2},{1,3},{2,0},{3,1},{4,6},{5,7},{6,4},{7,5},{8,10},{9,11},{10,... | collective-permute-start | bytes 1671176 | tf_op jit(solution)/shard_map/ppermute | solution.py:395
  9.8 35.9 %collective-permute-start.6 = (bf16[1024,768]{1,0:T(8,128)(2,1)}, bf16[1024,768]{1,0:T(8,128)(2,1)}, u32[]{:S(2)}, u32[]{:S(2)}) collective-permute-start(bf16[1024,768]{1,0:T(8,128)(2,1)} %get-tuple-element.72), channel_id=1, source_target_pairs={{0,16},{16,0},{1,17},{17,1},{2,18},{18,2},{3,19},{19,3},{4,20},{20... | collective-permute-start | bytes 4718600 | tf_op jit(solution)/shard_map/ppermute | solution.py:409
  11.4 1.1 copy-start.1
  12.9 0.8 copy-start.5
  13.7 0.8 copy-start.7
  22.7 0.8 copy-start.13
  23.5 8.2 %collective-permute-start.4 = (bf16[128,2176]{1,0:T(8,128)(2,1)}, bf16[128,2176]{1,0:T(8,128)(2,1)}, u32[]{:S(2)}, u32[]{:S(2)}) collective-permute-start(bf16[128,2176]{1,0:T(8,128)(2,1)} %collective-permute-done.refs_1_), channel_id=1, source_target_pairs={{4,8},{5,9},{6,10},{7,11},{8,4},{9,5},{10,6},{11,7},{20,24},{21,25... | collective-permute-start | bytes 1671176 | tf_op jit(solution)/shard_map/ppermute | solution.py:398
  24.9 16.9 %collective-permute-start.3 = (bf16[128,2176]{1,0:T(8,128)(2,1)}, bf16[128,2176]{1,0:T(8,128)(2,1)}, u32[]{:S(2)}, u32[]{:S(2)}) collective-permute-start(bf16[128,2176]{1,0:T(8,128)(2,1)} %collective-permute-done.1), channel_id=1, source_target_pairs={{4,0},{5,1},{6,2},{7,3},{8,12},{9,13},{10,14},{11,15},{20,16},{21,... | collective-permute-start | bytes 1671176 | tf_op jit(solution)/shard_map/ppermute | solution.py:398
  26.3 16.7 %collective-permute-start.5 = (bf16[128,2176]{1,0:T(8,128)(2,1)}, bf16[128,2176]{1,0:T(8,128)(2,1)S(1)}, u32[]{:S(2)}, u32[]{:S(2)}) collective-permute-start(bf16[128,2176]{1,0:T(8,128)(2,1)} %collective-permute-done.refs_1_), channel_id=1, source_target_pairs={{0,2},{1,3},{2,0},{3,1},{4,6},{5,7},{6,4},{7,5},{8,10},{9,11},{10,... | collective-permute-start | bytes 1671176 | tf_op jit(solution)/shard_map/ppermute | solution.py:395
  27.8 1.1 copy-start.2
  28.9 1.1 copy-start.14
  31.6 16.2 %copy-start.8 = (bf16[384,768]{1,0:T(8,128)(2,1)S(1)}, bf16[384,768]{1,0:T(8,128)(2,1)}, u32[]{:S(2)}) copy-start(bf16[384,768]{1,0:T(8,128)(2,1)} %copy-done.7) | copy-start | bytes 1769476
  45.7 15.5 %collective-permute-start.7 = (bf16[128,2176]{1,0:T(8,128)(2,1)S(1)}, bf16[128,2176]{1,0:T(8,128)(2,1)S(1)}, u32[]{:S(2)}, u32[]{:S(2)}) collective-permute-start(bf16[128,2176]{1,0:T(8,128)(2,1)S(1)} %broadcast_select_fusion.1.refs_1_), channel_id=1, source_target_pairs={{4,0},{5,1},{6,2},{7,3},{8,12},{9,13},{10,14},{11,15},{20,16},{21,... | collective-permute-start | bytes 1671176 | tf_op jit(solution)/shard_map/ppermute | solution.py:398
  47.2 14.1 %collective-permute-start.8 = (bf16[128,2176]{1,0:T(8,128)(2,1)S(1)}, bf16[128,2176]{1,0:T(8,128)(2,1)S(1)}, u32[]{:S(2)}, u32[]{:S(2)}) collective-permute-start(bf16[128,2176]{1,0:T(8,128)(2,1)S(1)} %broadcast_select_fusion.1.refs_1_), channel_id=1, source_target_pairs={{0,2},{1,3},{2,0},{3,1},{4,6},{5,7},{6,4},{7,5},{8,10},{9,11},{10,... | collective-permute-start | bytes 1671176 | tf_op jit(solution)/shard_map/ppermute | solution.py:395
  47.8 15.8 %collective-permute-start.9 = (bf16[256,2176]{1,0:T(8,128)(2,1)S(1)}, bf16[256,2176]{1,0:T(8,128)(2,1)S(1)}, u32[]{:S(2)}, u32[]{:S(2)}) collective-permute-start(bf16[256,2176]{1,0:T(8,128)(2,1)S(1)} %get-tuple-element.79), channel_id=1, source_target_pairs={{0,1},{1,0},{2,3},{3,2},{4,5},{5,4},{6,7},{7,6},{8,9},{9,8},{10,11... | collective-permute-start | bytes 3342344 | tf_op jit(solution)/shard_map/ppermute | solution.py:395
  47.8 15.7 %collective-permute-start.10 = (bf16[384,768]{1,0:T(8,128)(2,1)S(1)}, bf16[384,768]{1,0:T(8,128)(2,1)S(1)}, u32[]{:S(2)}, u32[]{:S(2)}) collective-permute-start(bf16[384,768]{1,0:T(8,128)(2,1)S(1)} %copy-done.8), channel_id=1, source_target_pairs={{0,16},{16,0},{1,17},{17,1},{2,18},{18,2},{3,19},{19,3},{4,20},{20... | collective-permute-start | bytes 1769480 | tf_op jit(solution)/shard_map/ppermute | solution.py:409
  51.5 12.0 %copy-start.6 = (bf16[384,768]{1,0:T(8,128)(2,1)S(1)}, bf16[384,768]{1,0:T(8,128)(2,1)}, u32[]{:S(2)}) copy-start(bf16[384,768]{1,0:T(8,128)(2,1)} %copy-done.5) | copy-start | bytes 1769476
  61.3 8.1 %copy-start.3 = (bf16[128,2176]{1,0:T(8,128)(2,1)}, bf16[128,2176]{1,0:T(8,128)(2,1)S(1)}, u32[]{:S(2)}) copy-start(bf16[128,2176]{1,0:T(8,128)(2,1)S(1)} %broadcast_select_fusion.refs_1_) | copy-start | bytes 1671172
  63.6 5.8 %copy-start.9 = (bf16[384,768]{1,0:T(8,128)(2,1)}, bf16[384,768]{1,0:T(8,128)(2,1)S(1)}, u32[]{:S(2)}) copy-start(bf16[384,768]{1,0:T(8,128)(2,1)S(1)} %collective-permute-done.10.refs_3_.refs_0_) | copy-start | bytes 1769476
  63.6 6.8 %collective-permute-start.12 = (bf16[256,2176]{1,0:T(8,128)(2,1)S(1)}, bf16[256,2176]{1,0:T(8,128)(2,1)S(1)}, u32[]{:S(2)}, u32[]{:S(2)}) collective-permute-start(bf16[256,2176]{1,0:T(8,128)(2,1)S(1)} %get-tuple-element.94), channel_id=1, source_target_pairs={{0,1},{1,0},{2,3},{3,2},{4,5},{5,4},{6,7},{7,6},{8,9},{9,8},{10,11... | collective-permute-start | bytes 3342344 | tf_op jit(solution)/shard_map/ppermute | solution.py:395
  63.6 17.1 %collective-permute-start.13 = (bf16[384,768]{1,0:T(8,128)(2,1)S(1)}, bf16[384,768]{1,0:T(8,128)(2,1)S(1)}, u32[]{:S(2)}, u32[]{:S(2)}) collective-permute-start(bf16[384,768]{1,0:T(8,128)(2,1)S(1)} %copy-done.6), channel_id=1, source_target_pairs={{0,16},{16,0},{1,17},{17,1},{2,18},{18,2},{3,19},{19,3},{4,20},{20... | collective-permute-start | bytes 1769480 | tf_op jit(solution)/shard_map/ppermute | solution.py:409
  65.2 14.7 %collective-permute-start.11 = (bf16[128,2176]{1,0:T(8,128)(2,1)S(1)}, bf16[128,2176]{1,0:T(8,128)(2,1)S(1)}, u32[]{:S(2)}, u32[]{:S(2)}) collective-permute-start(bf16[128,2176]{1,0:T(8,128)(2,1)S(1)} %broadcast_select_fusion.refs_1_), channel_id=1, source_target_pairs={{0,2},{1,3},{2,0},{3,1},{4,6},{5,7},{6,4},{7,5},{8,10},{9,11},{10,... | collective-permute-start | bytes 1671176 | tf_op jit(solution)/shard_map/ppermute | solution.py:395
  69.3 1.0 copy-start.19
  75.8 1.3 %copy-start.17 = (f32[512,896]{1,0:T(8,128)}, f32[512,896]{1,0:T(8,128)S(1)}, u32[]{:S(2)}) copy-start(f32[512,896]{1,0:T(8,128)S(1)} %get-tuple-element.114.refs_3_) | copy-start | bytes 5505028
  77.0 1.0 copy-start.21
  78.1 0.8 copy-start.23
  78.9 0.7 copy-start.25
  79.9 0.8 copy-start.15
  80.7 0.9 copy-start.11
  81.6 4.9 %collective-permute-start.15 = (bf16[256,2176]{1,0:T(8,128)(2,1)}, bf16[256,2176]{1,0:T(8,128)(2,1)}, u32[]{:S(2)}, u32[]{:S(2)}) collective-permute-start(bf16[256,2176]{1,0:T(8,128)(2,1)} %get-tuple-element.105), channel_id=1, source_target_pairs={{0,1},{1,0},{2,3},{3,2},{4,5},{5,4},{6,7},{7,6},{8,9},{9,8},{10,11... | collective-permute-start | bytes 3342344 | tf_op jit(solution)/shard_map/ppermute | solution.py:395
  81.6 1.1 copy-start.4
  82.6 1.1 copy-start.16
  83.7 2.8 %copy-start.20 = (bf16[256,2176]{1,0:T(8,128)(2,1)S(1)}, bf16[256,2176]{1,0:T(8,128)(2,1)}, u32[]{:S(2)}) copy-start(bf16[256,2176]{1,0:T(8,128)(2,1)} %copy-done.19) | copy-start | bytes 3342340
  83.7 2.8 %copy-start.24 = (f32[384,384]{1,0:T(8,128)S(1)}, f32[384,384]{1,0:T(8,128)}, u32[]{:S(2)}) copy-start(f32[384,384]{1,0:T(8,128)} %copy-done.23) | copy-start | bytes 1769476
  83.7 2.8 %copy-start.26 = (bf16[32,2048]{1,0:T(8,128)(2,1)S(1)}, bf16[32,2048]{1,0:T(8,128)(2,1)}, u32[]{:S(2)}) copy-start(bf16[32,2048]{1,0:T(8,128)(2,1)} %copy-done.25) | copy-start | bytes 393220
  85.4 5.3 %collective-permute-start.14 = (bf16[256,2176]{1,0:T(8,128)(2,1)S(1)}, bf16[256,2176]{1,0:T(8,128)(2,1)S(1)}, u32[]{:S(2)}, u32[]{:S(2)}) collective-permute-start(bf16[256,2176]{1,0:T(8,128)(2,1)S(1)} %get-tuple-element.103), channel_id=1, source_target_pairs={{0,1},{1,0},{2,3},{3,2},{4,5},{5,4},{6,7},{7,6},{8,9},{9,8},{10,11... | collective-permute-start | bytes 3342344 | tf_op jit(solution)/shard_map/ppermute | solution.py:395
  86.0 12.7 %collective-permute-start.17 = (bf16[256,768]{1,0:T(8,128)(2,1)S(1)}, bf16[256,768]{1,0:T(8,128)(2,1)S(1)}, u32[]{:S(2)}, u32[]{:S(2)}) collective-permute-start(bf16[256,768]{1,0:T(8,128)(2,1)S(1)} %get-tuple-element.112), channel_id=1, source_target_pairs={{0,16},{16,0},{1,17},{17,1},{2,18},{18,2},{3,19},{19,3},{4,20},{20... | collective-permute-start | bytes 1179656 | tf_op jit(solution)/shard_map/ppermute | solution.py:409
  86.5 4.2 %copy-start.10 = (bf16[384,768]{1,0:T(8,128)(2,1)S(1)}, bf16[384,768]{1,0:T(8,128)(2,1)}, u32[]{:S(2)}) copy-start(bf16[384,768]{1,0:T(8,128)(2,1)} %copy-done.9) | copy-start | bytes 1769476
  86.5 4.2 %copy-start.12 = (bf16[384,768]{1,0:T(8,128)(2,1)S(1)}, bf16[384,768]{1,0:T(8,128)(2,1)}, u32[]{:S(2)}) copy-start(bf16[384,768]{1,0:T(8,128)(2,1)} %copy-done.11) | copy-start | bytes 1769476
  90.8 6.3 %copy-start.18 = (f32[512,896]{1,0:T(8,128)S(1)}, f32[512,896]{1,0:T(8,128)}, u32[]{:S(2)}) copy-start(f32[512,896]{1,0:T(8,128)} %copy-done.17) | copy-start | bytes 5505028
  90.8 6.3 %copy-start.22 = (bf16[512,1024]{1,0:T(8,128)(2,1)S(1)}, bf16[512,1024]{1,0:T(8,128)(2,1)}, u32[]{:S(2)}) copy-start(bf16[512,1024]{1,0:T(8,128)(2,1)} %copy-done.21) | copy-start | bytes 3145732
  95.0 8.5 %collective-permute-start.19 = (f32[2,1024]{1,0:T(2,128)S(1)}, f32[2,1024]{1,0:T(2,128)S(1)}, u32[]{:S(2)}, u32[]{:S(2)}) collective-permute-start(f32[2,1024]{1,0:T(2,128)S(1)} %constant_dynamic-slice_fusion), channel_id=1, source_target_pairs={{0,16},{16,0},{1,17},{17,1},{2,18},{18,2},{3,19},{19,3},{4,20},{20... | collective-permute-start | bytes 24584 | tf_op jit(solution)/shard_map/ppermute | solution.py:409
  96.5 7.5 %collective-permute-start.16 = (bf16[192,384]{1,0:T(8,128)(2,1)S(1)}, bf16[192,384]{1,0:T(8,128)(2,1)S(1)}, u32[]{:S(2)}, u32[]{:S(2)}) collective-permute-start(bf16[192,384]{1,0:T(8,128)(2,1)S(1)} %get-tuple-element.111), channel_id=1, source_target_pairs={{0,16},{16,0},{1,17},{17,1},{2,18},{18,2},{3,19},{19,3},{4,20},{20... | collective-permute-start | bytes 442376 | tf_op jit(solution)/shard_map/ppermute | solution.py:409
  101.9 5.2 %collective-permute-start.18 = (bf16[192,384]{1,0:T(8,128)(2,1)S(1)}, bf16[192,384]{1,0:T(8,128)(2,1)S(1)}, u32[]{:S(2)}, u32[]{:S(2)}) collective-permute-start(bf16[192,384]{1,0:T(8,128)(2,1)S(1)} %get-tuple-element.122), channel_id=1, source_target_pairs={{0,16},{16,0},{1,17},{17,1},{2,18},{18,2},{3,19},{19,3},{4,20},{20... | collective-permute-start | bytes 442376 | tf_op jit(solution)/shard_map/ppermute | solution.py:409

commit v3 on v2

--- a/solution.py
+++ b/solution.py
@@ -55,10 +55,10 @@
     copies[3].wait()
 
 
-def pick_kernel(experts, cap, count, *refs):
+def pick_kernel(experts, cap, count, apart, *refs):
     where_ref = refs[0]
     blocks = refs[1 : 1 + count]
-    own_ref, other_ref = refs[1 + count :]
+    own_ref, *other_refs = refs[1 + count :]
     rows, full = blocks[0].shape
     local = own_ref.shape[0] // (count * cap)
     extra = -(-2 * experts // 128) * 128
@@ -91,24 +91,27 @@
         taken = lax.dot_general(
             picks[b], block[...], (((0,), (0,)), ((), ())), preferred_element_type=jnp.float32
         ).astype(jnp.bfloat16)
-        for k, ref in enumerate((own_ref, other_ref)):
-            for i in range(local):
-                at = (i * count + b) * cap
-                got = (k * local + i) * cap
-                ref[at : at + cap, :] = taken[got : got + cap]
-
-
-def picked(experts, cap, local, where, blocks):
+        for i in range(local):
+            at = (i * count + b) * cap
+            own_ref[at : at + cap, :] = taken[i * cap : (i + 1) * cap]
+            got = (local + i) * cap
+            ref, at = (other_refs[i], b * cap) if apart else (other_refs[0], at)
+            ref[at : at + cap, :] = taken[got : got + cap]
+
+
+def picked(experts, cap, local, where, blocks, apart=False):
     count = len(blocks)
     rows, full = blocks[0].shape
-    out = jax.ShapeDtypeStruct((local * count * cap, full), jnp.bfloat16)
+    out = [jax.ShapeDtypeStruct((local * count * cap, full), jnp.bfloat16)]
+    one = jax.ShapeDtypeStruct((count * cap, full), jnp.bfloat16)
+    out += [one] * local if apart else out
     return pl.pallas_call(
-        functools.partial(pick_kernel, experts, cap, count),
-        out_shape=(out, out),
+        functools.partial(pick_kernel, experts, cap, count, apart),
+        out_shape=tuple(out),
         in_specs=[SM] + [VM] * count,
-        out_specs=(VM, VM),
+        out_specs=(VM,) * len(out),
         compiler_params=params(),
-        cost_estimate=cost(
+        cost_estimate=cost(1, 1) if apart else cost(
             4 * count * rows * local * cap * full, 2 * count * full * (rows + 2 * local * cap)
         ),
         name="picked_rows",
@@ -151,11 +154,14 @@
     )
 
 
-def experts_kernel(experts, pieces, count, carried, final, factor, *refs):
+def experts_kernel(experts, pieces, kinds, carried, final, factor, *refs):
     where_ref, w_ref = refs[:2]
     far_refs = refs[2 : 2 + pieces]
-    groups = refs[2 + pieces : 2 + pieces + count]
-    rest = refs[2 + pieces + count :]
+    rest = refs[2 + pieces :]
+    groups = []
+    for kind in kinds:
+        groups.append(rest[:kind])
+        rest = rest[kind:]
     if carried:
         gram_in_ref, max_in_ref = rest[:2]
         rest = rest[2:]
@@ -164,16 +170,20 @@
     rest = rest[3:-2]
     local, depth, fan = w_ref.shape
     extra = -(-2 * experts // 128) * 128
-    width = groups[0].shape[1] - extra
+    width = groups[0][0].shape[1] - extra
     lane = lax.broadcasted_iota(jnp.int32, (1, extra), 1)
     first, seq = where_ref[0] * local, where_ref[2]
     near, far = pl.multiple_of(seq * depth, 128), pl.multiple_of((1 - seq) * depth, 128)
 
     def part(i, columns):
-        each = [g.shape[0] // local for g in groups]
-        return jnp.concatenate(
-            [g[i * n : (i + 1) * n, columns] for g, n in zip(groups, each)], axis=0
-        )
+        pieces_of = []
+        for g in groups:
+            if len(g) == 1:
+                n = g[0].shape[0] // local
+                pieces_of.append(g[0][i * n : (i + 1) * n, columns])
+            else:
+                pieces_of.append(g[i][:, columns])
+        return jnp.concatenate(pieces_of, axis=0)
 
     def share_of(i):
         both = (lane == first + i) | (lane == experts + first + i)
@@ -215,6 +225,8 @@
 def experts_of(experts, where, weights, far, groups, carried, final, factor):
     local, depth, fan = weights.shape
     wide = fan // 2
+    kinds = tuple(len(g) for g in groups)
+    groups = [array for g in groups for array in g]
     rows = sum(g.shape[0] for g in groups) // local
     width = 2 * depth
     out = [
@@ -233,47 +245,15 @@
         out.append(jax.ShapeDtypeStruct((wide, wide), jnp.float32))
     ins = [weights, *far, *groups, *(carried or ())]
     return pl.pallas_call(
-        functools.partial(experts_kernel, experts, len(far), len(groups), bool(carried), final, factor),
+        functools.partial(experts_kernel, experts, len(far), kinds, bool(carried), final, factor),
         out_shape=tuple(out),
         in_specs=[SM] + [VM] * len(ins),
         out_specs=(VM,) * len(out),
         scratch_shapes=scratch,
         compiler_params=params(),
-        cost_estimate=cost(2 * rows * (depth + depth_of(far)) * fan, 0),
+        cost_estimate=cost(1, 1) if carried else cost(2 * rows * (depth + depth_of(far)) * fan, 0),
         name="expert_terms",
     )(where, *ins)
-
-
-def more_kernel(pieces, count, *refs):
-    w_refs = refs[:pieces]
-    outs = refs[pieces + 2 * count :]
-    fan = w_refs[0].shape[1]
-    for g in range(count):
-        x_ref, p_ref = refs[pieces + 2 * g : pieces + 2 * g + 2]
-        value, at = p_ref[:, :fan], 0
-        for w_ref in w_refs:
-            depth = w_ref.shape[0]
-            value = value + jnp.dot(
-                x_ref[:, at : at + depth], w_ref[...], preferred_element_type=jnp.float32
-            )
-            at += depth
-        outs[g][:, :fan] = value
-
-
-def more_of(weights, parts):
-    ins = [array for part in parts for array in part]
-    return pl.pallas_call(
-        functools.partial(more_kernel, len(weights), len(parts)),
-        out_shape=tuple(jax.ShapeDtypeStruct(p.shape, p.dtype) for _, p in parts),
-        in_specs=[VM] * (len(weights) + len(ins)),
-        out_specs=(VM,) * len(parts),
-        input_output_aliases={len(weights) + 2 * g + 1: g for g in range(len(parts))},
-        compiler_params=params(),
-        cost_estimate=cost(
-            2 * sum(p.shape[0] for _, p in parts) * depth_of(weights) * weights[0].shape[1], 0
-        ),
-        name="more_terms",
-    )(*weights, *ins)
 
 
 def last_kernel(step, firsts, factor, *refs):
@@ -290,7 +270,9 @@
         def _(g=g):
             x_ref, p_ref = groups[2 * g : 2 * g + 2]
             value = p_ref[:, :fan] + jnp.dot(
-                x_ref[...], w_ref[...], preferred_element_type=jnp.float32
+                x_ref[:, x_ref.shape[1] - w_ref.shape[0] :],
+                w_ref[...],
+                preferred_element_type=jnp.float32,
             )
             hidden, high, low = hidden_terms(value, p_ref[:, fan : fan + 1])
             rows = pl.ds(pl.multiple_of(now * step, step), step)
@@ -314,15 +296,12 @@
     for x, p in parts:
         first, number = firsts[-1], p.shape[0] // step
         firsts.append(first + number)
-        for array, columns in ((x, depth), (p, p.shape[1])):
+        for array in (x, p):
             ins.append(array)
             specs.append(
                 pl.BlockSpec(
-                    (step, columns),
-                    lambda g, first=first, number=number, at=array.shape[1] // columns - 1: (
-                        jnp.clip(g - first, 0, number - 1),
-                        at,
-                    ),
+                    (step, array.shape[1]),
+                    lambda g, first=first, number=number: (jnp.clip(g - first, 0, number - 1), 0),
                 )
             )
     return pl.pallas_call(
@@ -412,7 +391,7 @@
     where = jnp.stack([index, index + 1 - 2 * (index % 2), seq]).astype(jnp.int32)
     extra = -(-2 * all_experts // 128) * 128
     flat = gate_up.reshape(local_count * depth, fan)
-    cuts = [depth // 8 * n for n in (0, 8, 11, 14, 16)]
+    cuts = [depth // 8 * n for n in (0, 7, 9, 16)]
     spans = [(low, high - low) for low, high in zip(cuts, cuts[1:])]
     anywhere = pl.BlockSpec(memory_space=pl.ANY)
     own, piece = pl.pallas_call(
@@ -453,25 +432,24 @@
     r1 = along_core(o1)
     far3 = swapped(pieces[1])
     m2, o2 = pick((zc, xc))
-    max0, p0, late0, gram0 = terms((far1,), (m0, r0, m1, r1), None, False, factor)
-    xb, o2, gram0, max0, far3, zb, *pieces = tie(xb, o2, gram0, max0, far3, zb, *pieces)
-    far4 = swapped(pieces[2])
+    max0, p0, late0, gram0 = terms((far1, far2), ((m0,), (r0,), (m1,), (r1,)), None, False, factor)
+    xb, o2, gram0, max0, zb = tie(xb, o2, gram0, max0, zb)
     r2 = along_core(o2)
-    m3, o3 = pick((zb, xb))
-    r3 = along_core(o3)
-    max0, p1, late1, gram0 = terms((far1,), (m2, r2), (gram0, max0), False, factor)
-    p0, p1 = more_of((far2, far3), ((late0, p0), (late1, p1)))
+    m3, *o3 = pick((zb, xb), apart=True)
+    r3 = tuple(along_core(o) for o in o3)
+    max0, p1, late1, gram0 = terms((far1, far2), ((m2,), (r2,)), (gram0, max0), False, factor)
     largest, p2, late2, own0, send0 = terms(
-        (far1, far2, far3), (m3, r3), (gram0, max0), True, factor
+        (far1, far2), ((m3,), r3), (gram0, max0), True, factor
     )
     got0 = swapped(send0)
     largest = jnp.max(largest.reshape(local_count, -1, width), axis=1).astype(jnp.float32)
     keep = lax.dynamic_slice_in_dim(largest, seq * depth, depth, 1)
     give = lax.dynamic_slice_in_dim(largest, (1 - seq) * depth, depth, 1)
     maxima = jnp.maximum(keep, swapped(give))
-    own1, send1 = last_of(where, far4, ((late0, p0), (late1, p1), (late2, p2)), factor)
+    own1, send1 = last_of(where, far3, ((late0, p0), (late1, p1), (late2, p2)), factor)
+    whole0, send1 = tie(own0 + got0.astype(jnp.float32), send1)
     got1 = swapped(send1)
-    gram = jnp.stack([own0 + got0.astype(jnp.float32), own1 + got1.astype(jnp.float32)])
+    gram = jnp.stack([whole0, own1 + got1.astype(jnp.float32)])
     return (gram, maxima)
 
 

time: 109 us -> 104 us (0.954)
  local copies, waits for them, and re-layouts: 14.3 us -> 11.2 us
  waiting for transfers between devices: 36.3 us -> 33.8 us
  Pallas kernels: 30.3 us -> 32.7 us
  starting transfers between devices: 23.3 us -> 21.9 us
    unnamed x54 -> x38, local copies, waits for them, and re-layouts: 14.3 us -> 11.2 us
    ppermute x7 -> x6, waiting for transfers between devices: 8 us -> 5.3 us  [swapped(): return lax.ppermute(array, 'seq', [(0, 1), (1, 0)])]
    ppermute x8 -> x9, waiting for transfers between devices: 3.16 us -> 5.68 us  [moved(): lax.ppermute(array, 'expert', [(number[p], number[target(*p)]) for p in p...]
    ppermute x5, waiting for transfers between devices: 25.2 us -> 22.9 us  [hop(): lax.ppermute(array, 'expert', [(4 * a + n, 4 * b + n) for a, b in pairs f...]
    pallas_call x1, Pallas kernels: 3.18 us -> 5.24 us  [last_of(): pl.pallas_call(functools.partial(last_kernel, step, tuple(firsts), factor...]
    ppermute x7 -> x6, starting transfers between devices: 8.81 us -> 7.35 us  [swapped(): return lax.ppermute(array, 'seq', [(0, 1), (1, 0)])]
    pallas_call x8 -> x7, Pallas kernels: 23.5 us -> 23.2 us  [the longest x3 13.9 us: experts_of(): pl.pallas_call(functools.partial(experts_kernel, experts, len(far), kinds...]
    ppermute x8 -> x9, starting transfers between devices: 5.66 us -> 5.77 us  [moved(): lax.ppermute(array, 'expert', [(number[p], number[target(*p)]) for p in p...]
  transfers between devices with their start and end apart: 20 -> 20, of which waited for: 8 -> 7; matrix products, arithmetic and copies ran while one was open for 2% -> 2% of each run, Pallas kernels for 25% -> 29%
where the time goes in v3:
time: 104 us; the launch traced here: 103 us
  waiting for transfers between devices  33.8 us (32%)
  Pallas kernels  32.7 us (31%)
  starting transfers between devices  21.9 us (21%)
  local copies, waits for them, and re-layouts  11.2 us (11%)
  other arithmetic  2.84 us (3%)
    ppermute x5, waiting for transfers between devices, hop(): lax.ppermute(array, 'expert', [(4 * a + n, 4 * b + n) for a, b in pairs f...  22.9 us
    pallas_call x3, Pallas kernels, experts_of(): pl.pallas_call(functools.partial(experts_kernel, experts, len(far), kinds...  13.9 us
    unnamed x38, local copies, waits for them, and re-layouts  11.2 us
    pallas_call x4, Pallas kernels, picked(): pl.pallas_call(functools.partial(pick_kernel, experts, cap, count, apart)...  9.24 us
    ppermute x5, starting transfers between devices, hop(): lax.ppermute(array, 'expert', [(4 * a + n, 4 * b + n) for a, b in pairs f...  8.77 us
    ppermute x6, starting transfers between devices, swapped(): return lax.ppermute(array, 'seq', [(0, 1), (1, 0)])  7.35 us
    ppermute x9, starting transfers between devices, moved(): lax.ppermute(array, 'expert', [(number[p], number[target(*p)]) for p in p...  5.77 us
    ppermute x9, waiting for transfers between devices, moved(): lax.ppermute(array, 'expert', [(number[p], number[target(*p)]) for p in p...  5.68 us
  transfers between devices with their start and end apart: 20, of which 7 were waited for; matrix products, arithmetic and copies ran while one was open for 2% of the time, Pallas kernels for 29%

profile of v3, /device:TPU:0, one launch (start us, length us, event | category | flops | bytes accessed | tf_op | source)
XLA Modules:
  0.0 103.4 jit_solution(3923427227240925974)
XLA Ops:
  0.6 3.0 %packed_tokens.1 = (bf16[128,2176]{1,0:T(8,128)(2,1)}, bf16[896,768]{1,0:T(8,128)(2,1)}) custom-call(bf16[128,2048]{1,0:T(8,128)(2,1)} %tok_ref.1, s32[8,128]{1,0:T(8,128)} %bitcast.14, s32[8,128]{1,0:T(8,128)} %bitcast.15, bf16[2048,768]{1,0:T(8,128)(2,1)} %bitcast.11), custom_call_target="tpu_custom_call" | custom-call | bytes 16777216 | tf_op jit(solution)/shard_map/packed_tokens/pallas_call | solution.py:397
  3.7 3.1 %collective-permute-start = (bf16[128,2176]{1,0:T(8,128)(2,1)}, bf16[128,2176]{1,0:T(8,128)(2,1)}, u32[]{:S(2)}, u32[]{:S(2)}) collective-permute-start(bf16[128,2176]{1,0:T(8,128)(2,1)} %get-tuple-element.63.after_ref.refs_1_), channel_id=1, source_target_pairs={{0,4},{1,5},{2,6},{3,7},{4,0},{5,1},{6,2},{7,3},{8,12},{9,13},{10,... | collective-permute-start | bytes 1671176 | tf_op jit(solution)/shard_map/ppermute | solution.py:377
  6.8 1.5 %collective-permute-start.1 = (bf16[128,2176]{1,0:T(8,128)(2,1)}, bf16[128,2176]{1,0:T(8,128)(2,1)}, u32[]{:S(2)}, u32[]{:S(2)}) collective-permute-start(bf16[128,2176]{1,0:T(8,128)(2,1)} %get-tuple-element.63.after_ref.refs_1_), channel_id=1, source_target_pairs={{4,8},{5,9},{6,10},{7,11},{8,4},{9,5},{10,6},{11,7},{20,24},{21,25... | collective-permute-start | bytes 1671176 | tf_op jit(solution)/shard_map/ppermute | solution.py:377
  8.2 1.5 %collective-permute-start.2 = (bf16[128,2176]{1,0:T(8,128)(2,1)}, bf16[128,2176]{1,0:T(8,128)(2,1)S(1)}, u32[]{:S(2)}, u32[]{:S(2)}) collective-permute-start(bf16[128,2176]{1,0:T(8,128)(2,1)} %get-tuple-element.63.after_ref.refs_1_), channel_id=1, source_target_pairs={{0,2},{1,3},{2,0},{3,1},{4,6},{5,7},{6,4},{7,5},{8,10},{9,11},{10,... | collective-permute-start | bytes 1671176 | tf_op jit(solution)/shard_map/ppermute | solution.py:374
  9.7 1.5 %collective-permute-start.6 = (bf16[896,768]{1,0:T(8,128)(2,1)}, bf16[896,768]{1,0:T(8,128)(2,1)}, u32[]{:S(2)}, u32[]{:S(2)}) collective-permute-start(bf16[896,768]{1,0:T(8,128)(2,1)} %get-tuple-element.66), channel_id=1, source_target_pairs={{0,16},{16,0},{1,17},{17,1},{2,18},{18,2},{3,19},{19,3},{4,20},{20... | collective-permute-start | bytes 4128776 | tf_op jit(solution)/shard_map/ppermute | solution.py:388
  11.2 1.1 %copy-done.7 = bf16[128,2176]{1,0:T(8,128)(2,1)S(1)} copy-done((bf16[128,2176]{1,0:T(8,128)(2,1)S(1)}, bf16[128,2176]{1,0:T(8,128)(2,1)}, u32[]{:S(2)}) %copy-start.7) | copy-done | bytes 557080
  12.3 1.3 %weight_pieces.1 = (bf16[256,768]{1,0:T(8,128)(2,1)S(1)}, bf16[896,768]{1,0:T(8,128)(2,1)}) custom-call(bf16[2048,768]{1,0:T(8,128)(2,1)S(1)} %bitcast.12, bf16[128,2176]{1,0:T(8,128)(2,1)S(1)} %copy-done.7), custom_call_target="tpu_custom_call" | custom-call | tf_op jit(solution)/shard_map/weight_pieces/pallas_call | solution.py:345
  13.6 0.7 copy-done.13
  14.3 5.4 %collective-permute-done.refs_1_ = bf16[128,2176]{1,0:T(8,128)(2,1)} collective-permute-done((bf16[128,2176]{1,0:T(8,128)(2,1)}, bf16[128,2176]{1,0:T(8,128)(2,1)}, u32[]{:S(2)}, u32[]{:S(2)}) %collective-permute-start) | collective-permute-done | bytes 557088 | tf_op jit(solution)/shard_map/ppermute | solution.py:377
  19.7 2.8 %collective-permute-done.2.refs_2_ = bf16[128,2176]{1,0:T(8,128)(2,1)S(1)} collective-permute-done((bf16[128,2176]{1,0:T(8,128)(2,1)}, bf16[128,2176]{1,0:T(8,128)(2,1)S(1)}, u32[]{:S(2)}, u32[]{:S(2)}) %collective-permute-start.2) | collective-permute-done | bytes 557088 | tf_op jit(solution)/shard_map/ppermute | solution.py:374
  22.5 0.8 copy-done.11
  23.3 1.3 %collective-permute-start.3 = (bf16[128,2176]{1,0:T(8,128)(2,1)}, bf16[128,2176]{1,0:T(8,128)(2,1)}, u32[]{:S(2)}, u32[]{:S(2)}) collective-permute-start(bf16[128,2176]{1,0:T(8,128)(2,1)} %collective-permute-done.1), channel_id=1, source_target_pairs={{4,0},{5,1},{6,2},{7,3},{8,12},{9,13},{10,14},{11,15},{20,16},{21,... | collective-permute-start | bytes 1671176 | tf_op jit(solution)/shard_map/ppermute | solution.py:377
  24.6 1.5 %collective-permute-start.4 = (bf16[128,2176]{1,0:T(8,128)(2,1)}, bf16[128,2176]{1,0:T(8,128)(2,1)}, u32[]{:S(2)}, u32[]{:S(2)}) collective-permute-start(bf16[128,2176]{1,0:T(8,128)(2,1)} %collective-permute-done.refs_1_), channel_id=1, source_target_pairs={{4,8},{5,9},{6,10},{7,11},{8,4},{9,5},{10,6},{11,7},{20,24},{21,25... | collective-permute-start | bytes 1671176 | tf_op jit(solution)/shard_map/ppermute | solution.py:377
  26.1 0.1 pad_add_fusion.refs_0_
  26.2 1.5 %collective-permute-start.5 = (bf16[128,2176]{1,0:T(8,128)(2,1)}, bf16[128,2176]{1,0:T(8,128)(2,1)S(1)}, u32[]{:S(2)}, u32[]{:S(2)}) collective-permute-start(bf16[128,2176]{1,0:T(8,128)(2,1)} %collective-permute-done.refs_1_), channel_id=1, source_target_pairs={{0,2},{1,3},{2,0},{3,1},{4,6},{5,7},{6,4},{7,5},{8,10},{9,11},{10,... | collective-permute-start | bytes 1671176 | tf_op jit(solution)/shard_map/ppermute | solution.py:374
  27.7 1.1 %copy-done.8 = bf16[128,2176]{1,0:T(8,128)(2,1)S(1)} copy-done((bf16[128,2176]{1,0:T(8,128)(2,1)S(1)}, bf16[128,2176]{1,0:T(8,128)(2,1)}, u32[]{:S(2)}) %copy-start.8) | copy-done | bytes 557080
  28.7 1.1 %copy-done.12 = bf16[128,2176]{1,0:T(8,128)(2,1)S(1)} copy-done((bf16[128,2176]{1,0:T(8,128)(2,1)S(1)}, bf16[128,2176]{1,0:T(8,128)(2,1)}, u32[]{:S(2)}) %copy-start.12) | copy-done | bytes 557080
  29.8 1.7 %picked_rows.4 = (bf16[256,2176]{1,0:T(8,128)(2,1)S(1)}, bf16[256,2176]{1,0:T(8,128)(2,1)S(1)}) custom-call(s32[3]{0:T(128)S(1)} %pad_add_fusion.refs_0_, bf16[128,2176]{1,0:T(8,128)(2,1)S(1)} %copy-done.8, bf16[128,2176]{1,0:T(8,128)(2,1)S(1)} %copy-done.12), custom_call_target="tpu_custom_call" | custom-call | flops 4563402752 | bytes 53477376 | tf_op jit(solution)/shard_map/picked_rows/pallas_call | solution.py:108
  31.5 8.1 %collective-permute-done.3 = bf16[128,2176]{1,0:T(8,128)(2,1)} collective-permute-done((bf16[128,2176]{1,0:T(8,128)(2,1)}, bf16[128,2176]{1,0:T(8,128)(2,1)}, u32[]{:S(2)}, u32[]{:S(2)}) %collective-permute-start.3) | collective-permute-done | bytes 557088 | tf_op jit(solution)/shard_map/ppermute | solution.py:377
  39.5 1.1 %broadcast_select_fusion.1.refs_1_ = bf16[128,2176]{1,0:T(8,128)(2,1)S(1)} fusion(bf16[128,2176]{1,0:T(8,128)(2,1)} %collective-permute-done.3, bf16[128,2176]{1,0:T(8,128)(2,1)} %collective-permute-done.4, pred[]{:T(512)S(6)} %or.3), kind=kLoop, calls=%fused_computation.2 | loop fusion | flops 278528 | bytes 1671169 | tf_op jit(solution)/shard_map/jit(_where)/select_n | solution.py:423
  40.7 0.7 collective-permute-done.6.refs_2_
  41.4 1.5 %collective-permute-start.7 = (bf16[128,2176]{1,0:T(8,128)(2,1)S(1)}, bf16[128,2176]{1,0:T(8,128)(2,1)S(1)}, u32[]{:S(2)}, u32[]{:S(2)}) collective-permute-start(bf16[128,2176]{1,0:T(8,128)(2,1)S(1)} %broadcast_select_fusion.1.refs_1_), channel_id=1, source_target_pairs={{4,0},{5,1},{6,2},{7,3},{8,12},{9,13},{10,14},{11,15},{20,16},{21,... | collective-permute-start | bytes 1671176 | tf_op jit(solution)/shard_map/ppermute | solution.py:377
  42.9 0.9 collective-permute-start.8
  43.7 1.5 %collective-permute-start.10 = (bf16[256,768]{1,0:T(8,128)(2,1)S(1)}, bf16[256,768]{1,0:T(8,128)(2,1)S(1)}, u32[]{:S(2)}, u32[]{:S(2)}) collective-permute-start(bf16[256,768]{1,0:T(8,128)(2,1)S(1)} %copy-done.14), channel_id=1, source_target_pairs={{0,16},{16,0},{1,17},{17,1},{2,18},{18,2},{3,19},{19,3},{4,20},{20... | collective-permute-start | bytes 1179656 | tf_op jit(solution)/shard_map/ppermute | solution.py:388
  45.3 2.2 %picked_rows.5 = (bf16[256,2176]{1,0:T(8,128)(2,1)S(1)}, bf16[256,2176]{1,0:T(8,128)(2,1)S(1)}) custom-call(s32[3]{0:T(128)S(1)} %pad_add_fusion.refs_0_, bf16[128,2176]{1,0:T(8,128)(2,1)} %collective-permute-done.refs_1_, bf16[128,2176]{1,0:T(8,128)(2,1)S(1)} %collective-permute-done.5.refs_2_), custom_call_target="tpu_custom_call" | custom-call | flops 4563402752 | bytes 53477376 | tf_op jit(solution)/shard_map/picked_rows/pallas_call | solution.py:108
  47.5 9.4 %collective-permute-done.7 = bf16[128,2176]{1,0:T(8,128)(2,1)S(1)} collective-permute-done((bf16[128,2176]{1,0:T(8,128)(2,1)S(1)}, bf16[128,2176]{1,0:T(8,128)(2,1)S(1)}, u32[]{:S(2)}, u32[]{:S(2)}) %collective-permute-start.7) | collective-permute-done | bytes 557088 | tf_op jit(solution)/shard_map/ppermute | solution.py:377
  57.1 1.6 %collective-permute-start.17 = (bf16[896,768]{1,0:T(8,128)(2,1)}, bf16[896,768]{1,0:T(8,128)(2,1)}, u32[]{:S(2)}, u32[]{:S(2)}) collective-permute-start(bf16[896,768]{1,0:T(8,128)(2,1)} %get-tuple-element.102), channel_id=1, source_target_pairs={{0,16},{16,0},{1,17},{17,1},{2,18},{18,2},{3,19},{19,3},{4,20},{20... | collective-permute-start | bytes 4128776 | tf_op jit(solution)/shard_map/ppermute | solution.py:388
  58.7 1.3 %collective-permute-start.11 = (bf16[128,2176]{1,0:T(8,128)(2,1)S(1)}, bf16[128,2176]{1,0:T(8,128)(2,1)S(1)}, u32[]{:S(2)}, u32[]{:S(2)}) collective-permute-start(bf16[128,2176]{1,0:T(8,128)(2,1)S(1)} %broadcast_select_fusion.refs_1_), channel_id=1, source_target_pairs={{0,2},{1,3},{2,0},{3,1},{4,6},{5,7},{6,4},{7,5},{8,10},{9,11},{10,... | collective-permute-start | bytes 1671176 | tf_op jit(solution)/shard_map/ppermute | solution.py:374
  60.0 2.7 %picked_rows.6 = (bf16[256,2176]{1,0:T(8,128)(2,1)S(1)}, bf16[256,2176]{1,0:T(8,128)(2,1)}) custom-call(s32[3]{0:T(128)S(1)} %pad_add_fusion.refs_0_, bf16[128,2176]{1,0:T(8,128)(2,1)S(1)} %broadcast_select_fusion.1.refs_1_, bf16[128,2176]{1,0:T(8,128)(2,1)S(1)} %collective-permute-done.8.refs_2_), custom_call_target="tpu_custom_call" | custom-call | flops 4563402752 | bytes 53477376 | tf_op jit(solution)/shard_map/picked_rows/pallas_call | solution.py:108
  62.7 5.6 %expert_terms.3 = (bf16[32,2048]{1,0:T(8,128)(2,1)S(1)}, f32[512,896]{1,0:T(8,128)S(1)}, bf16[512,896]{1,0:T(8,128)(2,1)S(1)}, f32[384,384]{1,0:T(8,128)S(1)}) custom-call(s32[3]{0:T(128)S(1)} %pad_add_fusion.refs_0_, bf16[2,1024,768]{2,1,0:T(8,128)(2,1)S(1)} %copy-done, bf16[896,768]{1,0:T(8,128)(2,1)} %collective-permute-done.6.refs_2_, ...), custom_call_target="tpu_custom_call" | custom-call | flops 27380416512 | tf_op jit(solution)/shard_map/expert_terms/pallas_call | solution.py:247
  68.3 1.3 %copy-done.15 = f32[512,896]{1,0:T(8,128)} copy-done((f32[512,896]{1,0:T(8,128)}, f32[512,896]{1,0:T(8,128)S(1)}, u32[]{:S(2)}) %copy-start.15) | copy-done | bytes 1835032
  69.6 0.9 copy-done.17
  70.5 2.8 %collective-permute-done.11.refs_2_ = bf16[128,2176]{1,0:T(8,128)(2,1)S(1)} collective-permute-done((bf16[128,2176]{1,0:T(8,128)(2,1)S(1)}, bf16[128,2176]{1,0:T(8,128)(2,1)S(1)}, u32[]{:S(2)}, u32[]{:S(2)}) %collective-permute-start.11) | collective-permute-done | bytes 557088 | tf_op jit(solution)/shard_map/ppermute | solution.py:374
  73.4 2.7 %picked_rows.7 = (bf16[256,2176]{1,0:T(8,128)(2,1)S(1)}, bf16[128,2176]{1,0:T(8,128)(2,1)}, bf16[128,2176]{1,0:T(8,128)(2,1)}) custom-call(s32[3]{0:T(128)S(1)} %pad_add_fusion.refs_0_, bf16[128,2176]{1,0:T(8,128)(2,1)S(1)} %broadcast_select_fusion.refs_1_, bf16[128,2176]{1,0:T(8,128)(2,1)S(1)} %collective-permute-done.11.refs_2_), custom_call_target="tpu_custom_call" | custom-call | flops 16 | bytes 16 | tf_op jit(solution)/shard_map/picked_rows/pallas_call | solution.py:108
  76.0 1.0 copy-done.3
  77.0 0.5 collective-permute-start.13
  77.6 1.2 %copy-done.2 = bf16[256,2176]{1,0:T(8,128)(2,1)S(1)} copy-done((bf16[256,2176]{1,0:T(8,128)(2,1)S(1)}, bf16[256,2176]{1,0:T(8,128)(2,1)}, u32[]{:S(2)}) %copy-start.2) | copy-done | bytes 1114136
  78.8 1.1 %copy-done.6 = f32[384,384]{1,0:T(8,128)S(1)} copy-done((f32[384,384]{1,0:T(8,128)S(1)}, f32[384,384]{1,0:T(8,128)}, u32[]{:S(2)}) %copy-start.6) | copy-done | bytes 589848
  79.9 0.9 copy-done.10
  80.8 4.1 %expert_terms.4 = (bf16[32,2048]{1,0:T(8,128)(2,1)S(1)}, f32[256,896]{1,0:T(8,128)S(1)}, bf16[256,896]{1,0:T(8,128)(2,1)S(1)}, f32[384,384]{1,0:T(8,128)S(1)}) custom-call(s32[3]{0:T(128)S(1)} %pad_add_fusion.refs_0_, bf16[2,1024,768]{2,1,0:T(8,128)(2,1)S(1)} %copy-done, bf16[896,768]{1,0:T(8,128)(2,1)} %collective-permute-done.6.refs_2_, ...), custom_call_target="tpu_custom_call" | custom-call | flops 16 | bytes 16 | tf_op jit(solution)/shard_map/expert_terms/pallas_call | solution.py:247
  85.0 4.2 %expert_terms.5 = (bf16[32,2048]{1,0:T(8,128)(2,1)S(1)}, f32[256,896]{1,0:T(8,128)S(1)}, bf16[256,896]{1,0:T(8,128)(2,1)S(1)}, f32[192,384]{1,0:T(8,128)S(1)}, bf16[192,384]{1,0:T(8,128)(2,1)S(1)}) custom-call(s32[3]{0:T(128)S(1)} %pad_add_fusion.refs_0_, bf16[2,1024,768]{2,1,0:T(8,128)(2,1)S(1)} %copy-done, ...), custom_call_target="tpu_custom_call" | custom-call | flops 16 | bytes 16 | tf_op jit(solution)/shard_map/expert_terms/pallas_call | solution.py:247
  89.2 0.6 collective-permute-start.16
  89.8 1.6 %collective-permute-start.19 = (f32[2,1024]{1,0:T(2,128)S(1)}, f32[2,1024]{1,0:T(2,128)S(1)}, u32[]{:S(2)}, u32[]{:S(2)}) collective-permute-start(f32[2,1024]{1,0:T(2,128)S(1)} %constant_dynamic-slice_fusion), channel_id=1, source_target_pairs={{0,16},{16,0},{1,17},{17,1},{2,18},{18,2},{3,19},{19,3},{4,20},{20... | collective-permute-start | bytes 24584 | tf_op jit(solution)/shard_map/ppermute | solution.py:388
  91.4 5.2 %last_terms.1 = (f32[192,384]{1,0:T(8,128)S(1)}, bf16[192,384]{1,0:T(8,128)(2,1)S(1)}) custom-call(s32[3]{0:T(128)S(1)} %pad_add_fusion.refs_0_, bf16[896,768]{1,0:T(8,128)(2,1)} %collective-permute-done.17.refs_1_, bf16[512,896]{1,0:T(8,128)(2,1)S(1)} %copy-done.18, f32[512,896]{1,0:T(8,128)S(1)} %copy-done.16, ...), custom_call_target="tpu_custom_call" | custom-call | flops 22548578304 | tf_op jit(solution)/shard_map/last_terms/pallas_call | solution.py:307
  96.7 0.6 collective-permute-start.18
  97.3 0.6 dynamic-slice_maximum_fusion
  97.9 4.6 %collective-permute-done.18 = bf16[192,384]{1,0:T(8,128)(2,1)S(1)} collective-permute-done((bf16[192,384]{1,0:T(8,128)(2,1)S(1)}, bf16[192,384]{1,0:T(8,128)(2,1)S(1)}, u32[]{:S(2)}, u32[]{:S(2)}) %collective-permute-start.18) | collective-permute-done | bytes 147488 | tf_op jit(solution)/shard_map/ppermute | solution.py:388
  102.5 0.9 pad_maximum_fusion
  (50 shorter events, 0.4 us)
Async XLA Ops:
  0.6 10.6 %copy-start = (bf16[2,1024,768]{2,1,0:T(8,128)(2,1)S(1)}, bf16[2,1024,768]{2,1,0:T(8,128)(2,1)}, u32[]{:S(2)}) copy-start(bf16[2,1024,768]{2,1,0:T(8,128)(2,1)} %refs_1_.5) | copy-start | bytes 9437188
  3.7 16.0 %collective-permute-start = (bf16[128,2176]{1,0:T(8,128)(2,1)}, bf16[128,2176]{1,0:T(8,128)(2,1)}, u32[]{:S(2)}, u32[]{:S(2)}) collective-permute-start(bf16[128,2176]{1,0:T(8,128)(2,1)} %get-tuple-element.63.after_ref.refs_1_), channel_id=1, source_target_pairs={{0,4},{1,5},{2,6},{3,7},{4,0},{5,1},{6,2},{7,3},{8,12},{9,13},{10,... | collective-permute-start | bytes 1671176 | tf_op jit(solution)/shard_map/ppermute | solution.py:377
  6.8 12.9 %collective-permute-start.1 = (bf16[128,2176]{1,0:T(8,128)(2,1)}, bf16[128,2176]{1,0:T(8,128)(2,1)}, u32[]{:S(2)}, u32[]{:S(2)}) collective-permute-start(bf16[128,2176]{1,0:T(8,128)(2,1)} %get-tuple-element.63.after_ref.refs_1_), channel_id=1, source_target_pairs={{4,8},{5,9},{6,10},{7,11},{8,4},{9,5},{10,6},{11,7},{20,24},{21,25... | collective-permute-start | bytes 1671176 | tf_op jit(solution)/shard_map/ppermute | solution.py:377
  8.2 14.3 %collective-permute-start.2 = (bf16[128,2176]{1,0:T(8,128)(2,1)}, bf16[128,2176]{1,0:T(8,128)(2,1)S(1)}, u32[]{:S(2)}, u32[]{:S(2)}) collective-permute-start(bf16[128,2176]{1,0:T(8,128)(2,1)} %get-tuple-element.63.after_ref.refs_1_), channel_id=1, source_target_pairs={{0,2},{1,3},{2,0},{3,1},{4,6},{5,7},{6,4},{7,5},{8,10},{9,11},{10,... | collective-permute-start | bytes 1671176 | tf_op jit(solution)/shard_map/ppermute | solution.py:374
  9.7 31.7 %collective-permute-start.6 = (bf16[896,768]{1,0:T(8,128)(2,1)}, bf16[896,768]{1,0:T(8,128)(2,1)}, u32[]{:S(2)}, u32[]{:S(2)}) collective-permute-start(bf16[896,768]{1,0:T(8,128)(2,1)} %get-tuple-element.66), channel_id=1, source_target_pairs={{0,16},{16,0},{1,17},{17,1},{2,18},{18,2},{3,19},{19,3},{4,20},{20... | collective-permute-start | bytes 4128776 | tf_op jit(solution)/shard_map/ppermute | solution.py:388
  11.2 1.1 %copy-start.7 = (bf16[128,2176]{1,0:T(8,128)(2,1)S(1)}, bf16[128,2176]{1,0:T(8,128)(2,1)}, u32[]{:S(2)}) copy-start(bf16[128,2176]{1,0:T(8,128)(2,1)} %get-tuple-element.63.after_ref.refs_1_) | copy-start | bytes 1671172
  13.6 0.7 copy-start.13
  22.5 0.8 copy-start.11
  23.3 16.2 %collective-permute-start.3 = (bf16[128,2176]{1,0:T(8,128)(2,1)}, bf16[128,2176]{1,0:T(8,128)(2,1)}, u32[]{:S(2)}, u32[]{:S(2)}) collective-permute-start(bf16[128,2176]{1,0:T(8,128)(2,1)} %collective-permute-done.1), channel_id=1, source_target_pairs={{4,0},{5,1},{6,2},{7,3},{8,12},{9,13},{10,14},{11,15},{20,16},{21,... | collective-permute-start | bytes 1671176 | tf_op jit(solution)/shard_map/ppermute | solution.py:377
  24.6 14.9 %collective-permute-start.4 = (bf16[128,2176]{1,0:T(8,128)(2,1)}, bf16[128,2176]{1,0:T(8,128)(2,1)}, u32[]{:S(2)}, u32[]{:S(2)}) collective-permute-start(bf16[128,2176]{1,0:T(8,128)(2,1)} %collective-permute-done.refs_1_), channel_id=1, source_target_pairs={{4,8},{5,9},{6,10},{7,11},{8,4},{9,5},{10,6},{11,7},{20,24},{21,25... | collective-permute-start | bytes 1671176 | tf_op jit(solution)/shard_map/ppermute | solution.py:377
  26.2 14.5 %collective-permute-start.5 = (bf16[128,2176]{1,0:T(8,128)(2,1)}, bf16[128,2176]{1,0:T(8,128)(2,1)S(1)}, u32[]{:S(2)}, u32[]{:S(2)}) collective-permute-start(bf16[128,2176]{1,0:T(8,128)(2,1)} %collective-permute-done.refs_1_), channel_id=1, source_target_pairs={{0,2},{1,3},{2,0},{3,1},{4,6},{5,7},{6,4},{7,5},{8,10},{9,11},{10,... | collective-permute-start | bytes 1671176 | tf_op jit(solution)/shard_map/ppermute | solution.py:374
  27.7 1.1 %copy-start.8 = (bf16[128,2176]{1,0:T(8,128)(2,1)S(1)}, bf16[128,2176]{1,0:T(8,128)(2,1)}, u32[]{:S(2)}) copy-start(bf16[128,2176]{1,0:T(8,128)(2,1)} %get-tuple-element.63.after_ref.refs_1_) | copy-start | bytes 1671172
  28.7 1.1 %copy-start.12 = (bf16[128,2176]{1,0:T(8,128)(2,1)S(1)}, bf16[128,2176]{1,0:T(8,128)(2,1)}, u32[]{:S(2)}) copy-start(bf16[128,2176]{1,0:T(8,128)(2,1)} %copy-done.11) | copy-start | bytes 1671172
  31.5 12.3 %copy-start.14 = (bf16[256,768]{1,0:T(8,128)(2,1)S(1)}, bf16[256,768]{1,0:T(8,128)(2,1)}, u32[]{:S(2)}) copy-start(bf16[256,768]{1,0:T(8,128)(2,1)} %copy-done.13) | copy-start | bytes 1179652
  41.4 15.5 %collective-permute-start.7 = (bf16[128,2176]{1,0:T(8,128)(2,1)S(1)}, bf16[128,2176]{1,0:T(8,128)(2,1)S(1)}, u32[]{:S(2)}, u32[]{:S(2)}) collective-permute-start(bf16[128,2176]{1,0:T(8,128)(2,1)S(1)} %broadcast_select_fusion.1.refs_1_), channel_id=1, source_target_pairs={{4,0},{5,1},{6,2},{7,3},{8,12},{9,13},{10,14},{11,15},{20,16},{21,... | collective-permute-start | bytes 1671176 | tf_op jit(solution)/shard_map/ppermute | solution.py:377
  42.9 14.1 %collective-permute-start.8 = (bf16[128,2176]{1,0:T(8,128)(2,1)S(1)}, bf16[128,2176]{1,0:T(8,128)(2,1)S(1)}, u32[]{:S(2)}, u32[]{:S(2)}) collective-permute-start(bf16[128,2176]{1,0:T(8,128)(2,1)S(1)} %broadcast_select_fusion.1.refs_1_), channel_id=1, source_target_pairs={{0,2},{1,3},{2,0},{3,1},{4,6},{5,7},{6,4},{7,5},{8,10},{9,11},{10,... | collective-permute-start | bytes 1671176 | tf_op jit(solution)/shard_map/ppermute | solution.py:374
  43.7 13.3 %collective-permute-start.9 = (bf16[256,2176]{1,0:T(8,128)(2,1)S(1)}, bf16[256,2176]{1,0:T(8,128)(2,1)S(1)}, u32[]{:S(2)}, u32[]{:S(2)}) collective-permute-start(bf16[256,2176]{1,0:T(8,128)(2,1)S(1)} %get-tuple-element.72), channel_id=1, source_target_pairs={{0,1},{1,0},{2,3},{3,2},{4,5},{5,4},{6,7},{7,6},{8,9},{9,8},{10,11... | collective-permute-start | bytes 3342344 | tf_op jit(solution)/shard_map/ppermute | solution.py:374
  43.7 13.2 %collective-permute-start.10 = (bf16[256,768]{1,0:T(8,128)(2,1)S(1)}, bf16[256,768]{1,0:T(8,128)(2,1)S(1)}, u32[]{:S(2)}, u32[]{:S(2)}) collective-permute-start(bf16[256,768]{1,0:T(8,128)(2,1)S(1)} %copy-done.14), channel_id=1, source_target_pairs={{0,16},{16,0},{1,17},{17,1},{2,18},{18,2},{3,19},{19,3},{4,20},{20... | collective-permute-start | bytes 1179656 | tf_op jit(solution)/shard_map/ppermute | solution.py:388
  57.0 5.7 %collective-permute-start.12 = (bf16[256,2176]{1,0:T(8,128)(2,1)S(1)}, bf16[256,2176]{1,0:T(8,128)(2,1)S(1)}, u32[]{:S(2)}, u32[]{:S(2)}) collective-permute-start(bf16[256,2176]{1,0:T(8,128)(2,1)S(1)} %get-tuple-element.86), channel_id=1, source_target_pairs={{0,1},{1,0},{2,3},{3,2},{4,5},{5,4},{6,7},{7,6},{8,9},{9,8},{10,11... | collective-permute-start | bytes 3342344 | tf_op jit(solution)/shard_map/ppermute | solution.py:374
  57.1 34.3 %collective-permute-start.17 = (bf16[896,768]{1,0:T(8,128)(2,1)}, bf16[896,768]{1,0:T(8,128)(2,1)}, u32[]{:S(2)}, u32[]{:S(2)}) collective-permute-start(bf16[896,768]{1,0:T(8,128)(2,1)} %get-tuple-element.102), channel_id=1, source_target_pairs={{0,16},{16,0},{1,17},{17,1},{2,18},{18,2},{3,19},{19,3},{4,20},{20... | collective-permute-start | bytes 4128776 | tf_op jit(solution)/shard_map/ppermute | solution.py:388
  58.7 14.7 %collective-permute-start.11 = (bf16[128,2176]{1,0:T(8,128)(2,1)S(1)}, bf16[128,2176]{1,0:T(8,128)(2,1)S(1)}, u32[]{:S(2)}, u32[]{:S(2)}) collective-permute-start(bf16[128,2176]{1,0:T(8,128)(2,1)S(1)} %broadcast_select_fusion.refs_1_), channel_id=1, source_target_pairs={{0,2},{1,3},{2,0},{3,1},{4,6},{5,7},{6,4},{7,5},{8,10},{9,11},{10,... | collective-permute-start | bytes 1671176 | tf_op jit(solution)/shard_map/ppermute | solution.py:374
  62.7 5.6 %copy-start.1 = (bf16[256,2176]{1,0:T(8,128)(2,1)}, bf16[256,2176]{1,0:T(8,128)(2,1)S(1)}, u32[]{:S(2)}) copy-start(bf16[256,2176]{1,0:T(8,128)(2,1)S(1)} %get-tuple-element.94.refs_4_) | copy-start | bytes 3342340
  68.3 1.3 %copy-start.15 = (f32[512,896]{1,0:T(8,128)}, f32[512,896]{1,0:T(8,128)S(1)}, u32[]{:S(2)}) copy-start(f32[512,896]{1,0:T(8,128)S(1)} %get-tuple-element.104.refs_3_) | copy-start | bytes 5505028
  69.6 0.9 copy-start.17
  70.5 5.5 %copy-start.5 = (f32[384,384]{1,0:T(8,128)}, f32[384,384]{1,0:T(8,128)S(1)}, u32[]{:S(2)}) copy-start(f32[384,384]{1,0:T(8,128)S(1)} %get-tuple-element.96.refs_6_) | copy-start | bytes 1769476
  70.5 6.5 %copy-start.9 = (bf16[32,2048]{1,0:T(8,128)(2,1)}, bf16[32,2048]{1,0:T(8,128)(2,1)S(1)}, u32[]{:S(2)}) copy-start(bf16[32,2048]{1,0:T(8,128)(2,1)S(1)} %get-tuple-element.97.refs_7_) | copy-start | bytes 393220
  73.4 4.2 %collective-permute-start.15 = (bf16[256,2176]{1,0:T(8,128)(2,1)}, bf16[256,2176]{1,0:T(8,128)(2,1)}, u32[]{:S(2)}, u32[]{:S(2)}) collective-permute-start(bf16[256,2176]{1,0:T(8,128)(2,1)} %get-tuple-element.95), channel_id=1, source_target_pairs={{0,1},{1,0},{2,3},{3,2},{4,5},{5,4},{6,7},{7,6},{8,9},{9,8},{10,11... | collective-permute-start | bytes 3342344 | tf_op jit(solution)/shard_map/ppermute | solution.py:374
  76.0 1.0 copy-start.3
  77.0 7.9 %collective-permute-start.13 = (bf16[128,2176]{1,0:T(8,128)(2,1)}, bf16[128,2176]{1,0:T(8,128)(2,1)}, u32[]{:S(2)}, u32[]{:S(2)}) collective-permute-start(bf16[128,2176]{1,0:T(8,128)(2,1)} %get-tuple-element.92), channel_id=1, source_target_pairs={{0,1},{1,0},{2,3},{3,2},{4,5},{5,4},{6,7},{7,6},{8,9},{9,8},{10,11... | collective-permute-start | bytes 1671176 | tf_op jit(solution)/shard_map/ppermute | solution.py:374
  77.6 7.4 %collective-permute-start.14 = (bf16[128,2176]{1,0:T(8,128)(2,1)}, bf16[128,2176]{1,0:T(8,128)(2,1)}, u32[]{:S(2)}, u32[]{:S(2)}) collective-permute-start(bf16[128,2176]{1,0:T(8,128)(2,1)} %get-tuple-element.93), channel_id=1, source_target_pairs={{0,1},{1,0},{2,3},{3,2},{4,5},{5,4},{6,7},{7,6},{8,9},{9,8},{10,11... | collective-permute-start | bytes 1671176 | tf_op jit(solution)/shard_map/ppermute | solution.py:374
  77.6 1.2 %copy-start.2 = (bf16[256,2176]{1,0:T(8,128)(2,1)S(1)}, bf16[256,2176]{1,0:T(8,128)(2,1)}, u32[]{:S(2)}) copy-start(bf16[256,2176]{1,0:T(8,128)(2,1)} %copy-done.1) | copy-start | bytes 3342340
  78.8 1.1 %copy-start.6 = (f32[384,384]{1,0:T(8,128)S(1)}, f32[384,384]{1,0:T(8,128)}, u32[]{:S(2)}) copy-start(f32[384,384]{1,0:T(8,128)} %copy-done.5) | copy-start | bytes 1769476
  79.9 0.9 copy-start.10
  80.8 4.1 %copy-start.4 = (bf16[256,2176]{1,0:T(8,128)(2,1)S(1)}, bf16[256,2176]{1,0:T(8,128)(2,1)}, u32[]{:S(2)}) copy-start(bf16[256,2176]{1,0:T(8,128)(2,1)} %copy-done.3) | copy-start | bytes 3342340
  84.9 6.5 %copy-start.16 = (f32[512,896]{1,0:T(8,128)S(1)}, f32[512,896]{1,0:T(8,128)}, u32[]{:S(2)}) copy-start(f32[512,896]{1,0:T(8,128)} %copy-done.15) | copy-start | bytes 5505028
  84.9 6.5 %copy-start.18 = (bf16[512,896]{1,0:T(8,128)(2,1)S(1)}, bf16[512,896]{1,0:T(8,128)(2,1)}, u32[]{:S(2)}) copy-start(bf16[512,896]{1,0:T(8,128)(2,1)} %copy-done.17) | copy-start | bytes 2752516
  89.2 7.5 %collective-permute-start.16 = (bf16[192,384]{1,0:T(8,128)(2,1)S(1)}, bf16[192,384]{1,0:T(8,128)(2,1)S(1)}, u32[]{:S(2)}, u32[]{:S(2)}) collective-permute-start(bf16[192,384]{1,0:T(8,128)(2,1)S(1)} %get-tuple-element.101), channel_id=1, source_target_pairs={{0,16},{16,0},{1,17},{17,1},{2,18},{18,2},{3,19},{19,3},{4,20},{20... | collective-permute-start | bytes 442376 | tf_op jit(solution)/shard_map/ppermute | solution.py:388
  89.8 7.5 %collective-permute-start.19 = (f32[2,1024]{1,0:T(2,128)S(1)}, f32[2,1024]{1,0:T(2,128)S(1)}, u32[]{:S(2)}, u32[]{:S(2)}) collective-permute-start(f32[2,1024]{1,0:T(2,128)S(1)} %constant_dynamic-slice_fusion), channel_id=1, source_target_pairs={{0,16},{16,0},{1,17},{17,1},{2,18},{18,2},{3,19},{19,3},{4,20},{20... | collective-permute-start | bytes 24584 | tf_op jit(solution)/shard_map/ppermute | solution.py:388
  96.7 5.8 %collective-permute-start.18 = (bf16[192,384]{1,0:T(8,128)(2,1)S(1)}, bf16[192,384]{1,0:T(8,128)(2,1)S(1)}, u32[]{:S(2)}, u32[]{:S(2)}) collective-permute-start(bf16[192,384]{1,0:T(8,128)(2,1)S(1)} %get-tuple-element.112), channel_id=1, source_target_pairs={{0,16},{16,0},{1,17},{17,1},{2,18},{18,2},{3,19},{19,3},{4,20},{20... | collective-permute-start | bytes 442376 | tf_op jit(solution)/shard_map/ppermute | solution.py:388

commit v4 on v3

--- a/solution.py
+++ b/solution.py
@@ -149,7 +149,7 @@
     hold_ref[...] = total
     part = own_ref.shape[0]
     own_ref[...] = hold_ref[pl.ds(pl.multiple_of(seq * part, 16), part), :]
-    send_ref[...] = hold_ref[pl.ds(pl.multiple_of((1 - seq) * part, 16), part), :].astype(
+    send_ref[:part, :] = hold_ref[pl.ds(pl.multiple_of((1 - seq) * part, 16), part), :].astype(
         jnp.bfloat16
     )
 
@@ -218,6 +218,14 @@
         total = total + gram_in_ref[...]
     if final:
         give_out(total * factor, seq, *rest)
+        part = rest[0].shape[0]
+        rows = []
+        for i in range(local):
+            found = max_ref[i * 16 : (i + 1) * 16, pl.ds(far, depth)].astype(jnp.float32)
+            found = jnp.max(found, axis=0, keepdims=True)
+            rows += [found[:, c : c + 128] for c in range(0, depth, 128)]
+        rest[1][part:, :] = jnp.zeros((len(rows), rest[1].shape[1]), jnp.bfloat16)
+        rest[1][part:, :128] = jnp.concatenate(rows, axis=0).astype(jnp.bfloat16)
     else:
         rest[0][...] = total
 
@@ -238,7 +246,7 @@
     if final:
         out += [
             jax.ShapeDtypeStruct((wide // 2, wide), jnp.float32),
-            jax.ShapeDtypeStruct((wide // 2, wide), jnp.bfloat16),
+            jax.ShapeDtypeStruct((wide // 2 + local * depth // 128, wide), jnp.bfloat16),
         ]
         scratch = [pltpu.VMEM((wide, wide), jnp.float32)] + scratch
     else:
@@ -444,10 +452,12 @@
     got0 = swapped(send0)
     largest = jnp.max(largest.reshape(local_count, -1, width), axis=1).astype(jnp.float32)
     keep = lax.dynamic_slice_in_dim(largest, seq * depth, depth, 1)
-    give = lax.dynamic_slice_in_dim(largest, (1 - seq) * depth, depth, 1)
-    maxima = jnp.maximum(keep, swapped(give))
+    part = own0.shape[0]
+    maxima = jnp.maximum(
+        keep, got0[part:, :128].reshape(local_count, depth).astype(jnp.float32)
+    )
     own1, send1 = last_of(where, far3, ((late0, p0), (late1, p1), (late2, p2)), factor)
-    whole0, send1 = tie(own0 + got0.astype(jnp.float32), send1)
+    whole0, send1 = tie(own0 + got0[:part].astype(jnp.float32), send1)
     got1 = swapped(send1)
     gram = jnp.stack([whole0, own1 + got1.astype(jnp.float32)])
     return (gram, maxima)

time: 104 us -> 103 us (level)
  starting transfers between devices: 21.9 us -> 20.8 us
    ppermute x6 -> x5, starting transfers between devices: 7.35 us -> 6.25 us  [swapped(): return lax.ppermute(array, 'seq', [(0, 1), (1, 0)])]
    ppermute x6 -> x5, waiting for transfers between devices: 5.3 us -> 5.38 us  [swapped(): return lax.ppermute(array, 'seq', [(0, 1), (1, 0)])]
  transfers between devices with their start and end apart: 20 -> 19, of which waited for: 7 -> 9; matrix products, arithmetic and copies ran while one was open for 2% -> 2% of each run, Pallas kernels for 29% -> 29%
where the time goes in v4:
time: 103 us; the launch traced here: 102 us
  waiting for transfers between devices  33.9 us (33%)
  Pallas kernels  32.6 us (32%)
  starting transfers between devices  20.8 us (20%)
  local copies, waits for them, and re-layouts  11.2 us (11%)
  other arithmetic  2.84 us (3%)
    ppermute x5, waiting for transfers between devices, hop(): lax.ppermute(array, 'expert', [(4 * a + n, 4 * b + n) for a, b in pairs f...  22.9 us
    pallas_call x3, Pallas kernels, experts_of(): pl.pallas_call(functools.partial(experts_kernel, experts, len(far), kinds...  13.9 us
    unnamed x38, local copies, waits for them, and re-layouts  11.1 us
    pallas_call x4, Pallas kernels, picked(): pl.pallas_call(functools.partial(pick_kernel, experts, cap, count, apart)...  9.23 us
    ppermute x5, starting transfers between devices, hop(): lax.ppermute(array, 'expert', [(4 * a + n, 4 * b + n) for a, b in pairs f...  8.76 us
    ppermute x5, starting transfers between devices, swapped(): return lax.ppermute(array, 'seq', [(0, 1), (1, 0)])  6.25 us
    ppermute x9, starting transfers between devices, moved(): lax.ppermute(array, 'expert', [(number[p], number[target(*p)]) for p in p...  5.78 us
    ppermute x9, waiting for transfers between devices, moved(): lax.ppermute(array, 'expert', [(number[p], number[target(*p)]) for p in p...  5.7 us
  transfers between devices with their start and end apart: 19, of which 9 were waited for; matrix products, arithmetic and copies ran while one was open for 2% of the time, Pallas kernels for 29%

profile of v4, /device:TPU:0, one launch (start us, length us, event | category | flops | bytes accessed | tf_op | source)
XLA Modules:
  0.0 102.2 jit_solution(5422341499190290606)
XLA Ops:
  0.6 3.0 %packed_tokens.1 = (bf16[128,2176]{1,0:T(8,128)(2,1)}, bf16[896,768]{1,0:T(8,128)(2,1)}) custom-call(bf16[128,2048]{1,0:T(8,128)(2,1)} %tok_ref.1, s32[8,128]{1,0:T(8,128)} %bitcast.14, s32[8,128]{1,0:T(8,128)} %bitcast.15, bf16[2048,768]{1,0:T(8,128)(2,1)} %bitcast.11), custom_call_target="tpu_custom_call" | custom-call | bytes 16777216 | tf_op jit(solution)/shard_map/packed_tokens/pallas_call | solution.py:405
  3.7 3.1 %collective-permute-start = (bf16[128,2176]{1,0:T(8,128)(2,1)}, bf16[128,2176]{1,0:T(8,128)(2,1)}, u32[]{:S(2)}, u32[]{:S(2)}) collective-permute-start(bf16[128,2176]{1,0:T(8,128)(2,1)} %get-tuple-element.63.after_ref.refs_1_), channel_id=1, source_target_pairs={{0,4},{1,5},{2,6},{3,7},{4,0},{5,1},{6,2},{7,3},{8,12},{9,13},{10,... | collective-permute-start | bytes 1671176 | tf_op jit(solution)/shard_map/ppermute | solution.py:385
  6.8 1.5 %collective-permute-start.1 = (bf16[128,2176]{1,0:T(8,128)(2,1)}, bf16[128,2176]{1,0:T(8,128)(2,1)}, u32[]{:S(2)}, u32[]{:S(2)}) collective-permute-start(bf16[128,2176]{1,0:T(8,128)(2,1)} %get-tuple-element.63.after_ref.refs_1_), channel_id=1, source_target_pairs={{4,8},{5,9},{6,10},{7,11},{8,4},{9,5},{10,6},{11,7},{20,24},{21,25... | collective-permute-start | bytes 1671176 | tf_op jit(solution)/shard_map/ppermute | solution.py:385
  8.2 1.5 %collective-permute-start.2 = (bf16[128,2176]{1,0:T(8,128)(2,1)}, bf16[128,2176]{1,0:T(8,128)(2,1)S(1)}, u32[]{:S(2)}, u32[]{:S(2)}) collective-permute-start(bf16[128,2176]{1,0:T(8,128)(2,1)} %get-tuple-element.63.after_ref.refs_1_), channel_id=1, source_target_pairs={{0,2},{1,3},{2,0},{3,1},{4,6},{5,7},{6,4},{7,5},{8,10},{9,11},{10,... | collective-permute-start | bytes 1671176 | tf_op jit(solution)/shard_map/ppermute | solution.py:382
  9.7 1.5 %collective-permute-start.6 = (bf16[896,768]{1,0:T(8,128)(2,1)}, bf16[896,768]{1,0:T(8,128)(2,1)}, u32[]{:S(2)}, u32[]{:S(2)}) collective-permute-start(bf16[896,768]{1,0:T(8,128)(2,1)} %get-tuple-element.66), channel_id=1, source_target_pairs={{0,16},{16,0},{1,17},{17,1},{2,18},{18,2},{3,19},{19,3},{4,20},{20... | collective-permute-start | bytes 4128776 | tf_op jit(solution)/shard_map/ppermute | solution.py:396
  11.2 1.1 %copy-done.7 = bf16[128,2176]{1,0:T(8,128)(2,1)S(1)} copy-done((bf16[128,2176]{1,0:T(8,128)(2,1)S(1)}, bf16[128,2176]{1,0:T(8,128)(2,1)}, u32[]{:S(2)}) %copy-start.7) | copy-done | bytes 557080
  12.3 1.3 %weight_pieces.1 = (bf16[256,768]{1,0:T(8,128)(2,1)S(1)}, bf16[896,768]{1,0:T(8,128)(2,1)}) custom-call(bf16[2048,768]{1,0:T(8,128)(2,1)S(1)} %bitcast.12, bf16[128,2176]{1,0:T(8,128)(2,1)S(1)} %copy-done.7), custom_call_target="tpu_custom_call" | custom-call | tf_op jit(solution)/shard_map/weight_pieces/pallas_call | solution.py:353
  13.6 0.7 copy-done.13
  14.3 5.4 %collective-permute-done.refs_1_ = bf16[128,2176]{1,0:T(8,128)(2,1)} collective-permute-done((bf16[128,2176]{1,0:T(8,128)(2,1)}, bf16[128,2176]{1,0:T(8,128)(2,1)}, u32[]{:S(2)}, u32[]{:S(2)}) %collective-permute-start) | collective-permute-done | bytes 557088 | tf_op jit(solution)/shard_map/ppermute | solution.py:385
  19.7 2.8 %collective-permute-done.2.refs_2_ = bf16[128,2176]{1,0:T(8,128)(2,1)S(1)} collective-permute-done((bf16[128,2176]{1,0:T(8,128)(2,1)}, bf16[128,2176]{1,0:T(8,128)(2,1)S(1)}, u32[]{:S(2)}, u32[]{:S(2)}) %collective-permute-start.2) | collective-permute-done | bytes 557088 | tf_op jit(solution)/shard_map/ppermute | solution.py:382
  22.5 0.8 copy-done.11
  23.3 1.3 %collective-permute-start.3 = (bf16[128,2176]{1,0:T(8,128)(2,1)}, bf16[128,2176]{1,0:T(8,128)(2,1)}, u32[]{:S(2)}, u32[]{:S(2)}) collective-permute-start(bf16[128,2176]{1,0:T(8,128)(2,1)} %collective-permute-done.1), channel_id=1, source_target_pairs={{4,0},{5,1},{6,2},{7,3},{8,12},{9,13},{10,14},{11,15},{20,16},{21,... | collective-permute-start | bytes 1671176 | tf_op jit(solution)/shard_map/ppermute | solution.py:385
  24.6 1.5 %collective-permute-start.4 = (bf16[128,2176]{1,0:T(8,128)(2,1)}, bf16[128,2176]{1,0:T(8,128)(2,1)}, u32[]{:S(2)}, u32[]{:S(2)}) collective-permute-start(bf16[128,2176]{1,0:T(8,128)(2,1)} %collective-permute-done.refs_1_), channel_id=1, source_target_pairs={{4,8},{5,9},{6,10},{7,11},{8,4},{9,5},{10,6},{11,7},{20,24},{21,25... | collective-permute-start | bytes 1671176 | tf_op jit(solution)/shard_map/ppermute | solution.py:385
  26.2 1.5 %collective-permute-start.5 = (bf16[128,2176]{1,0:T(8,128)(2,1)}, bf16[128,2176]{1,0:T(8,128)(2,1)S(1)}, u32[]{:S(2)}, u32[]{:S(2)}) collective-permute-start(bf16[128,2176]{1,0:T(8,128)(2,1)} %collective-permute-done.refs_1_), channel_id=1, source_target_pairs={{0,2},{1,3},{2,0},{3,1},{4,6},{5,7},{6,4},{7,5},{8,10},{9,11},{10,... | collective-permute-start | bytes 1671176 | tf_op jit(solution)/shard_map/ppermute | solution.py:382
  27.7 1.1 %copy-done.8 = bf16[128,2176]{1,0:T(8,128)(2,1)S(1)} copy-done((bf16[128,2176]{1,0:T(8,128)(2,1)S(1)}, bf16[128,2176]{1,0:T(8,128)(2,1)}, u32[]{:S(2)}) %copy-start.8) | copy-done | bytes 557080
  28.7 1.1 %copy-done.12 = bf16[128,2176]{1,0:T(8,128)(2,1)S(1)} copy-done((bf16[128,2176]{1,0:T(8,128)(2,1)S(1)}, bf16[128,2176]{1,0:T(8,128)(2,1)}, u32[]{:S(2)}) %copy-start.12) | copy-done | bytes 557080
  29.8 1.7 %picked_rows.4 = (bf16[256,2176]{1,0:T(8,128)(2,1)S(1)}, bf16[256,2176]{1,0:T(8,128)(2,1)S(1)}) custom-call(s32[3]{0:T(128)S(1)} %pad_add_fusion.refs_0_, bf16[128,2176]{1,0:T(8,128)(2,1)S(1)} %copy-done.8, bf16[128,2176]{1,0:T(8,128)(2,1)S(1)} %copy-done.12), custom_call_target="tpu_custom_call" | custom-call | flops 4563402752 | bytes 53477376 | tf_op jit(solution)/shard_map/picked_rows/pallas_call | solution.py:108
  31.5 8.1 %collective-permute-done.3 = bf16[128,2176]{1,0:T(8,128)(2,1)} collective-permute-done((bf16[128,2176]{1,0:T(8,128)(2,1)}, bf16[128,2176]{1,0:T(8,128)(2,1)}, u32[]{:S(2)}, u32[]{:S(2)}) %collective-permute-start.3) | collective-permute-done | bytes 557088 | tf_op jit(solution)/shard_map/ppermute | solution.py:385
  39.6 1.1 %broadcast_select_fusion.1.refs_1_ = bf16[128,2176]{1,0:T(8,128)(2,1)S(1)} fusion(bf16[128,2176]{1,0:T(8,128)(2,1)} %collective-permute-done.3, bf16[128,2176]{1,0:T(8,128)(2,1)} %collective-permute-done.4, pred[]{:T(512)S(6)} %or.3), kind=kLoop, calls=%fused_computation.2 | loop fusion | flops 278528 | bytes 1671169 | tf_op jit(solution)/shard_map/jit(_where)/select_n | solution.py:431
  40.7 0.7 collective-permute-done.6.refs_2_
  41.4 1.5 %collective-permute-start.7 = (bf16[128,2176]{1,0:T(8,128)(2,1)S(1)}, bf16[128,2176]{1,0:T(8,128)(2,1)S(1)}, u32[]{:S(2)}, u32[]{:S(2)}) collective-permute-start(bf16[128,2176]{1,0:T(8,128)(2,1)S(1)} %broadcast_select_fusion.1.refs_1_), channel_id=1, source_target_pairs={{4,0},{5,1},{6,2},{7,3},{8,12},{9,13},{10,14},{11,15},{20,16},{21,... | collective-permute-start | bytes 1671176 | tf_op jit(solution)/shard_map/ppermute | solution.py:385
  42.9 0.9 collective-permute-start.8
  43.7 1.5 %collective-permute-start.10 = (bf16[256,768]{1,0:T(8,128)(2,1)S(1)}, bf16[256,768]{1,0:T(8,128)(2,1)S(1)}, u32[]{:S(2)}, u32[]{:S(2)}) collective-permute-start(bf16[256,768]{1,0:T(8,128)(2,1)S(1)} %copy-done.14), channel_id=1, source_target_pairs={{0,16},{16,0},{1,17},{17,1},{2,18},{18,2},{3,19},{19,3},{4,20},{20... | collective-permute-start | bytes 1179656 | tf_op jit(solution)/shard_map/ppermute | solution.py:396
  45.3 2.2 %picked_rows.5 = (bf16[256,2176]{1,0:T(8,128)(2,1)S(1)}, bf16[256,2176]{1,0:T(8,128)(2,1)S(1)}) custom-call(s32[3]{0:T(128)S(1)} %pad_add_fusion.refs_0_, bf16[128,2176]{1,0:T(8,128)(2,1)} %collective-permute-done.refs_1_, bf16[128,2176]{1,0:T(8,128)(2,1)S(1)} %collective-permute-done.5.refs_2_), custom_call_target="tpu_custom_call" | custom-call | flops 4563402752 | bytes 53477376 | tf_op jit(solution)/shard_map/picked_rows/pallas_call | solution.py:108
  47.5 9.4 %collective-permute-done.7 = bf16[128,2176]{1,0:T(8,128)(2,1)S(1)} collective-permute-done((bf16[128,2176]{1,0:T(8,128)(2,1)S(1)}, bf16[128,2176]{1,0:T(8,128)(2,1)S(1)}, u32[]{:S(2)}, u32[]{:S(2)}) %collective-permute-start.7) | collective-permute-done | bytes 557088 | tf_op jit(solution)/shard_map/ppermute | solution.py:385
  57.1 1.6 %collective-permute-start.17 = (bf16[896,768]{1,0:T(8,128)(2,1)}, bf16[896,768]{1,0:T(8,128)(2,1)}, u32[]{:S(2)}, u32[]{:S(2)}) collective-permute-start(bf16[896,768]{1,0:T(8,128)(2,1)} %get-tuple-element.102), channel_id=1, source_target_pairs={{0,16},{16,0},{1,17},{17,1},{2,18},{18,2},{3,19},{19,3},{4,20},{20... | collective-permute-start | bytes 4128776 | tf_op jit(solution)/shard_map/ppermute | solution.py:396
  58.7 1.3 %collective-permute-start.11 = (bf16[128,2176]{1,0:T(8,128)(2,1)S(1)}, bf16[128,2176]{1,0:T(8,128)(2,1)S(1)}, u32[]{:S(2)}, u32[]{:S(2)}) collective-permute-start(bf16[128,2176]{1,0:T(8,128)(2,1)S(1)} %broadcast_select_fusion.refs_1_), channel_id=1, source_target_pairs={{0,2},{1,3},{2,0},{3,1},{4,6},{5,7},{6,4},{7,5},{8,10},{9,11},{10,... | collective-permute-start | bytes 1671176 | tf_op jit(solution)/shard_map/ppermute | solution.py:382
  60.0 2.7 %picked_rows.6 = (bf16[256,2176]{1,0:T(8,128)(2,1)S(1)}, bf16[256,2176]{1,0:T(8,128)(2,1)}) custom-call(s32[3]{0:T(128)S(1)} %pad_add_fusion.refs_0_, bf16[128,2176]{1,0:T(8,128)(2,1)S(1)} %broadcast_select_fusion.1.refs_1_, bf16[128,2176]{1,0:T(8,128)(2,1)S(1)} %collective-permute-done.8.refs_2_), custom_call_target="tpu_custom_call" | custom-call | flops 4563402752 | bytes 53477376 | tf_op jit(solution)/shard_map/picked_rows/pallas_call | solution.py:108
  62.7 5.6 %expert_terms.3 = (bf16[32,2048]{1,0:T(8,128)(2,1)S(1)}, f32[512,896]{1,0:T(8,128)S(1)}, bf16[512,896]{1,0:T(8,128)(2,1)S(1)}, f32[384,384]{1,0:T(8,128)S(1)}) custom-call(s32[3]{0:T(128)S(1)} %pad_add_fusion.refs_0_, bf16[2,1024,768]{2,1,0:T(8,128)(2,1)S(1)} %copy-done, bf16[896,768]{1,0:T(8,128)(2,1)} %collective-permute-done.6.refs_2_, ...), custom_call_target="tpu_custom_call" | custom-call | flops 27380416512 | tf_op jit(solution)/shard_map/expert_terms/pallas_call | solution.py:255
  68.3 1.3 %copy-done.15 = f32[512,896]{1,0:T(8,128)} copy-done((f32[512,896]{1,0:T(8,128)}, f32[512,896]{1,0:T(8,128)S(1)}, u32[]{:S(2)}) %copy-start.15) | copy-done | bytes 1835032
  69.6 0.9 copy-done.17
  70.5 2.9 %collective-permute-done.11.refs_2_ = bf16[128,2176]{1,0:T(8,128)(2,1)S(1)} collective-permute-done((bf16[128,2176]{1,0:T(8,128)(2,1)S(1)}, bf16[128,2176]{1,0:T(8,128)(2,1)S(1)}, u32[]{:S(2)}, u32[]{:S(2)}) %collective-permute-start.11) | collective-permute-done | bytes 557088 | tf_op jit(solution)/shard_map/ppermute | solution.py:382
  73.4 2.7 %picked_rows.7 = (bf16[256,2176]{1,0:T(8,128)(2,1)S(1)}, bf16[128,2176]{1,0:T(8,128)(2,1)}, bf16[128,2176]{1,0:T(8,128)(2,1)}) custom-call(s32[3]{0:T(128)S(1)} %pad_add_fusion.refs_0_, bf16[128,2176]{1,0:T(8,128)(2,1)S(1)} %broadcast_select_fusion.refs_1_, bf16[128,2176]{1,0:T(8,128)(2,1)S(1)} %collective-permute-done.11.refs_2_), custom_call_target="tpu_custom_call" | custom-call | flops 16 | bytes 16 | tf_op jit(solution)/shard_map/picked_rows/pallas_call | solution.py:108
  76.0 1.0 copy-done.3
  77.0 0.5 collective-permute-start.13
  77.6 1.2 %copy-done.2 = bf16[256,2176]{1,0:T(8,128)(2,1)S(1)} copy-done((bf16[256,2176]{1,0:T(8,128)(2,1)S(1)}, bf16[256,2176]{1,0:T(8,128)(2,1)}, u32[]{:S(2)}) %copy-start.2) | copy-done | bytes 1114136
  78.8 1.1 %copy-done.6 = f32[384,384]{1,0:T(8,128)S(1)} copy-done((f32[384,384]{1,0:T(8,128)S(1)}, f32[384,384]{1,0:T(8,128)}, u32[]{:S(2)}) %copy-start.6) | copy-done | bytes 589848
  79.9 0.9 copy-done.10
  80.8 4.1 %expert_terms.4 = (bf16[32,2048]{1,0:T(8,128)(2,1)S(1)}, f32[256,896]{1,0:T(8,128)S(1)}, bf16[256,896]{1,0:T(8,128)(2,1)S(1)}, f32[384,384]{1,0:T(8,128)S(1)}) custom-call(s32[3]{0:T(128)S(1)} %pad_add_fusion.refs_0_, bf16[2,1024,768]{2,1,0:T(8,128)(2,1)S(1)} %copy-done, bf16[896,768]{1,0:T(8,128)(2,1)} %collective-permute-done.6.refs_2_, ...), custom_call_target="tpu_custom_call" | custom-call | flops 16 | bytes 16 | tf_op jit(solution)/shard_map/expert_terms/pallas_call | solution.py:255
  85.0 4.2 %expert_terms.5 = (bf16[32,2048]{1,0:T(8,128)(2,1)S(1)}, f32[256,896]{1,0:T(8,128)S(1)}, bf16[256,896]{1,0:T(8,128)(2,1)S(1)}, f32[192,384]{1,0:T(8,128)S(1)}, bf16[208,384]{1,0:T(8,128)(2,1)S(1)}) custom-call(s32[3]{0:T(128)S(1)} %pad_add_fusion.refs_0_, bf16[2,1024,768]{2,1,0:T(8,128)(2,1)S(1)} %copy-done, ...), custom_call_target="tpu_custom_call" | custom-call | flops 16 | bytes 16 | tf_op jit(solution)/shard_map/expert_terms/pallas_call | solution.py:255
  89.2 0.6 collective-permute-start.16
  89.7 0.3 collective-permute-done.17.refs_1_
  90.0 5.1 %last_terms.1 = (f32[192,384]{1,0:T(8,128)S(1)}, bf16[192,384]{1,0:T(8,128)(2,1)S(1)}) custom-call(s32[3]{0:T(128)S(1)} %pad_add_fusion.refs_0_, bf16[896,768]{1,0:T(8,128)(2,1)} %collective-permute-done.17.refs_1_, bf16[512,896]{1,0:T(8,128)(2,1)S(1)} %copy-done.18, f32[512,896]{1,0:T(8,128)S(1)} %copy-done.16, ...), custom_call_target="tpu_custom_call" | custom-call | flops 22548578304 | tf_op jit(solution)/shard_map/last_terms/pallas_call | solution.py:315
  95.2 0.5 collective-permute-done.16
  95.8 1.1 %collective-permute-start.18 = (bf16[192,384]{1,0:T(8,128)(2,1)S(1)}, bf16[192,384]{1,0:T(8,128)(2,1)S(1)}, u32[]{:S(2)}, u32[]{:S(2)}) collective-permute-start(bf16[192,384]{1,0:T(8,128)(2,1)S(1)} %get-tuple-element.112), channel_id=1, source_target_pairs={{0,16},{16,0},{1,17},{17,1},{2,18},{18,2},{3,19},{19,3},{4,20},{20... | collective-permute-start | bytes 442376 | tf_op jit(solution)/shard_map/ppermute | solution.py:396
  96.8 0.6 convert_maximum_fusion
  97.4 3.9 %collective-permute-done.18 = bf16[192,384]{1,0:T(8,128)(2,1)S(1)} collective-permute-done((bf16[192,384]{1,0:T(8,128)(2,1)S(1)}, bf16[192,384]{1,0:T(8,128)(2,1)S(1)}, u32[]{:S(2)}, u32[]{:S(2)}) %collective-permute-start.18) | collective-permute-done | bytes 147488 | tf_op jit(solution)/shard_map/ppermute | solution.py:396
  101.4 0.9 pad_maximum_fusion
  (48 shorter events, 0.4 us)
Async XLA Ops:
  0.6 10.6 %copy-start = (bf16[2,1024,768]{2,1,0:T(8,128)(2,1)S(1)}, bf16[2,1024,768]{2,1,0:T(8,128)(2,1)}, u32[]{:S(2)}) copy-start(bf16[2,1024,768]{2,1,0:T(8,128)(2,1)} %refs_1_.5) | copy-start | bytes 9437188
  3.7 16.0 %collective-permute-start = (bf16[128,2176]{1,0:T(8,128)(2,1)}, bf16[128,2176]{1,0:T(8,128)(2,1)}, u32[]{:S(2)}, u32[]{:S(2)}) collective-permute-start(bf16[128,2176]{1,0:T(8,128)(2,1)} %get-tuple-element.63.after_ref.refs_1_), channel_id=1, source_target_pairs={{0,4},{1,5},{2,6},{3,7},{4,0},{5,1},{6,2},{7,3},{8,12},{9,13},{10,... | collective-permute-start | bytes 1671176 | tf_op jit(solution)/shard_map/ppermute | solution.py:385
  6.8 12.9 %collective-permute-start.1 = (bf16[128,2176]{1,0:T(8,128)(2,1)}, bf16[128,2176]{1,0:T(8,128)(2,1)}, u32[]{:S(2)}, u32[]{:S(2)}) collective-permute-start(bf16[128,2176]{1,0:T(8,128)(2,1)} %get-tuple-element.63.after_ref.refs_1_), channel_id=1, source_target_pairs={{4,8},{5,9},{6,10},{7,11},{8,4},{9,5},{10,6},{11,7},{20,24},{21,25... | collective-permute-start | bytes 1671176 | tf_op jit(solution)/shard_map/ppermute | solution.py:385
  8.2 14.3 %collective-permute-start.2 = (bf16[128,2176]{1,0:T(8,128)(2,1)}, bf16[128,2176]{1,0:T(8,128)(2,1)S(1)}, u32[]{:S(2)}, u32[]{:S(2)}) collective-permute-start(bf16[128,2176]{1,0:T(8,128)(2,1)} %get-tuple-element.63.after_ref.refs_1_), channel_id=1, source_target_pairs={{0,2},{1,3},{2,0},{3,1},{4,6},{5,7},{6,4},{7,5},{8,10},{9,11},{10,... | collective-permute-start | bytes 1671176 | tf_op jit(solution)/shard_map/ppermute | solution.py:382
  9.7 31.7 %collective-permute-start.6 = (bf16[896,768]{1,0:T(8,128)(2,1)}, bf16[896,768]{1,0:T(8,128)(2,1)}, u32[]{:S(2)}, u32[]{:S(2)}) collective-permute-start(bf16[896,768]{1,0:T(8,128)(2,1)} %get-tuple-element.66), channel_id=1, source_target_pairs={{0,16},{16,0},{1,17},{17,1},{2,18},{18,2},{3,19},{19,3},{4,20},{20... | collective-permute-start | bytes 4128776 | tf_op jit(solution)/shard_map/ppermute | solution.py:396
  11.2 1.1 %copy-start.7 = (bf16[128,2176]{1,0:T(8,128)(2,1)S(1)}, bf16[128,2176]{1,0:T(8,128)(2,1)}, u32[]{:S(2)}) copy-start(bf16[128,2176]{1,0:T(8,128)(2,1)} %get-tuple-element.63.after_ref.refs_1_) | copy-start | bytes 1671172
  13.6 0.8 copy-start.13
  22.5 0.8 copy-start.11
  23.3 16.2 %collective-permute-start.3 = (bf16[128,2176]{1,0:T(8,128)(2,1)}, bf16[128,2176]{1,0:T(8,128)(2,1)}, u32[]{:S(2)}, u32[]{:S(2)}) collective-permute-start(bf16[128,2176]{1,0:T(8,128)(2,1)} %collective-permute-done.1), channel_id=1, source_target_pairs={{4,0},{5,1},{6,2},{7,3},{8,12},{9,13},{10,14},{11,15},{20,16},{21,... | collective-permute-start | bytes 1671176 | tf_op jit(solution)/shard_map/ppermute | solution.py:385
  24.6 14.9 %collective-permute-start.4 = (bf16[128,2176]{1,0:T(8,128)(2,1)}, bf16[128,2176]{1,0:T(8,128)(2,1)}, u32[]{:S(2)}, u32[]{:S(2)}) collective-permute-start(bf16[128,2176]{1,0:T(8,128)(2,1)} %collective-permute-done.refs_1_), channel_id=1, source_target_pairs={{4,8},{5,9},{6,10},{7,11},{8,4},{9,5},{10,6},{11,7},{20,24},{21,25... | collective-permute-start | bytes 1671176 | tf_op jit(solution)/shard_map/ppermute | solution.py:385
  26.2 14.5 %collective-permute-start.5 = (bf16[128,2176]{1,0:T(8,128)(2,1)}, bf16[128,2176]{1,0:T(8,128)(2,1)S(1)}, u32[]{:S(2)}, u32[]{:S(2)}) collective-permute-start(bf16[128,2176]{1,0:T(8,128)(2,1)} %collective-permute-done.refs_1_), channel_id=1, source_target_pairs={{0,2},{1,3},{2,0},{3,1},{4,6},{5,7},{6,4},{7,5},{8,10},{9,11},{10,... | collective-permute-start | bytes 1671176 | tf_op jit(solution)/shard_map/ppermute | solution.py:382
  27.7 1.1 %copy-start.8 = (bf16[128,2176]{1,0:T(8,128)(2,1)S(1)}, bf16[128,2176]{1,0:T(8,128)(2,1)}, u32[]{:S(2)}) copy-start(bf16[128,2176]{1,0:T(8,128)(2,1)} %get-tuple-element.63.after_ref.refs_1_) | copy-start | bytes 1671172
  28.7 1.1 %copy-start.12 = (bf16[128,2176]{1,0:T(8,128)(2,1)S(1)}, bf16[128,2176]{1,0:T(8,128)(2,1)}, u32[]{:S(2)}) copy-start(bf16[128,2176]{1,0:T(8,128)(2,1)} %copy-done.11) | copy-start | bytes 1671172
  31.5 12.3 %copy-start.14 = (bf16[256,768]{1,0:T(8,128)(2,1)S(1)}, bf16[256,768]{1,0:T(8,128)(2,1)}, u32[]{:S(2)}) copy-start(bf16[256,768]{1,0:T(8,128)(2,1)} %copy-done.13) | copy-start | bytes 1179652
  41.4 15.5 %collective-permute-start.7 = (bf16[128,2176]{1,0:T(8,128)(2,1)S(1)}, bf16[128,2176]{1,0:T(8,128)(2,1)S(1)}, u32[]{:S(2)}, u32[]{:S(2)}) collective-permute-start(bf16[128,2176]{1,0:T(8,128)(2,1)S(1)} %broadcast_select_fusion.1.refs_1_), channel_id=1, source_target_pairs={{4,0},{5,1},{6,2},{7,3},{8,12},{9,13},{10,14},{11,15},{20,16},{21,... | collective-permute-start | bytes 1671176 | tf_op jit(solution)/shard_map/ppermute | solution.py:385
  42.9 14.1 %collective-permute-start.8 = (bf16[128,2176]{1,0:T(8,128)(2,1)S(1)}, bf16[128,2176]{1,0:T(8,128)(2,1)S(1)}, u32[]{:S(2)}, u32[]{:S(2)}) collective-permute-start(bf16[128,2176]{1,0:T(8,128)(2,1)S(1)} %broadcast_select_fusion.1.refs_1_), channel_id=1, source_target_pairs={{0,2},{1,3},{2,0},{3,1},{4,6},{5,7},{6,4},{7,5},{8,10},{9,11},{10,... | collective-permute-start | bytes 1671176 | tf_op jit(solution)/shard_map/ppermute | solution.py:382
  43.7 13.3 %collective-permute-start.9 = (bf16[256,2176]{1,0:T(8,128)(2,1)S(1)}, bf16[256,2176]{1,0:T(8,128)(2,1)S(1)}, u32[]{:S(2)}, u32[]{:S(2)}) collective-permute-start(bf16[256,2176]{1,0:T(8,128)(2,1)S(1)} %get-tuple-element.72), channel_id=1, source_target_pairs={{0,1},{1,0},{2,3},{3,2},{4,5},{5,4},{6,7},{7,6},{8,9},{9,8},{10,11... | collective-permute-start | bytes 3342344 | tf_op jit(solution)/shard_map/ppermute | solution.py:382
  43.7 13.2 %collective-permute-start.10 = (bf16[256,768]{1,0:T(8,128)(2,1)S(1)}, bf16[256,768]{1,0:T(8,128)(2,1)S(1)}, u32[]{:S(2)}, u32[]{:S(2)}) collective-permute-start(bf16[256,768]{1,0:T(8,128)(2,1)S(1)} %copy-done.14), channel_id=1, source_target_pairs={{0,16},{16,0},{1,17},{17,1},{2,18},{18,2},{3,19},{19,3},{4,20},{20... | collective-permute-start | bytes 1179656 | tf_op jit(solution)/shard_map/ppermute | solution.py:396
  57.0 5.7 %collective-permute-start.12 = (bf16[256,2176]{1,0:T(8,128)(2,1)S(1)}, bf16[256,2176]{1,0:T(8,128)(2,1)S(1)}, u32[]{:S(2)}, u32[]{:S(2)}) collective-permute-start(bf16[256,2176]{1,0:T(8,128)(2,1)S(1)} %get-tuple-element.86), channel_id=1, source_target_pairs={{0,1},{1,0},{2,3},{3,2},{4,5},{5,4},{6,7},{7,6},{8,9},{9,8},{10,11... | collective-permute-start | bytes 3342344 | tf_op jit(solution)/shard_map/ppermute | solution.py:382
  57.1 32.9 %collective-permute-start.17 = (bf16[896,768]{1,0:T(8,128)(2,1)}, bf16[896,768]{1,0:T(8,128)(2,1)}, u32[]{:S(2)}, u32[]{:S(2)}) collective-permute-start(bf16[896,768]{1,0:T(8,128)(2,1)} %get-tuple-element.102), channel_id=1, source_target_pairs={{0,16},{16,0},{1,17},{17,1},{2,18},{18,2},{3,19},{19,3},{4,20},{20... | collective-permute-start | bytes 4128776 | tf_op jit(solution)/shard_map/ppermute | solution.py:396
  58.7 14.7 %collective-permute-start.11 = (bf16[128,2176]{1,0:T(8,128)(2,1)S(1)}, bf16[128,2176]{1,0:T(8,128)(2,1)S(1)}, u32[]{:S(2)}, u32[]{:S(2)}) collective-permute-start(bf16[128,2176]{1,0:T(8,128)(2,1)S(1)} %broadcast_select_fusion.refs_1_), channel_id=1, source_target_pairs={{0,2},{1,3},{2,0},{3,1},{4,6},{5,7},{6,4},{7,5},{8,10},{9,11},{10,... | collective-permute-start | bytes 1671176 | tf_op jit(solution)/shard_map/ppermute | solution.py:382
  62.7 5.6 %copy-start.1 = (bf16[256,2176]{1,0:T(8,128)(2,1)}, bf16[256,2176]{1,0:T(8,128)(2,1)S(1)}, u32[]{:S(2)}) copy-start(bf16[256,2176]{1,0:T(8,128)(2,1)S(1)} %get-tuple-element.94.refs_4_) | copy-start | bytes 3342340
  68.3 1.3 %copy-start.15 = (f32[512,896]{1,0:T(8,128)}, f32[512,896]{1,0:T(8,128)S(1)}, u32[]{:S(2)}) copy-start(f32[512,896]{1,0:T(8,128)S(1)} %get-tuple-element.104.refs_3_) | copy-start | bytes 5505028
  69.6 0.9 copy-start.17
  70.5 5.6 %copy-start.5 = (f32[384,384]{1,0:T(8,128)}, f32[384,384]{1,0:T(8,128)S(1)}, u32[]{:S(2)}) copy-start(f32[384,384]{1,0:T(8,128)S(1)} %get-tuple-element.96.refs_6_) | copy-start | bytes 1769476
  70.5 6.6 %copy-start.9 = (bf16[32,2048]{1,0:T(8,128)(2,1)}, bf16[32,2048]{1,0:T(8,128)(2,1)S(1)}, u32[]{:S(2)}) copy-start(bf16[32,2048]{1,0:T(8,128)(2,1)S(1)} %get-tuple-element.97.refs_7_) | copy-start | bytes 393220
  73.4 4.2 %collective-permute-start.15 = (bf16[256,2176]{1,0:T(8,128)(2,1)}, bf16[256,2176]{1,0:T(8,128)(2,1)}, u32[]{:S(2)}, u32[]{:S(2)}) collective-permute-start(bf16[256,2176]{1,0:T(8,128)(2,1)} %get-tuple-element.95), channel_id=1, source_target_pairs={{0,1},{1,0},{2,3},{3,2},{4,5},{5,4},{6,7},{7,6},{8,9},{9,8},{10,11... | collective-permute-start | bytes 3342344 | tf_op jit(solution)/shard_map/ppermute | solution.py:382
  76.0 1.0 copy-start.3
  77.0 7.9 %collective-permute-start.13 = (bf16[128,2176]{1,0:T(8,128)(2,1)}, bf16[128,2176]{1,0:T(8,128)(2,1)}, u32[]{:S(2)}, u32[]{:S(2)}) collective-permute-start(bf16[128,2176]{1,0:T(8,128)(2,1)} %get-tuple-element.92), channel_id=1, source_target_pairs={{0,1},{1,0},{2,3},{3,2},{4,5},{5,4},{6,7},{7,6},{8,9},{9,8},{10,11... | collective-permute-start | bytes 1671176 | tf_op jit(solution)/shard_map/ppermute | solution.py:382
  77.5 7.4 %collective-permute-start.14 = (bf16[128,2176]{1,0:T(8,128)(2,1)}, bf16[128,2176]{1,0:T(8,128)(2,1)}, u32[]{:S(2)}, u32[]{:S(2)}) collective-permute-start(bf16[128,2176]{1,0:T(8,128)(2,1)} %get-tuple-element.93), channel_id=1, source_target_pairs={{0,1},{1,0},{2,3},{3,2},{4,5},{5,4},{6,7},{7,6},{8,9},{9,8},{10,11... | collective-permute-start | bytes 1671176 | tf_op jit(solution)/shard_map/ppermute | solution.py:382
  77.6 1.2 %copy-start.2 = (bf16[256,2176]{1,0:T(8,128)(2,1)S(1)}, bf16[256,2176]{1,0:T(8,128)(2,1)}, u32[]{:S(2)}) copy-start(bf16[256,2176]{1,0:T(8,128)(2,1)} %copy-done.1) | copy-start | bytes 3342340
  78.8 1.1 %copy-start.6 = (f32[384,384]{1,0:T(8,128)S(1)}, f32[384,384]{1,0:T(8,128)}, u32[]{:S(2)}) copy-start(f32[384,384]{1,0:T(8,128)} %copy-done.5) | copy-start | bytes 1769476
  79.9 0.9 copy-start.10
  80.8 4.1 %copy-start.4 = (bf16[256,2176]{1,0:T(8,128)(2,1)S(1)}, bf16[256,2176]{1,0:T(8,128)(2,1)}, u32[]{:S(2)}) copy-start(bf16[256,2176]{1,0:T(8,128)(2,1)} %copy-done.3) | copy-start | bytes 3342340
  84.9 5.1 %copy-start.16 = (f32[512,896]{1,0:T(8,128)S(1)}, f32[512,896]{1,0:T(8,128)}, u32[]{:S(2)}) copy-start(f32[512,896]{1,0:T(8,128)} %copy-done.15) | copy-start | bytes 5505028
  84.9 5.1 %copy-start.18 = (bf16[512,896]{1,0:T(8,128)(2,1)S(1)}, bf16[512,896]{1,0:T(8,128)(2,1)}, u32[]{:S(2)}) copy-start(bf16[512,896]{1,0:T(8,128)(2,1)} %copy-done.17) | copy-start | bytes 2752516
  89.2 6.6 %collective-permute-start.16 = (bf16[208,384]{1,0:T(8,128)(2,1)S(1)}, bf16[208,384]{1,0:T(8,128)(2,1)S(1)}, u32[]{:S(2)}, u32[]{:S(2)}) collective-permute-start(bf16[208,384]{1,0:T(8,128)(2,1)S(1)} %get-tuple-element.101), channel_id=1, source_target_pairs={{0,16},{16,0},{1,17},{17,1},{2,18},{18,2},{3,19},{19,3},{4,20},{20... | collective-permute-start | bytes 479240 | tf_op jit(solution)/shard_map/ppermute | solution.py:396
  95.8 5.5 %collective-permute-start.18 = (bf16[192,384]{1,0:T(8,128)(2,1)S(1)}, bf16[192,384]{1,0:T(8,128)(2,1)S(1)}, u32[]{:S(2)}, u32[]{:S(2)}) collective-permute-start(bf16[192,384]{1,0:T(8,128)(2,1)S(1)} %get-tuple-element.112), channel_id=1, source_target_pairs={{0,16},{16,0},{1,17},{17,1},{2,18},{18,2},{3,19},{19,3},{4,20},{20... | collective-permute-start | bytes 442376 | tf_op jit(solution)/shard_map/ppermute | solution.py:396
